TPU v7x, 32 devices: a whole 2x2x4 slice. The times are simulated.
32 devices in a mesh: dp: 8 (over z, y), rows: 4 (over x, core).
Axes of the slice: x: 2, y: 2, z: 4, core: 2. Of those that a mesh axis runs over, the one named last changes fastest.
Arguments:
- latents: float32 [16, 32, 32, 3], P('dp', 'rows'), may hold values from -6 to 6
- target_noise: float32 [16, 32, 32, 3], P('dp', 'rows'), may hold values from -6 to 6
- labels: int32 [16], P('dp'), may hold values from 0 to 999
- timesteps: int32 [16], P('dp'), may hold values from 0 to 999
- orient: int32 [16], P('dp'), may hold values from 0 to 1, as said below
- extent: int32 [16], P('dp'), may hold values from 8 to 32, as said below
- mat_params: float32 [12860416], P(('dp', 'rows'))
- mat_first: float32 [12860416], P(('dp', 'rows'))
- mat_second: float32 [12860416], P(('dp', 'rows')), as said below
- mat_ema: float32 [12860416], P(('dp', 'rows'))
- vec_params: float32 [16928], P(('dp', 'rows'))
- vec_first: float32 [16928], P(('dp', 'rows'))
- vec_second: float32 [16928], P(('dp', 'rows')), as said below
- vec_ema: float32 [16928], P(('dp', 'rows'))
Outputs:
- new_mat_params: float32 [12860416], P(('dp', 'rows'))
- new_mat_first: float32 [12860416], P(('dp', 'rows'))
- new_mat_second: float32 [12860416], P(('dp', 'rows'))
- new_mat_ema: float32 [12860416], P(('dp', 'rows'))
- new_vec_params: float32 [16928], P(('dp', 'rows'))
- new_vec_first: float32 [16928], P(('dp', 'rows'))
- new_vec_second: float32 [16928], P(('dp', 'rows'))
- new_vec_ema: float32 [16928], P(('dp', 'rows'))
- grad_norm: float32 [], replicated
- loss_sum: float32 [], replicated
- pixel_count: float32 [], replicated
Inputs may be any that keep to these rules, and one draw needn't show every extreme that they name: `orient`: 1 where the image's bucket is portrait (long side along the rows), 0 for landscape; in each aligned group of 2 images one is portrait with extent 32. `extent`: valid length along the bucket's orientation (rows for portrait, columns for landscape); the other side is 16. `mat_second`: positive. `vec_second`: positive.
All inputs are finite; a program needn't handle non-finite values.
Results may differ from a plain program's by a relative error of at most 0.0006.
The roundings to bfloat16 on the way count: a program that leaves them out, or rounds other values in their place, can miss the bound.
Values may be sent and summed in bfloat16 or wider, within the bound.
No kernel may reach another device: no remote copies, remote signals or barrier semaphores. Data moves between devices by JAX's collectives and lax.ppermute only.
A program may use at most 320 MiB of HBM per device.

v0:
```python
import math

import jax
import jax.numpy as jnp
from jax import lax
from jax.sharding import PartitionSpec as P

C = 512
HEADS = 8
DHEAD = 64
FFI = 2048
TE = 256
TD = 1024
NCLS = 1000
LC = 3
GROUPS = 32
SIDE = 32
NT = 1000
STEP = 10


tap_offsets = [(-1, -1), (-1, 0), (-1, 1), (0, -1), (0, 0), (0, 1), (1, -1), (1, 0), (1, 1)]
eps_group = 1e-06
eps_layer = 1e-05
beta_first = 0.00085
beta_last = 0.012
adam_one = 0.9
adam_two = 0.999
adam_eps = 1e-08
learn_rate = 0.05
weight_decay = 0.01
ema_ceiling = 0.9999
clip_norm = 0.1


def mat_layout():
    return [
        ("w_in", 9 * LC, C),
        ("w_t1", TE, TD),
        ("w_t2", TD, TD),
        ("w_tp", TD, C),
        ("table", NCLS, C),
        ("w_c1", 9 * C, C),
        ("w_c2", 9 * C, C),
        ("w_pin", C, C),
        ("w_qkv", C, 3 * C),
        ("w_o", C, C),
        ("w_cq", C, C),
        ("w_ckv", C, 2 * C),
        ("w_co", C, C),
        ("w_ff1", C, 2 * FFI),
        ("w_ff2", FFI, C),
        ("w_pout", C, C),
        ("w_out", 9 * C, LC),
    ]


def vec_layout():
    names = [
        "b_tp",
        "b_in",
        "g1",
        "bb1",
        "b_c1",
        "g2",
        "bb2",
        "b_c2",
        "g3",
        "bb3",
        "b_pin",
        "n1g",
        "n1b",
        "b_o",
        "n2g",
        "n2b",
        "b_co",
        "n3g",
        "n3b",
    ]
    return (
        [("b_t1", TD), ("b_t2", TD)]
        + [(name_one, C) for name_one in names]
        + [("b_ff1", 2 * FFI), ("b_ff2", C), ("b_pout", C), ("b_out", LC)]
    )


def unpack(joined, layout):
    pieces = {}
    start_at = 0
    for record in layout:
        length = 1
        for extent_one in record[1:]:
            length = length * extent_one
        pieces[record[0]] = joined[start_at : start_at + length].reshape(record[1:])
        start_at = start_at + length
    return pieces


def noise_level(step_value):
    steps_idx = jnp.arange(NT).astype(jnp.float32)
    root_beta = math.sqrt(beta_first) + (
        math.sqrt(beta_last) - math.sqrt(beta_first)
    ) * steps_idx / (NT - 1)
    log_keep = jnp.log1p(-root_beta * root_beta)
    return jnp.exp(jnp.sum(jnp.where(jnp.arange(NT) <= step_value, log_keep, 0.0)))


def time_embed(step_value):
    frequency = jnp.exp(-math.log(10000.0) * jnp.arange(TE // 2).astype(jnp.float32) / (TE // 2))
    angles = step_value.astype(jnp.float32) * frequency
    return jnp.concatenate([jnp.cos(angles), jnp.sin(angles)])


WIDE = 512
HALF = 256
LEAD = 5
FRAME = 16
TOKENS = SIDE * FRAME
LOCAL_HEADS = HEADS // 2
WIRE_TOP = 16384.0


def silu_slope(values):
    logistic = jax.nn.sigmoid(values)
    return logistic * (1.0 + values * (1.0 - logistic))


def dot(left, right):
    return jnp.dot(left, right, preferred_element_type=jnp.float32)


def dot_t(left, right):
    return lax.dot_general(
        left, right, (((1,), (1,)), ((), ())), preferred_element_type=jnp.float32
    )


def t_dot(left, right):
    return lax.dot_general(
        left, right, (((0,), (0,)), ((), ())), preferred_element_type=jnp.float32
    )


def low(values):
    return values.astype(jnp.bfloat16)


class Place:
    def __init__(self):
        self.dp, self.rows = (lax.axis_size("dp"), lax.axis_size("rows"))
        self.count = self.dp * self.rows
        self.index = lax.axis_index("dp") * self.rows + lax.axis_index("rows")
        self.side = self.index % 2
        self.slot = (self.index // 2) % 2
        digits, left = ([], self.dp)
        while left > 4:
            digits.append(4)
            left //= 4
        digits.append(left)
        self.digits = digits + [2]
        strides, step = ([], 2)
        for size in reversed(self.digits):
            strides.insert(0, step)
            step *= size
        self.strides = strides
        self.coords = [(self.index // s) % n for s, n in zip(strides, self.digits)]

    def move(self, value, pairs):
        return lax.ppermute(value, ("dp", "rows"), pairs)

    def swap(self, value, stride=1):
        return self.move(value, [(k, k ^ stride) for k in range(self.count)])

    def shift(self, value, by):
        return self.move(
            value, [(k, k + by) for k in range(self.count) if 0 <= k + by < self.count]
        )

    def step(self, value, axis, direction, hops):
        stride, size = (self.strides[axis], self.digits[axis])
        pairs = []
        for k in range(self.count):
            at = (k // stride) % size
            rank = at if direction > 0 else size - 1 - at
            if rank <= hops and rank < size - 1:
                pairs.append((k, k + direction * stride))
        return self.move(value, pairs)

    def half(self, value, axis=-1):
        axis = axis % value.ndim
        return lax.dynamic_slice_in_dim(value, self.side * HALF, HALF, axis)

    def join(self, mine, other):
        first = jnp.where(self.side == 0, mine, other)
        second = jnp.where(self.side == 0, other, mine)
        return jnp.concatenate([first, second], axis=-1)

    def full(self, mine):
        return self.join(mine, self.swap(mine))

    def chip_sum(self, value):
        stride = 2
        while stride < self.count:
            value = value + self.swap(value, stride)
            stride *= 2
        return value


def shard_rows(flat_len, count):
    length = flat_len // count
    rows = -(-(LEAD * WIDE + flat_len) // (WIDE * count))
    rows = -(-rows // 8) * 8
    while rows * WIDE - length < LEAD * WIDE:
        rows += 8
    return rows


def to_blocks(place, shard, rows):
    length, block = (shard.shape[0], rows * WIDE)
    drift = block - length
    reach = drift * (place.count - 1) - LEAD * WIDE + block
    parts, hop = ([jnp.zeros((LEAD * WIDE,), shard.dtype), shard], 1)
    while hop * length < reach:
        take = min(length, reach - hop * length)
        take = min(length, -(-take // 1024) * 1024)
        parts.append(place.shift(shard[:take], -hop))
        hop += 1
    joined = jnp.concatenate(parts)
    lack = drift * (place.count - 1) + block - joined.shape[0]
    if lack > 0:
        joined = jnp.pad(joined, (0, lack))
    return lax.dynamic_slice(joined, (drift * place.index,), (block,)).reshape(rows, WIDE)


def from_blocks(place, block, length):
    flat = block.reshape(-1)
    drift = flat.shape[0] - length
    reach = drift * (place.count - 1) - LEAD * WIDE
    parts, hop, lead = ([flat], 1, 0)
    while lead < reach:
        take = min(flat.shape[0], -(-(reach - lead) // 1024) * 1024)
        parts.insert(0, place.shift(flat[flat.shape[0] - take :], hop))
        lead += take
        hop += 1
    joined = jnp.concatenate(parts)
    start = lead + LEAD * WIDE - drift * place.index
    return lax.dynamic_slice(joined, (start,), (length,))


def wire_out(values, bound):
    return (values * (WIRE_TOP / bound)).astype(jnp.float16)


def wire_in(values, bound):
    return values.astype(jnp.float32) * (bound * (1.0 / WIRE_TOP))


def pick(values, index, axis):
    return lax.dynamic_index_in_dim(values, index, axis, keepdims=False)


def scatter_pair(place, held, bound, axis, dim):
    me, stride = (place.coords[axis], place.strides[axis])
    got = place.swap(wire_out(pick(held, 1 - me, dim), bound), stride)
    other = place.swap(bound, stride)
    return (pick(held, me, dim) + wire_in(got, other), bound + other)


def scatter_line(place, held, bound, axis, dim):
    me, size = (place.coords[axis], place.digits[axis])
    total, limit = (pick(held, me, dim), bound)
    for direction in (1, -1):
        rank = me if direction > 0 else size - 1 - me
        got, other = (None, None)
        for hops in range(size - 1):
            aim = jnp.minimum(size - 1 - hops + rank, size - 1)
            aim = aim if direction > 0 else size - 1 - aim
            value, top = (pick(held, aim, dim), bound)
            if got is not None:
                value, top = (value + wire_in(got, other), top + other)
            got = place.step(wire_out(value, top), axis, direction, hops)
            other = place.step(top, axis, direction, hops)
        total, limit = (total + wire_in(got, other), limit + other)
    return (total, limit)


def scatter_part(place, held, bound, order):
    left = list(range(len(place.digits)))
    for axis in order:
        dim = left.index(axis)
        if place.digits[axis] == 2:
            held, bound = scatter_pair(place, held, bound, axis, dim)
        else:
            held, bound = scatter_line(place, held, bound, axis, dim)
        left.remove(axis)
    return held


def scatter_sum(place, grads, rows):
    bound = jnp.maximum(jnp.max(jnp.abs(grads)), 1e-30).reshape(1, 1)
    bound = jnp.broadcast_to(bound, (8, 128))[:1, :1]
    held = grads.reshape(*place.digits, 2 * rows, HALF)
    axes = list(range(len(place.digits)))[::-1]
    shares = [0.45, 0.45, 0.1]
    total = 2 * rows
    cuts = [0] + [int(total * sum(shares[: i + 1]) / 8 + 0.5) * 8 for i in range(2)] + [total]
    parts = []
    for i in range(3):
        order = axes[i:] + axes[:i]
        piece = held[..., cuts[i] : cuts[i + 1], :]
        parts.append(scatter_part(place, piece, bound, order))
    chip = jnp.concatenate(parts, axis=0).reshape(2, rows, HALF)
    mine = pick(chip, place.side, 0)
    other = place.swap(pick(chip, 1 - place.side, 0))
    return place.join(mine, other)


def gather_small(place, value):
    stride, joined = (1, value[None])
    while stride < place.count:
        other = place.swap(joined, stride)
        upper = (place.index // stride) % 2 == 1
        joined = jnp.where(
            upper,
            jnp.concatenate([other, joined], axis=0),
            jnp.concatenate([joined, other], axis=0),
        )
        stride *= 2
    return joined


def windows(values, turned, sign):
    width = values.shape[1]
    col = (lax.iota(jnp.int32, TOKENS) % FRAME)[:, None]
    zero_one = jnp.zeros((1, width), values.dtype)
    zero_row = jnp.zeros((FRAME, width), values.dtype)
    none = jnp.zeros((), values.dtype)
    across = {
        -1: jnp.where(col > 0, jnp.concatenate([zero_one, values[:-1]], axis=0), none),
        0: values,
        1: jnp.where(col < FRAME - 1, jnp.concatenate([values[1:], zero_one], axis=0), none),
    }
    moved = {}
    for col_off, value in across.items():
        moved[-1, col_off] = jnp.concatenate([zero_row, value[:-FRAME]], axis=0)
        moved[0, col_off] = value
        moved[1, col_off] = jnp.concatenate([value[FRAME:], zero_row], axis=0)
    out = []
    for row_off, col_off in tap_offsets:
        plain = moved[sign * row_off, sign * col_off]
        other = moved[sign * col_off, sign * row_off]
        out.append(plain if row_off == col_off else jnp.where(turned, other, plain))
    return jnp.concatenate(out, axis=1)


def group_spread(channel_sums):
    at = lax.iota(jnp.int32, HALF) // (C // GROUPS)
    same = (at[:, None] == at[None, :]).astype(jnp.float32)
    return jnp.dot(channel_sums, same, precision=lax.Precision.HIGHEST)


def group_forward(values, mask, denominator, gain_vec, bias_vec):
    mean_val = group_spread(jnp.sum(values * mask, axis=0)[None]) / denominator
    centered = values - mean_val
    var_val = group_spread(jnp.sum(centered * centered * mask, axis=0)[None]) / denominator
    inv_std = lax.rsqrt(var_val + eps_group)
    normed = centered * inv_std
    return (normed * gain_vec + bias_vec, normed, inv_std)


def group_backward(gradient, normed, inv_std, mask, denominator, gain_vec):
    scaled = gradient * gain_vec
    sums = group_spread(
        jnp.stack([jnp.sum(scaled * mask, axis=0), jnp.sum(scaled * normed * mask, axis=0)])
    )
    input_grad = mask * inv_std * (
        scaled - sums[0:1] / denominator - normed * (sums[1:2] / denominator)
    )
    return (input_grad, jnp.sum(gradient * normed, axis=0), jnp.sum(gradient, axis=0))


def layer_forward(values, gain_vec, bias_vec):
    mean_val = jnp.mean(values, axis=-1, keepdims=True)
    centered = values - mean_val
    var_val = jnp.mean(centered * centered, axis=-1, keepdims=True)
    inv_std = lax.rsqrt(var_val + eps_layer)
    normed = centered * inv_std
    return (low(normed * gain_vec + bias_vec), normed, inv_std)


def layer_backward(gradient, normed, inv_std, gain_vec):
    scaled = gradient * gain_vec
    first = jnp.mean(scaled, axis=-1, keepdims=True)
    second = jnp.mean(scaled * normed, axis=-1, keepdims=True)
    input_grad = inv_std * (scaled - first - normed * second)
    return (input_grad, jnp.sum(gradient * normed, axis=0), jnp.sum(gradient, axis=0))


def heads_of(value):
    return value.reshape(value.shape[0], LOCAL_HEADS, DHEAD)


def head_scores(query, key, key_mask):
    scores = jnp.einsum("qhd,khd->hqk", query, key, preferred_element_type=jnp.float32) * 0.125
    return jnp.where(key_mask, scores, -1e30)


def attend(query, key, value, key_mask):
    scores = head_scores(query, key, key_mask)
    row_max = jnp.max(scores, axis=-1, keepdims=True)
    exponent = jnp.exp(scores - row_max)
    totals = jnp.sum(exponent, axis=-1, keepdims=True)
    out = jnp.einsum(
        "hqk,khd->qhd", low(exponent / totals), value, preferred_element_type=jnp.float32
    )
    return (low(out).reshape(TOKENS, HALF), row_max + jnp.log(totals))


def attend_back(query, key, value, key_mask, log_total, out_grad):
    probs = jnp.exp(head_scores(query, key, key_mask) - log_total)
    prob_grad = jnp.einsum("qhd,khd->hqk", out_grad, value, preferred_element_type=jnp.float32)
    inner = jnp.sum(probs * prob_grad, axis=-1, keepdims=True)
    score_grad = low(probs * (prob_grad - inner) * 0.125)
    query_grad = jnp.einsum("hqk,khd->qhd", score_grad, key, preferred_element_type=jnp.float32)
    key_grad = jnp.einsum("hqk,qhd->khd", score_grad, query, preferred_element_type=jnp.float32)
    value_grad = jnp.einsum(
        "hqk,qhd->khd", low(probs), out_grad, preferred_element_type=jnp.float32
    )
    return low(
        jnp.concatenate(
            [part.reshape(TOKENS, HALF) for part in (query_grad, key_grad, value_grad)], axis=1
        )
    )


def cross_split(context_kv):
    return (
        context_kv[:, :HALF].reshape(2, LOCAL_HEADS, DHEAD),
        context_kv[:, HALF:].reshape(2, LOCAL_HEADS, DHEAD),
    )


def cross_attend(query, context_kv):
    key, value = cross_split(context_kv)
    scores = jnp.einsum("thd,jhd->thj", query, key, preferred_element_type=jnp.float32) * 0.125
    probs = jax.nn.softmax(scores, axis=-1)
    out = jnp.einsum("thj,jhd->thd", probs, value.astype(jnp.float32))
    return (probs, low(out).reshape(TOKENS, HALF))


def cross_back(query, context_kv, probs, out_grad):
    key, value = cross_split(context_kv)
    prob_grad = jnp.einsum("thd,jhd->thj", out_grad, value, preferred_element_type=jnp.float32)
    score_grad = probs * (prob_grad - jnp.sum(probs * prob_grad, axis=-1, keepdims=True)) * 0.125
    query_grad = jnp.einsum("thj,jhd->thd", score_grad, key.astype(jnp.float32))
    key_grad = jnp.einsum("thj,thd->jhd", score_grad, query.astype(jnp.float32))
    value_grad = jnp.einsum("thj,thd->jhd", probs, out_grad.astype(jnp.float32))
    return (
        query_grad.reshape(TOKENS, HALF),
        jnp.concatenate([key_grad.reshape(2, HALF), value_grad.reshape(2, HALF)], axis=1),
    )


def own_columns(place, weight):
    split = weight.reshape(weight.shape[0], -1, 2, HALF)
    return pick(split, place.side, 2).reshape(weight.shape[0], -1)


def frame_of(place, latents, target_noise, turned):
    both = jnp.concatenate([latents, target_noise], axis=-1)
    stride, joined = (1, both[None])
    while stride < place.rows:
        other = place.swap(joined, stride)
        upper = (place.index // stride) % 2 == 1
        joined = jnp.where(
            upper,
            jnp.concatenate([other, joined], axis=0),
            jnp.concatenate([joined, other], axis=0),
        )
        stride *= 2
    image = pick(joined, place.slot, 1).reshape(SIDE, SIDE, 2 * LC)
    portrait = image[:, :FRAME]
    landscape = jnp.transpose(image[:FRAME], (1, 0, 2))
    return jnp.where(turned, landscape, portrait).reshape(TOKENS, 2 * LC)


def train_step(place, mats, vecs, latents, target_noise, label, step_value, orient, extent):
    grads, bias_grads = ({}, {})
    half, full = (place.half, place.full)
    turned = orient != 1
    seen = lax.iota(jnp.int32, TOKENS) < extent * FRAME
    mask = seen.astype(jnp.float32)[:, None]
    denominator = (extent * FRAME * (C // GROUPS)).astype(jnp.float32)
    frame = frame_of(place, latents, target_noise, turned)
    noise_img = frame[:, LC:]
    share = noise_level(step_value)
    noisy = mask * (jnp.sqrt(share) * frame[:, :LC] + jnp.sqrt(1.0 - share) * noise_img)

    embed_in = low(time_embed(step_value))[None]
    pre_one = dot(embed_in, mats["w_t1"]) + vecs["b_t1"]
    hidden_one = low(jax.nn.silu(pre_one))
    pre_two = dot(hidden_one, mats["w_t2"]) + vecs["b_t2"]
    hidden_two = low(jax.nn.silu(pre_two))
    time_vec = dot(hidden_two, mats["w_tp"]) + vecs["b_tp"]
    class_vec = lax.dynamic_slice(mats["table"], (label, 0), (1, C)).astype(jnp.float32)

    pad_in = windows(low(noisy), turned, 1)
    state_zero = mask * (dot(pad_in, half(mats["w_in"])) + half(vecs["b_in"]))
    norm_one, normed_one, inv_one = group_forward(
        state_zero, mask, denominator, half(vecs["g1"]), half(vecs["bb1"])
    )
    pad_one = windows(full(low(mask * jax.nn.silu(norm_one))), turned, 1)
    conv_one = mask * (
        dot(pad_one, half(mats["w_c1"])) + half(vecs["b_c1"]) + half(time_vec)
    )
    norm_two, normed_two, inv_two = group_forward(
        conv_one, mask, denominator, half(vecs["g2"]), half(vecs["bb2"])
    )
    pad_two = windows(full(low(mask * jax.nn.silu(norm_two))), turned, 1)
    state_one = state_zero + mask * (dot(pad_two, half(mats["w_c2"])) + half(vecs["b_c2"]))
    norm_three, normed_three, inv_three = group_forward(
        state_one, mask, denominator, half(vecs["g3"]), half(vecs["bb3"])
    )
    token_in = full(low(norm_three))
    resid_zero = dot(token_in, mats["w_pin"]) + vecs["b_pin"]
    ln_one, normed_ln1, inv_ln1 = layer_forward(resid_zero, vecs["n1g"], vecs["n1b"])
    qkv_own = own_columns(place, mats["w_qkv"])
    packed = low(dot(ln_one, qkv_own))
    query, key, value = [heads_of(packed[:, i * HALF : (i + 1) * HALF]) for i in range(3)]
    attended_own, log_total = attend(query, key, value, seen)
    attended = full(attended_own)
    resid_one = resid_zero + dot(attended, mats["w_o"]) + vecs["b_o"]
    ln_two, normed_ln2, inv_ln2 = layer_forward(resid_one, vecs["n2g"], vecs["n2b"])
    cq_own = half(mats["w_cq"])
    cross_query = heads_of(low(dot(ln_two, cq_own)))
    context = low(jnp.concatenate([class_vec, time_vec], axis=0))
    ckv_own = own_columns(place, mats["w_ckv"])
    context_kv = low(dot(context, ckv_own))
    cross_prob, cross_own = cross_attend(cross_query, context_kv)
    cross_out = full(cross_own)
    resid_two = resid_one + dot(cross_out, mats["w_co"]) + vecs["b_co"]
    ln_three, normed_ln3, inv_ln3 = layer_forward(resid_two, vecs["n3g"], vecs["n3b"])
    ff1_own = own_columns(place, mats["w_ff1"])
    projected = dot(ln_three, ff1_own) + own_columns(place, vecs["b_ff1"][None])
    wide = FFI // 2
    lift, gate = (projected[:, :wide], projected[:, wide:])
    cdf = 0.5 * (1.0 + lax.erf(gate * math.sqrt(0.5)))
    gated_own = low(lift * gate * cdf)
    gated_peer = place.swap(gated_own)
    gated = jnp.concatenate(
        [
            place.join(gated_own[:, i * HALF : (i + 1) * HALF], gated_peer[:, i * HALF : (i + 1) * HALF])
            for i in range(FFI // WIDE)
        ],
        axis=1,
    )
    resid_three = resid_two + dot(gated, mats["w_ff2"]) + vecs["b_ff2"]
    out_in = low(resid_three)
    branch = dot(out_in, half(mats["w_pout"])) + half(vecs["b_pout"])
    state_two = state_one + mask * branch
    pad_out = windows(full(low(state_two)), turned, 1)
    predicted = dot(pad_out, mats["w_out"]) + vecs["b_out"]
    residual_err = predicted - noise_img
    loss = jnp.sum(mask * residual_err * residual_err)

    out_grad = 2.0 * mask * residual_err
    bias_grads["b_out"] = jnp.sum(out_grad, axis=0)
    out_low = low(out_grad)
    grads["w_out"] = half(t_dot(pad_out, out_low).reshape(9 * LC, C))
    w_out_back = jnp.transpose(mats["w_out"].reshape(9, C, LC), (0, 2, 1)).reshape(9 * LC, C)
    state_grad = dot(windows(out_low, turned, -1), w_out_back)
    branch_grad = mask * state_grad
    state_grad = half(state_grad)
    bias_grads["b_pout"] = half(jnp.sum(branch_grad, axis=0))
    grad_low = low(branch_grad)
    grads["w_pout"] = t_dot(out_in, half(grad_low))
    resid_grad = dot_t(grad_low, mats["w_pout"])
    bias_grads["b_ff2"] = half(jnp.sum(resid_grad, axis=0))
    grad_low = low(resid_grad)
    grads["w_ff2"] = t_dot(gated, half(grad_low))
    ff2_own = pick(mats["w_ff2"].reshape(-1, 2, HALF, C), place.side, 1).reshape(wide, C)
    gated_grad = dot_t(grad_low, ff2_own)
    density = jnp.exp(-0.5 * gate * gate) * (1.0 / math.sqrt(2.0 * math.pi))
    proj_grad = jnp.concatenate(
        [gated_grad * gate * cdf, gated_grad * lift * (cdf + gate * density)], axis=1
    )
    bias_grads["b_ff1"] = jnp.sum(proj_grad, axis=0)
    grad_low = low(proj_grad)
    grads["w_ff1"] = t_dot(ln_three, grad_low)
    ln_grad = dot_t(grad_low, ff1_own)
    ln_grad = ln_grad + place.swap(ln_grad)
    ln_grad, gain, bias = layer_backward(ln_grad, normed_ln3, inv_ln3, vecs["n3g"])
    bias_grads["n3g"], bias_grads["n3b"] = (half(gain), half(bias))
    resid_grad = resid_grad + ln_grad
    bias_grads["b_co"] = half(jnp.sum(resid_grad, axis=0))
    grad_low = low(resid_grad)
    grads["w_co"] = t_dot(cross_out, half(grad_low))
    cross_grad = heads_of(low(dot_t(grad_low, half(mats["w_co"], 0))))
    query_grad, kv_grad = cross_back(cross_query, context_kv, cross_prob, cross_grad)
    query_low, kv_low = (low(query_grad), low(kv_grad))
    grads["w_cq"] = t_dot(ln_two, query_low)
    grads["w_ckv"] = t_dot(context, kv_low)
    context_grad = dot_t(kv_low, ckv_own)
    context_grad = context_grad + place.swap(context_grad)
    ln_grad = dot_t(full(query_low), mats["w_cq"])
    ln_grad, gain, bias = layer_backward(ln_grad, normed_ln2, inv_ln2, vecs["n2g"])
    bias_grads["n2g"], bias_grads["n2b"] = (half(gain), half(bias))
    resid_grad = resid_grad + ln_grad
    bias_grads["b_o"] = half(jnp.sum(resid_grad, axis=0))
    grad_low = low(resid_grad)
    grads["w_o"] = t_dot(attended, half(grad_low))
    attended_grad = heads_of(low(dot_t(grad_low, half(mats["w_o"], 0))))
    packed_grad = attend_back(query, key, value, seen, log_total, attended_grad)
    grads["w_qkv"] = t_dot(ln_one, packed_grad)
    ln_grad = dot_t(packed_grad, qkv_own)
    ln_grad = ln_grad + place.swap(ln_grad)
    ln_grad, gain, bias = layer_backward(ln_grad, normed_ln1, inv_ln1, vecs["n1g"])
    bias_grads["n1g"], bias_grads["n1b"] = (half(gain), half(bias))
    resid_grad = resid_grad + ln_grad
    bias_grads["b_pin"] = half(jnp.sum(resid_grad, axis=0))
    grad_low = low(resid_grad)
    grads["w_pin"] = t_dot(token_in, half(grad_low))
    token_grad = dot_t(grad_low, half(mats["w_pin"], 0))
    norm_grad, bias_grads["g3"], bias_grads["bb3"] = group_backward(
        token_grad, normed_three, inv_three, mask, denominator, half(vecs["g3"])
    )
    state_grad = state_grad + norm_grad

    conv_grad = mask * state_grad
    bias_grads["b_c2"] = jnp.sum(conv_grad, axis=0)
    conv_low = low(conv_grad)
    grads["w_c2"] = t_dot(pad_two, conv_low)
    act_grad = conv_input_grad(place, full(conv_low), mats["w_c2"], turned)
    conv_grad, bias_grads["g2"], bias_grads["bb2"] = group_backward(
        mask * act_grad * silu_slope(norm_two),
        normed_two,
        inv_two,
        mask,
        denominator,
        half(vecs["g2"]),
    )
    conv_sum = jnp.sum(conv_grad, axis=0)
    bias_grads["b_c1"] = conv_sum
    conv_low = low(conv_grad)
    grads["w_c1"] = t_dot(pad_one, conv_low)
    act_grad = conv_input_grad(place, full(conv_low), mats["w_c1"], turned)
    norm_grad, bias_grads["g1"], bias_grads["bb1"] = group_backward(
        mask * act_grad * silu_slope(norm_one),
        normed_one,
        inv_one,
        mask,
        denominator,
        half(vecs["g1"]),
    )
    in_grad = mask * (state_grad + norm_grad)
    bias_grads["b_in"] = jnp.sum(in_grad, axis=0)
    grads["w_in"] = t_dot(pad_in, low(in_grad))

    time_grad = full(conv_sum[None]) + context_grad[1:2]
    bias_grads["b_tp"] = half(time_grad[0])
    time_low = low(time_grad)
    grads["w_tp"] = outer(hidden_two, half(time_low))
    pre_grad = dot_t(time_low, mats["w_tp"]) * silu_slope(pre_two)
    bias_grads["b_t2"] = own_columns(place, pre_grad)[0]
    pre_low = low(pre_grad)
    grads["w_t2"] = outer(hidden_one, own_columns(place, pre_low))
    pre_grad = dot_t(pre_low, mats["w_t2"]) * silu_slope(pre_one)
    bias_grads["b_t1"] = own_columns(place, pre_grad)[0]
    grads["w_t1"] = outer(embed_in, own_columns(place, low(pre_grad)))
    rows = lax.iota(jnp.int32, NCLS)[:, None] == label
    grads["table"] = jnp.where(rows, half(context_grad[0:1]), 0.0)
    return (grads, bias_grads, loss)


def outer(inputs, gradient):
    return inputs.astype(jnp.float32).reshape(-1, 1) * gradient.astype(jnp.float32)


def conv_input_grad(place, gradient, weight, turned):
    moved = windows(gradient, turned, -1).reshape(TOKENS, 9, C)
    own = place.half(weight.reshape(9, C, C), 1)
    return lax.dot_general(
        moved, own, (((1, 2), (0, 2)), ((), ())), preferred_element_type=jnp.float32
    )


def adam_update(params, first_mom, second, gradient, decay_rate):
    first_new = adam_one * first_mom + (1.0 - adam_one) * gradient
    second_new = adam_two * second + (1.0 - adam_two) * gradient * gradient
    step_size = (
        first_new
        / (1.0 - adam_one**STEP)
        / (jnp.sqrt(second_new / (1.0 - adam_two**STEP)) + adam_eps)
    )
    return (params - learn_rate * (step_size + decay_rate * params), first_new, second_new)


def local(
    latents,
    target_noise,
    labels,
    timesteps,
    orient,
    extent,
    mat_params,
    mat_first,
    mat_second,
    mat_ema,
    vec_params,
    vec_first,
    vec_second,
    vec_ema,
):
    place = Place()
    length = mat_params.shape[0]
    rows = shard_rows(length * place.count, place.count)
    block = to_blocks(place, mat_params.astype(jnp.bfloat16), rows)
    table = lax.all_gather(block, ("dp", "rows"), axis=0, tiled=True)
    mats, at = ({}, LEAD)
    for name, depth, width in mat_layout():
        count = depth * width // WIDE
        mats[name] = table[at : at + count].reshape(depth, width)
        if name == "w_in":
            mats[name] = table[at : at + count]
        at += count
    vec_len = vec_params.shape[0]
    vec_wide = -(-vec_len // 128) * 128
    padded = jnp.pad(vec_params, (0, vec_wide - vec_len)).reshape(-1, 128)
    vec_all = gather_small(place, padded).reshape(place.count, vec_wide)[:, :vec_len]
    vec_all = vec_all.reshape(-1).astype(jnp.bfloat16).astype(jnp.float32)
    vecs = unpack(vec_all, vec_layout())
    own = lambda values: pick(values, place.slot, 0)
    grads, bias_grads, loss = train_step(
        place,
        mats,
        vecs,
        latents,
        target_noise,
        own(labels),
        own(timesteps),
        own(orient),
        own(extent),
    )
    pieces = [jnp.zeros((LEAD, HALF), jnp.float32)]
    pieces += [grads[record[0]].reshape(-1, HALF) for record in mat_layout()]
    used = sum(piece.shape[0] for piece in pieces)
    pieces.append(jnp.zeros((place.count * rows - used, HALF), jnp.float32))
    grad_rows = jnp.concatenate(pieces, axis=0)

    small = [bias_grads[record[0]].reshape(-1, HALF) for record in vec_layout()[:-1]]
    count_local = (own(extent) * FRAME).astype(jnp.float32)
    extra = jnp.concatenate([bias_grads["b_out"], jnp.stack([loss, count_local])])
    extra = jnp.pad(extra, (0, HALF - LC - 2))[None]
    small = jnp.concatenate(small + [extra], axis=0)
    small = jnp.pad(small, ((0, -small.shape[0] % 8), (0, 0)))
    small = place.full(place.chip_sum(small))
    body = sum(record[1] for record in vec_layout()[:-1]) // WIDE
    loss_sum, pixel_count = (small[body, LC], small[body, LC + 1])
    vec_flat = jnp.concatenate([small[:body].reshape(-1), small[body, :LC]])
    vec_flat = jnp.pad(vec_flat, (0, vec_len * place.count - vec_flat.shape[0]))
    shard_vec = lax.dynamic_slice(vec_flat, (vec_len * place.index,), (vec_len,))

    block_grad = scatter_sum(place, grad_rows, rows)
    shard_mat = from_blocks(place, block_grad, length)
    square = jnp.sum(block_grad * block_grad).reshape(1, 1)
    square = place.chip_sum(square + place.swap(square))[0, 0]
    square = square + jnp.sum(vec_flat * vec_flat)
    inverse = 1.0 / pixel_count
    grad_norm = jnp.sqrt(square) * inverse
    factor = clip_norm / jnp.maximum(grad_norm, clip_norm) * inverse
    new_mat, mat_first_new, mat_second_new = adam_update(
        mat_params, mat_first, mat_second, shard_mat * factor, weight_decay
    )
    new_vec, vec_first_new, vec_second_new = adam_update(
        vec_params, vec_first, vec_second, shard_vec * factor, 0.0
    )
    ema_rate = min(ema_ceiling, (1.0 + STEP) / (10.0 + STEP))
    mat_ema_new = ema_rate * mat_ema + (1.0 - ema_rate) * new_mat
    vec_ema_new = ema_rate * vec_ema + (1.0 - ema_rate) * new_vec
    return (
        new_mat,
        mat_first_new,
        mat_second_new,
        mat_ema_new,
        new_vec,
        vec_first_new,
        vec_second_new,
        vec_ema_new,
        grad_norm,
        loss_sum,
        pixel_count,
    )


def solution(mesh):
    return jax.shard_map(
        local,
        mesh=mesh,
        in_specs=(
            P("dp", "rows", None, None),
            P("dp", "rows", None, None),
            P("dp"),
            P("dp"),
            P("dp"),
            P("dp"),
            P(("dp", "rows")),
            P(("dp", "rows")),
            P(("dp", "rows")),
            P(("dp", "rows")),
            P(("dp", "rows")),
            P(("dp", "rows")),
            P(("dp", "rows")),
            P(("dp", "rows")),
        ),
        out_specs=(
            P(("dp", "rows")),
            P(("dp", "rows")),
            P(("dp", "rows")),
            P(("dp", "rows")),
            P(("dp", "rows")),
            P(("dp", "rows")),
            P(("dp", "rows")),
            P(("dp", "rows")),
            P(),
            P(),
            P(),
        ),
        check_vma=False,
    )
```

profile of v0, /device:TPU:4, one launch (start us, length us, event | category | flops | bytes accessed | tf_op | source)
XLA Modules:
  0.0 941.2 jit_solution(16367085320493448208)
XLA Ops:
  15.1 5.3 concatenate.369
  35.2 3.7 collective-permute-done.5
  49.8 134.4 %all-gather.2.cloned.1.call-done = bf16[25344,512]{1,0:T(8,128)(2,1)} async-done(((bf16[792,512]{1,0:T(8,128)(2,1)}), bf16[25344,512]{1,0:T(8,128)(2,1)}) %all-gather.2.cloned.1.call-update) | async-done | bytes 25952272 | tf_op jit(solution)/shard_map/all_gather | solution.py:718
  190.9 4.5 fusion.335
  199.4 6.6 fusion.337
  228.6 4.6 copy.101
  275.9 3.7 fusion.58
  320.2 5.5 fusion.200
  325.7 5.1 reshape.673
  333.1 3.8 fusion.206
  361.0 8.6 fusion.98
  369.6 8.7 fusion.101
  400.6 3.7 fusion.378
  416.0 6.7 copy.133
  422.7 4.7 multiply_reduce_fusion.21
  429.1 6.1 fusion.377
  460.8 6.7 copy.135
  467.6 5.0 multiply_reduce_fusion.17
  473.4 69.6 %concatenate.461 = f32[25344,256]{1,0:T(8,128)} concatenate(f32[5,256]{1,0:T(8,128)S(1)} %broadcast_in_dim.144, f32[27,256]{1,0:T(8,128)S(1)} %fusion.211, f32[512,256]{1,0:T(8,128)} %broadcast_multiply_fusion.2, f32[2048,256]{1,0:T(8,128)} %broadcast_multiply_fusion, f32[1024,256]{1,0:T(8,128)} %broadcast_multiply_fusion.1, f32[1000,256]{1,0:T(8,128)} %broadcast_select_fusion, ...), dimensions={0} | concatenate | bytes 51904512 | tf_op jit(solution)/shard_map/concatenate | solution.py:748
  543.0 10.0 %abs_reduce_fusion = f32[]{:T(128)} fusion(f32[25344,256]{1,0:T(8,128)} %concatenate.461), kind=kLoop, calls=%fused_computation.1 | loop fusion | flops 12976127 | bytes 25952260 | tf_op jit(solution)/shard_map/reduce_max | solution.py:300
  552.9 17.7 %fusion.333 = (f32[4,2,2,712,256]{4,3,2,1,0:T(8,128)}, f32[4,2,2,712,256]{4,3,2,1,0:T(8,128)}) fusion(f32[4,2,2,1584,256]{4,3,2,1,0:T(8,128)} %bitcast.400), kind=kLoop, calls=%fused_computation.678 | loop fusion | bytes 46661632 | tf_op jit(solution)/shard_map/slice | solution.py:310
  571.3 7.6 constant_dynamic-slice_fusion.3
  581.7 5.1 fusion.10
  590.2 54.7 %collective-permute-start.23 = (f32[1,1]{1,0:T(1,128)}, f32[1,1]{1,0:T(1,128)}, u32[]{:S(2)}, u32[]{:S(2)}) collective-permute-start(f32[1,1]{1,0:T(1,128)} %bitcast.85), channel_id=1, source_target_pairs={{0,2},{1,3},{2,0},{3,1},{4,6},{5,7},{6,4},{7,5},{8,10},{9,11},{10,... | collective-permute-start | bytes 20 | tf_op jit(solution)/shard_map/ppermute | solution.py:169
  644.9 6.2 collective-permute-start.39
  656.1 4.3 fusion.2
  676.6 16.9 %collective-permute-start.55 = (f32[1,1]{1,0:T(1,128)}, f32[1,1]{1,0:T(1,128)}, u32[]{:S(2)}, u32[]{:S(2)}) collective-permute-start(f32[1,1]{1,0:T(1,128)} %bitcast.85), channel_id=1, source_target_pairs={{0,8},{1,9},{2,10},{3,11},{4,12},{5,13},{6,14},{7,15}} | collective-permute-start | bytes 20 | tf_op jit(solution)/shard_map/ppermute | solution.py:169
  697.8 3.8 collective-permute-start.56
  713.8 8.3 collective-permute-start.57
  727.9 4.7 collective-permute-start.27
  735.1 8.5 collective-permute-start.43
  744.3 4.7 collective-permute-start.59
  751.5 3.7 collective-permute-done.65
  760.8 4.9 collective-permute-start.29
  766.5 7.1 collective-permute-start.45
  776.1 3.7 collective-permute-done.51
  788.7 6.7 collective-permute-start.31
  813.2 4.7 collective-permute-start.58
  820.9 5.9 collective-permute-start.26
  829.6 12.9 %collective-permute-done.26 = f16[712,256]{1,0:T(8,128)(2,1)S(1)} collective-permute-done((f16[712,256]{1,0:T(8,128)(2,1)S(1)}, f16[712,256]{1,0:T(8,128)(2,1)S(1)}, u32[]{:S(2)}, u32[]{:S(2)}) %collective-permute-start.26) | collective-permute-done | bytes 364576 | tf_op jit(solution)/shard_map/ppermute | solution.py:169
  843.3 5.0 collective-permute-start.28
  849.6 4.8 collective-permute-start.44
  859.2 11.2 %collective-permute-start.30 = (f16[712,256]{1,0:T(8,128)(2,1)S(1)}, f16[712,256]{1,0:T(8,128)(2,1)S(1)}, u32[]{:S(2)}, u32[]{:S(2)}) collective-permute-start(f16[712,256]{1,0:T(8,128)(2,1)S(1)} %get-tuple-element.100), channel_id=1, source_target_pairs={{0,8},{1,9},{2,10},{3,11},{4,12},{5,13},{6,14},{7,15},{8,16},{9,17... | collective-permute-start | bytes 1093640 | tf_op jit(solution)/shard_map/ppermute | solution.py:169
  875.4 4.6 collective-permute-done.36
  880.6 4.2 collective-permute-start.79
  905.4 4.0 collective-permute-start.73
  919.1 3.7 collective-permute-start.76
  925.8 7.2 multiply_add_fusion
  (950 shorter events, 338.9 us)
Async XLA Ops:
  7.2 176.9 %all-gather.2.cloned.1.call-start = ((), (), s32[]{:S(2)}) async-start(), calls=%async_computation | async-start | bytes 26763264 | tf_op jit(solution)/shard_map/all_gather | solution.py:718
  8.8 6.3 collective-permute-start.2
  22.3 7.8 collective-permute-start.3
  23.3 17.2 %collective-permute-start = (f32[1,2,8,32,6]{3,2,0,4,1:T(8,128)S(1)}, f32[1,2,8,32,6]{3,2,0,4,1:T(8,128)S(1)}, u32[]{:S(2)}, u32[]{:S(2)}) collective-permute-start(f32[1,2,8,32,6]{3,2,0,4,1:T(8,128)S(1)} %maximum_bitcast_fusion), channel_id=1, source_target_pairs={{0,1},{1,0},{2,3},{3,2},{4,5},{5,4},{6,7},{7,6},{8,9},{9,8},{10,11... | collective-permute-start | bytes 36872 | tf_op jit(solution)/shard_map/ppermute | solution.py:169
  43.4 6.0 collective-permute-start.7
  186.8 22.4 %collective-permute-start.8 = (bf16[512,256]{1,0:T(8,128)(2,1)S(1)}, bf16[512,256]{1,0:T(8,128)(2,1)S(1)}, u32[]{:S(2)}, u32[]{:S(2)}) collective-permute-start(bf16[512,256]{1,0:T(8,128)(2,1)S(1)} %multiply_convert_fusion.13), channel_id=1, source_target_pairs={{0,1},{1,0},{2,3},{3,2},{4,5},{5,4},{6,7},{7,6},{8,9},{9,8},{10,11... | collective-permute-start | bytes 786440 | tf_op jit(solution)/shard_map/ppermute | solution.py:169
  225.5 12.8 %collective-permute-start.10 = (bf16[512,256]{1,0:T(8,128)(2,1)S(1)}, bf16[512,256]{1,0:T(8,128)(2,1)}, u32[]{:S(2)}, u32[]{:S(2)}) collective-permute-start(bf16[512,256]{1,0:T(8,128)(2,1)S(1)} %add_convert_fusion.3), channel_id=1, source_target_pairs={{0,1},{1,0},{2,3},{3,2},{4,5},{5,4},{6,7},{7,6},{8,9},{9,8},{10,11... | collective-permute-start | bytes 786440 | tf_op jit(solution)/shard_map/ppermute | solution.py:169
  281.2 12.9 %collective-permute-start.14 = (bf16[512,256]{1,0:T(8,128)(2,1)}, bf16[512,256]{1,0:T(8,128)(2,1)}, u32[]{:S(2)}, u32[]{:S(2)}) collective-permute-start(bf16[512,256]{1,0:T(8,128)(2,1)} %fusion.104), channel_id=1, source_target_pairs={{0,1},{1,0},{2,3},{3,2},{4,5},{5,4},{6,7},{7,6},{8,9},{9,8},{10,11... | collective-permute-start | bytes 786440 | tf_op jit(solution)/shard_map/ppermute | solution.py:169
  314.0 22.9 %collective-permute-start.15 = (f32[512,512]{0,1:T(8,128)}, f32[512,512]{0,1:T(8,128)}, u32[]{:S(2)}, u32[]{:S(2)}) collective-permute-start(f32[512,512]{0,1:T(8,128)} %fusion.202), channel_id=1, source_target_pairs={{0,1},{1,0},{2,3},{3,2},{4,5},{5,4},{6,7},{7,6},{8,9},{9,8},{10,11... | collective-permute-start | bytes 3145736 | tf_op jit(solution)/shard_map/ppermute | solution.py:169
  346.1 41.1 %collective-permute-start.21 = (f32[2,512]{1,0:T(2,128)S(1)}, f32[2,512]{1,0:T(2,128)S(1)}, u32[]{:S(2)}, u32[]{:S(2)}) collective-permute-start(f32[2,512]{1,0:T(2,128)S(1)} %fusion.375), channel_id=1, source_target_pairs={{0,1},{1,0},{2,3},{3,2},{4,5},{5,4},{6,7},{7,6},{8,9},{9,8},{10,11... | collective-permute-start | bytes 12296 | tf_op jit(solution)/shard_map/ppermute | solution.py:169
  383.2 11.0 %collective-permute-start.17 = (f32[512,512]{0,1:T(8,128)}, f32[512,512]{0,1:T(8,128)}, u32[]{:S(2)}, u32[]{:S(2)}) collective-permute-start(f32[512,512]{0,1:T(8,128)} %fusion.199), channel_id=1, source_target_pairs={{0,1},{1,0},{2,3},{3,2},{4,5},{5,4},{6,7},{7,6},{8,9},{9,8},{10,11... | collective-permute-start | bytes 3145736 | tf_op jit(solution)/shard_map/ppermute | solution.py:169
  428.6 6.6 collective-permute-start.20
  428.8 20.7 %collective-permute-start.19 = (bf16[512,256]{1,0:T(8,128)(2,1)S(1)}, bf16[512,256]{1,0:T(8,128)(2,1)}, u32[]{:S(2)}, u32[]{:S(2)}) collective-permute-start(bf16[512,256]{1,0:T(8,128)(2,1)S(1)} %get-tuple-element.112), channel_id=1, source_target_pairs={{0,1},{1,0},{2,3},{3,2},{4,5},{5,4},{6,7},{7,6},{8,9},{9,8},{10,11... | collective-permute-start | bytes 786440 | tf_op jit(solution)/shard_map/ppermute | solution.py:169
  581.2 74.9 %collective-permute-start.22 = (f16[4,2,712,256]{3,2,0,1:T(8,128)(2,1)}, f16[4,2,712,256]{3,2,0,1:T(8,128)(2,1)}, u32[]{:S(2)}, u32[]{:S(2)}) collective-permute-start(f16[4,2,712,256]{3,2,0,1:T(8,128)(2,1)} %fusion.11), channel_id=1, source_target_pairs={{0,2},{1,3},{2,0},{3,1},{4,6},{5,7},{6,4},{7,5},{8,10},{9,11},{10,... | collective-permute-start | bytes 8749064 | tf_op jit(solution)/shard_map/ppermute | solution.py:169
  586.8 75.6 %collective-permute-start.38 = (f16[4,2,712,256]{3,2,1,0:T(8,128)(2,1)}, f16[4,2,712,256]{3,2,1,0:T(8,128)(2,1)}, u32[]{:S(2)}, u32[]{:S(2)}) collective-permute-start(f16[4,2,712,256]{3,2,1,0:T(8,128)(2,1)} %fusion.10), channel_id=1, source_target_pairs={{0,4},{1,5},{2,6},{3,7},{4,0},{5,1},{6,2},{7,3},{8,12},{9,13},{10,... | collective-permute-start | bytes 8749064 | tf_op jit(solution)/shard_map/ppermute | solution.py:169
  590.2 63.1 %collective-permute-start.23 = (f32[1,1]{1,0:T(1,128)}, f32[1,1]{1,0:T(1,128)}, u32[]{:S(2)}, u32[]{:S(2)}) collective-permute-start(f32[1,1]{1,0:T(1,128)} %bitcast.85), channel_id=1, source_target_pairs={{0,2},{1,3},{2,0},{3,1},{4,6},{5,7},{6,4},{7,5},{8,10},{9,11},{10,... | collective-permute-start | bytes 20 | tf_op jit(solution)/shard_map/ppermute | solution.py:169
  644.9 9.1 collective-permute-start.39
  661.9 151.4 %collective-permute-start.24 = (f16[4,712,256]{2,1,0:T(8,128)(2,1)}, f16[4,712,256]{2,1,0:T(8,128)(2,1)}, u32[]{:S(2)}, u32[]{:S(2)}) collective-permute-start(f16[4,712,256]{2,1,0:T(8,128)(2,1)} %fusion.44), channel_id=1, source_target_pairs={{0,4},{1,5},{2,6},{3,7},{4,0},{5,1},{6,2},{7,3},{8,12},{9,13},{10,... | collective-permute-start | bytes 4374536 | tf_op jit(solution)/shard_map/ppermute | solution.py:169
  669.7 135.3 %collective-permute-start.40 = (f16[2,712,256]{2,1,0:T(8,128)(2,1)}, f16[2,712,256]{2,1,0:T(8,128)(2,1)}, u32[]{:S(2)}, u32[]{:S(2)}) collective-permute-start(f16[2,712,256]{2,1,0:T(8,128)(2,1)} %get-tuple-element.98), channel_id=1, source_target_pairs={{0,8},{1,9},{2,10},{3,11},{4,12},{5,13},{6,14},{7,15}} | collective-permute-start | bytes 2187272 | tf_op jit(solution)/shard_map/ppermute | solution.py:169
  673.0 22.9 %collective-permute-start.54 = (f16[2,2,160,256]{3,2,1,0:T(8,128)(2,1)}, f16[2,2,160,256]{3,2,1,0:T(8,128)(2,1)}, u32[]{:S(2)}, u32[]{:S(2)}) collective-permute-start(f16[2,2,160,256]{3,2,1,0:T(8,128)(2,1)} %get-tuple-element.106), channel_id=1, source_target_pairs={{0,8},{1,9},{2,10},{3,11},{4,12},{5,13},{6,14},{7,15}} | collective-permute-start | bytes 983048 | tf_op jit(solution)/shard_map/ppermute | solution.py:169
  676.6 18.2 %collective-permute-start.55 = (f32[1,1]{1,0:T(1,128)}, f32[1,1]{1,0:T(1,128)}, u32[]{:S(2)}, u32[]{:S(2)}) collective-permute-start(f32[1,1]{1,0:T(1,128)} %bitcast.85), channel_id=1, source_target_pairs={{0,8},{1,9},{2,10},{3,11},{4,12},{5,13},{6,14},{7,15}} | collective-permute-start | bytes 20 | tf_op jit(solution)/shard_map/ppermute | solution.py:169
  693.4 114.2 %collective-permute-start.60 = (f16[2,2,160,256]{3,2,1,0:T(8,128)(2,1)}, f16[2,2,160,256]{3,2,1,0:T(8,128)(2,1)}, u32[]{:S(2)}, u32[]{:S(2)}) collective-permute-start(f16[2,2,160,256]{3,2,1,0:T(8,128)(2,1)} %get-tuple-element.107), channel_id=1, source_target_pairs={{24,16},{25,17},{26,18},{27,19},{28,20},{29,21},{30,22},{31,23}} | collective-permute-start | bytes 983048 | tf_op jit(solution)/shard_map/ppermute | solution.py:169
  697.8 113.4 %collective-permute-start.56 = (f16[2,2,160,256]{3,2,1,0:T(8,128)(2,1)}, f16[2,2,160,256]{3,2,1,0:T(8,128)(2,1)}, u32[]{:S(2)}, u32[]{:S(2)}) collective-permute-start(f16[2,2,160,256]{3,2,1,0:T(8,128)(2,1)} %fusion.161), channel_id=1, source_target_pairs={{0,8},{1,9},{2,10},{3,11},{4,12},{5,13},{6,14},{7,15},{8,16},{9,17... | collective-permute-start | bytes 983048 | tf_op jit(solution)/shard_map/ppermute | solution.py:169
  713.8 9.0 collective-permute-start.57
  735.1 9.2 collective-permute-start.43
  766.5 7.8 collective-permute-start.45
  788.7 7.4 collective-permute-start.31
  803.3 53.7 %collective-permute-start.77 = (f32[40,256]{1,0:T(8,128)S(1)}, f32[40,256]{1,0:T(8,128)S(1)}, u32[]{:S(2)}, u32[]{:S(2)}) collective-permute-start(f32[40,256]{1,0:T(8,128)S(1)} %pad.74), channel_id=1, source_target_pairs={{0,2},{1,3},{2,0},{3,1},{4,6},{5,7},{6,4},{7,5},{8,10},{9,11},{10,... | collective-permute-start | bytes 122888 | tf_op jit(solution)/shard_map/ppermute | solution.py:169
  805.0 21.9 %collective-permute-start.46 = (f16[2,712,256]{2,1,0:T(8,128)(2,1)S(1)}, f16[2,712,256]{2,1,0:T(8,128)(2,1)S(1)}, u32[]{:S(2)}, u32[]{:S(2)}) collective-permute-start(f16[2,712,256]{2,1,0:T(8,128)(2,1)S(1)} %get-tuple-element.99), channel_id=1, source_target_pairs={{24,16},{25,17},{26,18},{27,19},{28,20},{29,21},{30,22},{31,23}} | collective-permute-start | bytes 2187272 | tf_op jit(solution)/shard_map/ppermute | solution.py:169
  807.6 20.6 %collective-permute-start.42 = (f16[2,712,256]{2,1,0:T(8,128)(2,1)S(1)}, f16[2,712,256]{2,1,0:T(8,128)(2,1)S(1)}, u32[]{:S(2)}, u32[]{:S(2)}) collective-permute-start(f16[2,712,256]{2,1,0:T(8,128)(2,1)S(1)} %fusion.50), channel_id=1, source_target_pairs={{0,8},{1,9},{2,10},{3,11},{4,12},{5,13},{6,14},{7,15},{8,16},{9,17... | collective-permute-start | bytes 2187272 | tf_op jit(solution)/shard_map/ppermute | solution.py:169
  812.5 8.3 collective-permute-start.62
  813.2 30.0 %collective-permute-start.58 = (f16[2,2,160,256]{3,2,1,0:T(8,128)(2,1)S(1)}, f16[2,2,160,256]{3,2,1,0:T(8,128)(2,1)S(1)}, u32[]{:S(2)}, u32[]{:S(2)}) collective-permute-start(f16[2,2,160,256]{3,2,1,0:T(8,128)(2,1)S(1)} %get-tuple-element.104), channel_id=1, source_target_pairs={{0,8},{1,9},{2,10},{3,11},{4,12},{5,13},{6,14},{7,15},{8,16},{9,17... | collective-permute-start | bytes 983048 | tf_op jit(solution)/shard_map/ppermute | solution.py:169
  820.9 21.5 %collective-permute-start.26 = (f16[712,256]{1,0:T(8,128)(2,1)S(1)}, f16[712,256]{1,0:T(8,128)(2,1)S(1)}, u32[]{:S(2)}, u32[]{:S(2)}) collective-permute-start(f16[712,256]{1,0:T(8,128)(2,1)S(1)} %get-tuple-element.102), channel_id=1, source_target_pairs={{0,8},{1,9},{2,10},{3,11},{4,12},{5,13},{6,14},{7,15}} | collective-permute-start | bytes 1093640 | tf_op jit(solution)/shard_map/ppermute | solution.py:169
  826.9 21.4 %collective-permute-start.64 = (f16[2,2,160,256]{3,2,1,0:T(8,128)(2,1)S(1)}, f16[2,2,160,256]{3,2,1,0:T(8,128)(2,1)S(1)}, u32[]{:S(2)}, u32[]{:S(2)}) collective-permute-start(f16[2,2,160,256]{3,2,1,0:T(8,128)(2,1)S(1)} %fusion.159), channel_id=1, source_target_pairs={{8,0},{9,1},{10,2},{11,3},{12,4},{13,5},{14,6},{15,7},{16,8},{17,9... | collective-permute-start | bytes 983048 | tf_op jit(solution)/shard_map/ppermute | solution.py:169
  828.2 21.3 %collective-permute-start.32 = (f16[712,256]{1,0:T(8,128)(2,1)S(1)}, f16[712,256]{1,0:T(8,128)(2,1)S(1)}, u32[]{:S(2)}, u32[]{:S(2)}) collective-permute-start(f16[712,256]{1,0:T(8,128)(2,1)S(1)} %get-tuple-element.103), channel_id=1, source_target_pairs={{24,16},{25,17},{26,18},{27,19},{28,20},{29,21},{30,22},{31,23}} | collective-permute-start | bytes 1093640 | tf_op jit(solution)/shard_map/ppermute | solution.py:169
  842.4 13.0 %collective-permute-start.48 = (f16[2,712,256]{2,1,0:T(8,128)(2,1)S(1)}, f16[2,712,256]{2,1,0:T(8,128)(2,1)S(1)}, u32[]{:S(2)}, u32[]{:S(2)}) collective-permute-start(f16[2,712,256]{2,1,0:T(8,128)(2,1)S(1)} %get-tuple-element.97), channel_id=1, source_target_pairs={{16,8},{17,9},{18,10},{19,11},{20,12},{21,13},{22,14},{23,15},{24,... | collective-permute-start | bytes 2187272 | tf_op jit(solution)/shard_map/ppermute | solution.py:169
  843.3 11.0 %collective-permute-start.28 = (f16[712,256]{1,0:T(8,128)(2,1)S(1)}, f16[712,256]{1,0:T(8,128)(2,1)S(1)}, u32[]{:S(2)}, u32[]{:S(2)}) collective-permute-start(f16[712,256]{1,0:T(8,128)(2,1)S(1)} %fusion.152), channel_id=1, source_target_pairs={{0,8},{1,9},{2,10},{3,11},{4,12},{5,13},{6,14},{7,15},{8,16},{9,17... | collective-permute-start | bytes 1093640 | tf_op jit(solution)/shard_map/ppermute | solution.py:169
  848.5 9.5 %collective-permute-start.66 = (f16[2,160,256]{2,1,0:T(8,128)(2,1)S(1)}, f16[2,160,256]{2,1,0:T(8,128)(2,1)S(1)}, u32[]{:S(2)}, u32[]{:S(2)}) collective-permute-start(f16[2,160,256]{2,1,0:T(8,128)(2,1)S(1)} %fusion.219), channel_id=1, source_target_pairs={{0,2},{1,3},{2,0},{3,1},{4,6},{5,7},{6,4},{7,5},{8,10},{9,11},{10,... | collective-permute-start | bytes 491528 | tf_op jit(solution)/shard_map/ppermute | solution.py:169
  849.6 21.0 %collective-permute-start.44 = (f16[2,712,256]{2,1,0:T(8,128)(2,1)S(1)}, f16[2,712,256]{2,1,0:T(8,128)(2,1)S(1)}, u32[]{:S(2)}, u32[]{:S(2)}) collective-permute-start(f16[2,712,256]{2,1,0:T(8,128)(2,1)S(1)} %get-tuple-element.96), channel_id=1, source_target_pairs={{0,8},{1,9},{2,10},{3,11},{4,12},{5,13},{6,14},{7,15},{8,16},{9,17... | collective-permute-start | bytes 2187272 | tf_op jit(solution)/shard_map/ppermute | solution.py:169
  855.7 16.3 %collective-permute-start.50 = (f16[2,712,256]{2,1,0:T(8,128)(2,1)S(1)}, f16[2,712,256]{2,1,0:T(8,128)(2,1)S(1)}, u32[]{:S(2)}, u32[]{:S(2)}) collective-permute-start(f16[2,712,256]{2,1,0:T(8,128)(2,1)S(1)} %fusion.48), channel_id=1, source_target_pairs={{8,0},{9,1},{10,2},{11,3},{12,4},{13,5},{14,6},{15,7},{16,8},{17,9... | collective-permute-start | bytes 2187272 | tf_op jit(solution)/shard_map/ppermute | solution.py:169
  857.0 23.5 %collective-permute-start.78 = (f32[40,256]{1,0:T(8,128)S(1)}, f32[40,256]{1,0:T(8,128)S(1)}, u32[]{:S(2)}, u32[]{:S(2)}) collective-permute-start(f32[40,256]{1,0:T(8,128)S(1)} %pad_add_fusion), channel_id=1, source_target_pairs={{0,4},{1,5},{2,6},{3,7},{4,0},{5,1},{6,2},{7,3},{8,12},{9,13},{10,... | collective-permute-start | bytes 122888 | tf_op jit(solution)/shard_map/ppermute | solution.py:169
  858.1 15.3 %collective-permute-start.68 = (f16[160,256]{1,0:T(8,128)(2,1)S(1)}, f16[160,256]{1,0:T(8,128)(2,1)S(1)}, u32[]{:S(2)}, u32[]{:S(2)}) collective-permute-start(f16[160,256]{1,0:T(8,128)(2,1)S(1)} %fusion.241), channel_id=1, source_target_pairs={{0,4},{1,5},{2,6},{3,7},{4,0},{5,1},{6,2},{7,3},{8,12},{9,13},{10,... | collective-permute-start | bytes 245768 | tf_op jit(solution)/shard_map/ppermute | solution.py:169
  859.2 16.1 %collective-permute-start.30 = (f16[712,256]{1,0:T(8,128)(2,1)S(1)}, f16[712,256]{1,0:T(8,128)(2,1)S(1)}, u32[]{:S(2)}, u32[]{:S(2)}) collective-permute-start(f16[712,256]{1,0:T(8,128)(2,1)S(1)} %get-tuple-element.100), channel_id=1, source_target_pairs={{0,8},{1,9},{2,10},{3,11},{4,12},{5,13},{6,14},{7,15},{8,16},{9,17... | collective-permute-start | bytes 1093640 | tf_op jit(solution)/shard_map/ppermute | solution.py:169
  870.6 9.4 collective-permute-start.36
  872.5 7.7 collective-permute-start.52
  880.5 14.1 %collective-permute-start.70 = (f32[792,256]{1,0:T(8,128)S(1)}, f32[792,256]{1,0:T(8,128)}, u32[]{:S(2)}, u32[]{:S(2)}) collective-permute-start(f32[792,256]{1,0:T(8,128)S(1)} %dynamic-slice_bitcast_fusion), channel_id=1, source_target_pairs={{0,1},{1,0},{2,3},{3,2},{4,5},{5,4},{6,7},{7,6},{8,9},{9,8},{10,11... | collective-permute-start | bytes 2433032 | tf_op jit(solution)/shard_map/ppermute | solution.py:169
  880.6 6.4 collective-permute-start.79
  898.6 27.2 %collective-permute-start.71 = (f32[109568]{0:T(1024)}, f32[109568]{0:T(1024)}, u32[]{:S(2)}, u32[]{:S(2)}) collective-permute-start(f32[109568]{0:T(1024)} %slice.547), channel_id=1, source_target_pairs={{0,1},{1,2},{2,3},{3,4},{4,5},{5,6},{6,7},{7,8},{8,9},{9,10},{10,1... | collective-permute-start | bytes 1314824 | tf_op jit(solution)/shard_map/ppermute | solution.py:169
  (228 other events, 2628.2 us)
Sparse Core Ops, SparseCore 0:
  22.4 161.7 all-gather.1
where the time goes:
time: 955 us; the launch traced here: 941 us
  starting transfers between devices  245 us (26%)
  local copies, waits for them, and re-layouts  222 us (23%)
  waiting for transfers between devices  187 us (20%)
  other arithmetic  117 us (12%)
  matrix products  112 us (12%)
  between operations  58.9 us (6%)
    ppermute x82, starting transfers between devices, move(): return lax.ppermute(value, ('dp', 'rows'), pairs)  245 us
    all_gather x1, waiting for transfers between devices, local(): table = lax.all_gather(block, ('dp', 'rows'), axis=0, tiled=True)  134 us
    concatenate x1, local copies, waits for them, and re-layouts, local(): grad_rows = jnp.concatenate(pieces, axis=0)  69.6 us
    ppermute x82, waiting for transfers between devices, move(): return lax.ppermute(value, ('dp', 'rows'), pairs)  52.5 us
    dot_general x13, matrix products, t_dot(): lax.dot_general(left, right, (((0,), (0,)), ((), ())), preferred_element_...  32.3 us
    unnamed x42, other arithmetic  25.3 us
    dot_general x17, matrix products, dot(): return jnp.dot(left, right, preferred_element_type=jnp.float32)  23.3 us
    dynamic_slice x14, local copies, waits for them, and re-layouts, pick(): return lax.dynamic_index_in_dim(values, index, axis, keepdims=False)  22.4 us
  transfers between devices with their start and end apart: 83, of which 26 were waited for; matrix products, arithmetic and copies ran while one was open for 20% of the time, Pallas kernels for 0%

commit v1 on v0

--- a/solution.py
+++ b/solution.py
@@ -3,6 +3,8 @@
 import jax
 import jax.numpy as jnp
 from jax import lax
+from jax.experimental import pallas as pl
+from jax.experimental.pallas import tpu as pltpu
 from jax.sharding import PartitionSpec as P
 
 C = 512
@@ -117,7 +119,7 @@
 FRAME = 16
 TOKENS = SIDE * FRAME
 LOCAL_HEADS = HEADS // 2
-WIRE_TOP = 16384.0
+WIRE_TOP = 32768.0
 
 
 def silu_slope(values):
@@ -176,6 +178,14 @@
             value, [(k, k + by) for k in range(self.count) if 0 <= k + by < self.count]
         )
 
+    def rotate(self, value, axis, by):
+        stride, size = (self.strides[axis], self.digits[axis])
+        pairs = []
+        for k in range(self.count):
+            at = (k // stride) % size
+            pairs.append((k, k + ((at + by) % size - at) * stride))
+        return self.move(value, pairs)
+
     def step(self, value, axis, direction, hops):
         stride, size = (self.strides[axis], self.digits[axis])
         pairs = []
@@ -247,72 +257,469 @@
     return lax.dynamic_slice(joined, (start,), (length,))
 
 
-def wire_out(values, bound):
-    return (values * (WIRE_TOP / bound)).astype(jnp.float16)
-
-
-def wire_in(values, bound):
-    return values.astype(jnp.float32) * (bound * (1.0 / WIRE_TOP))
-
-
 def pick(values, index, axis):
     return lax.dynamic_index_in_dim(values, index, axis, keepdims=False)
 
 
-def scatter_pair(place, held, bound, axis, dim):
-    me, stride = (place.coords[axis], place.strides[axis])
-    got = place.swap(wire_out(pick(held, 1 - me, dim), bound), stride)
-    other = place.swap(bound, stride)
-    return (pick(held, me, dim) + wire_in(got, other), bound + other)
-
-
-def scatter_line(place, held, bound, axis, dim):
-    me, size = (place.coords[axis], place.digits[axis])
-    total, limit = (pick(held, me, dim), bound)
-    for direction in (1, -1):
-        rank = me if direction > 0 else size - 1 - me
-        got, other = (None, None)
-        for hops in range(size - 1):
-            aim = jnp.minimum(size - 1 - hops + rank, size - 1)
-            aim = aim if direction > 0 else size - 1 - aim
-            value, top = (pick(held, aim, dim), bound)
-            if got is not None:
-                value, top = (value + wire_in(got, other), top + other)
-            got = place.step(wire_out(value, top), axis, direction, hops)
-            other = place.step(top, axis, direction, hops)
-        total, limit = (total + wire_in(got, other), limit + other)
-    return (total, limit)
-
-
-def scatter_part(place, held, bound, order):
-    left = list(range(len(place.digits)))
+def wire(values):
+    return values.astype(jnp.float16)
+
+
+def plain(values):
+    return values.astype(jnp.float32)
+
+
+def largest_of_all(place, top):
+    stride = 1
+    while stride < place.count:
+        top = jnp.maximum(top, place.swap(top, stride))
+        stride *= 2
+    return top
+
+
+def scatter_part(place, grads, low_row, rows, order, scale):
+    held, left, first, factor = (grads, list(range(len(place.digits))), low_row, scale)
+
+    def part_of(dim, index):
+        starts, sizes, shape = ([], [], [])
+        for at, axis in enumerate(left):
+            starts.append(index if at == dim else 0)
+            sizes.append(1 if at == dim else place.digits[axis])
+            if at != dim:
+                shape.append(place.digits[axis])
+        out = lax.dynamic_slice(held, starts + [first, 0], sizes + [rows, HALF])
+        return out.reshape(shape + [rows, HALF]) * factor
+
     for axis in order:
         dim = left.index(axis)
-        if place.digits[axis] == 2:
-            held, bound = scatter_pair(place, held, bound, axis, dim)
+        me, size = (place.coords[axis], place.digits[axis])
+        total = part_of(dim, me)
+        if size == 2 or axis == order[-1]:
+            for away in range(1, size):
+                sent = wire(part_of(dim, (me + away) % size))
+                total = total + plain(place.rotate(sent, axis, away))
         else:
-            held, bound = scatter_line(place, held, bound, axis, dim)
+            flows = {1: None, -1: None}
+            for hops in range(size - 1):
+                for direction in (1, -1):
+                    rank = me if direction > 0 else size - 1 - me
+                    aim = jnp.minimum(size - 1 - hops + rank, size - 1)
+                    aim = aim if direction > 0 else size - 1 - aim
+                    value = part_of(dim, aim)
+                    if flows[direction] is not None:
+                        value = value + plain(flows[direction])
+                    flows[direction] = place.step(wire(value), axis, direction, hops)
+            total = total + plain(flows[1]) + plain(flows[-1])
+        held, first, factor = (total, 0, 1.0)
         left.remove(axis)
     return held
 
 
-def scatter_sum(place, grads, rows):
-    bound = jnp.maximum(jnp.max(jnp.abs(grads)), 1e-30).reshape(1, 1)
-    bound = jnp.broadcast_to(bound, (8, 128))[:1, :1]
+SHARES = (0.39, 0.39)
+
+
+def scatter_sum(place, grads, scale, rows):
     held = grads.reshape(*place.digits, 2 * rows, HALF)
     axes = list(range(len(place.digits)))[::-1]
-    shares = [0.45, 0.45, 0.1]
     total = 2 * rows
-    cuts = [0] + [int(total * sum(shares[: i + 1]) / 8 + 0.5) * 8 for i in range(2)] + [total]
+    cuts = [0] + [int(total * sum(SHARES[: i + 1]) / 8 + 0.5) * 8 for i in range(2)] + [total]
     parts = []
     for i in range(3):
         order = axes[i:] + axes[:i]
-        piece = held[..., cuts[i] : cuts[i + 1], :]
-        parts.append(scatter_part(place, piece, bound, order))
-    chip = jnp.concatenate(parts, axis=0).reshape(2, rows, HALF)
+        parts.append(scatter_part(place, held, cuts[i], cuts[i + 1] - cuts[i], order, scale))
+    chip = jnp.concatenate(parts, axis=0).reshape(2, rows, HALF) * (1.0 / scale)
     mine = pick(chip, place.side, 0)
     other = place.swap(pick(chip, 1 - place.side, 0))
     return place.join(mine, other)
+
+
+class Store:
+    def __init__(self, place, rows):
+        self.total = place.count * rows
+        self.buffer = None
+        self.top = jnp.zeros((1, 1), jnp.float32)
+        self.places, at = ({}, LEAD)
+        for name, depth, width in mat_layout():
+            self.places[name] = at
+            at += depth * width // WIDE
+
+    def write(self, out, top):
+        self.buffer = out
+        if top is not None:
+            self.top = jnp.maximum(self.top, top)
+
+    def add(self, name, inputs, gradient):
+        if inputs.shape[0] < 16:
+            spare = ((0, 16 - inputs.shape[0]), (0, 0))
+            inputs, gradient = (jnp.pad(inputs, spare), jnp.pad(gradient, spare))
+        grad_into(self, inputs, gradient, self.places[name])
+
+    def put(self, at, values):
+        self.top = jnp.maximum(self.top, jnp.max(jnp.abs(values)).reshape(1, 1))
+        self.buffer = lax.dynamic_update_slice(self.buffer, values, (at, 0))
+
+
+def store_specs(store, at, tile):
+    old = [] if store.buffer is None else [store.buffer]
+    out = pl.BlockSpec(
+        (pl.Element(tile), pl.Element(HALF)), lambda i, *_: (pl.multiple_of(at + tile * i, 8), 0)
+    )
+    shape = jax.ShapeDtypeStruct((store.total, HALF), jnp.float32)
+    return (old, [pl.BlockSpec(memory_space=pl.ANY) for _ in old], out, shape)
+
+
+def grad_into(store, inputs, gradient, at):
+    tokens, depth = inputs.shape
+    pieces = gradient.shape[1] // HALF
+    tile = min(depth, 512 if pieces == 1 else 256 if pieces < 8 else 128)
+    rows, tiles = (tile * pieces, depth // tile)
+    old, old_specs, out_spec, out_shape = store_specs(store, at, rows)
+
+    def body(*refs):
+        refs = refs[len(old) :]
+        input_ref, gradient_ref, out_ref, top_out = refs[:4]
+        step = pl.program_id(0)
+        part = t_dot(input_ref[...], gradient_ref[...])
+        if pieces == 1:
+            out_ref[...] = part
+        else:
+            mixed = refs[-1]
+            for side in range(HALF // 128):
+                for j in range(pieces):
+                    column = j * HALF + side * 128
+                    mixed[pl.ds(j, tile, stride=pieces), :] = part[:, column : column + 128]
+                out_ref[:, side * 128 : (side + 1) * 128] = mixed[...]
+        largest = jnp.max(jnp.abs(part))
+
+        @pl.when(step == 0)
+        def _():
+            top_out[0, 0] = largest
+
+        @pl.when(step > 0)
+        def _():
+            top_out[0, 0] = jnp.maximum(top_out[0, 0], largest)
+
+    out, top = pl.pallas_call(
+        body,
+        grid=(tiles,),
+        in_specs=old_specs
+        + [
+            pl.BlockSpec((tokens, tile), lambda i: (0, i)),
+            pl.BlockSpec(gradient.shape, lambda i: (0, 0)),
+        ],
+        out_specs=[out_spec, pl.BlockSpec(memory_space=pltpu.SMEM)],
+        out_shape=[out_shape, jax.ShapeDtypeStruct((1, 1), jnp.float32)],
+        scratch_shapes=[] if pieces == 1 else [pltpu.VMEM((rows, 128), jnp.float32)],
+        input_output_aliases={k: k for k in range(len(old))},
+        compiler_params=params(),
+        cost_estimate=cost(
+            2 * tokens * depth * gradient.shape[1],
+            depth * gradient.shape[1] * 4 + tokens * depth * 2,
+        ),
+    )(*old, inputs, gradient)
+    store.write(out, top)
+
+
+VMEM_LIMIT = 50 * 1024 * 1024
+PADDED = TOKENS + 2 * FRAME
+
+
+def params():
+    return pltpu.CompilerParams(vmem_limit_bytes=VMEM_LIMIT)
+
+
+def whole(shape):
+    return pl.BlockSpec(shape, lambda *_: (0,) * len(shape))
+
+
+def cost(flops, nbytes):
+    return pl.CostEstimate(flops=flops, bytes_accessed=nbytes, transcendentals=0)
+
+
+def token_mask(limit):
+    return (lax.broadcasted_iota(jnp.int32, (TOKENS, 1), 0) < limit).astype(jnp.float32)
+
+
+def columns_moved(values, col_off):
+    if col_off == 0:
+        return values
+    col = lax.broadcasted_iota(jnp.int32, (TOKENS, 1), 0) % FRAME
+    keep = col > 0 if col_off < 0 else col < FRAME - 1
+    return jnp.where(keep, pltpu.roll(values, (-col_off) % TOKENS, 0), 0.0)
+
+
+def two_sides(side, mine, other):
+    first = jnp.where(side == 0, mine, other)
+    second = jnp.where(side == 0, other, mine)
+    return jnp.concatenate([first, second], axis=1)
+
+
+def fill_moved(moved, values):
+    width = moved.shape[2]
+    empty = jnp.zeros((FRAME, width), moved.dtype)
+    for slab in range(3):
+        moved[slab, 0:FRAME, :] = empty
+        moved[slab, FRAME : FRAME + TOKENS, :] = columns_moved(values, slab - 1).astype(moved.dtype)
+        moved[slab, FRAME + TOKENS : PADDED, :] = empty
+
+
+def tap_of(step, turned):
+    row_off, col_off = (step // 3 - 1, step % 3 - 1)
+    return (
+        jnp.where(turned == 1, col_off, row_off),
+        jnp.where(turned == 1, row_off, col_off),
+    )
+
+
+def rows_from(row_off):
+    return pl.ds(pl.multiple_of(FRAME * (1 + row_off), FRAME), TOKENS)
+
+
+def group_same():
+    left = lax.broadcasted_iota(jnp.int32, (HALF, HALF), 0) // (C // GROUPS)
+    right = lax.broadcasted_iota(jnp.int32, (HALF, HALF), 1) // (C // GROUPS)
+    return (left == right).astype(jnp.float32)
+
+
+def spread_in(sums, same):
+    wide = jnp.broadcast_to(sums, (8, HALF))
+    return jnp.dot(
+        wide, same, precision=lax.Precision.HIGHEST, preferred_element_type=jnp.float32
+    )[0:1]
+
+
+def norm_in(value, mask, limit, gain, bias):
+    same = group_same()
+    share = 1.0 / (limit.astype(jnp.float32) * (C // GROUPS))
+    mean_val = spread_in(jnp.sum(value * mask, axis=0, keepdims=True), same) * share
+    centered = value - mean_val
+    var_val = spread_in(jnp.sum(centered * centered * mask, axis=0, keepdims=True), same) * share
+    inv_std = lax.rsqrt(var_val + eps_group)
+    normed = centered * inv_std
+    return (normed * gain + bias, normed, inv_std)
+
+
+def silu_in(values):
+    return values / (1.0 + jnp.exp(-values))
+
+
+def finish_forward(total, limit, base, rows, act, act_out, normed_out, inv_out, value_out):
+    mask = token_mask(limit)
+    value = mask * (total + rows[0:1])
+    if base is not None:
+        value = value + base
+    norm, normed, inv_std = norm_in(value, mask, limit, rows[1:2], rows[2:3])
+    result = mask * silu_in(norm) if act else norm
+    low_result = result.astype(jnp.bfloat16)
+    act_out[...] = low_result
+    normed_out[...] = normed
+    inv_out[0:1] = inv_std
+    inv_out[1:2] = column_squares(low_result)
+    if value_out is not None:
+        value_out[...] = value
+
+
+def forward_outs(with_value):
+    shapes = [
+        jax.ShapeDtypeStruct((TOKENS, HALF), jnp.bfloat16),
+        jax.ShapeDtypeStruct((TOKENS, HALF), jnp.float32),
+        jax.ShapeDtypeStruct((8, HALF), jnp.float32),
+    ]
+    if with_value:
+        shapes.append(jax.ShapeDtypeStruct((TOKENS, HALF), jnp.float32))
+    return shapes
+
+
+def first_forward(info, inputs, weight, rows):
+    def body(info_ref, input_ref, weight_ref, rows_ref, *outs):
+        total = dot(input_ref[...], weight_ref[...])
+        finish_forward(total, info_ref[2], None, rows_ref[...], True, *outs)
+
+    outs = forward_outs(True)
+    return pl.pallas_call(
+        body,
+        grid_spec=pltpu.PrefetchScalarGridSpec(
+            num_scalar_prefetch=1,
+            grid=(1,),
+            in_specs=[whole(inputs.shape), whole(weight.shape), whole(rows.shape)],
+            out_specs=[whole(one.shape) for one in outs],
+        ),
+        out_shape=outs,
+        compiler_params=params(),
+        cost_estimate=cost(2 * TOKENS * 27 * HALF, 3 * TOKENS * HALF * 4),
+    )(info, inputs, weight, rows)
+
+
+def conv_forward(info, mine, other, table, at, base, rows, act):
+    with_base = base is not None
+
+    def body(info_ref, mine_ref, other_ref, weight_ref, rows_ref, *rest):
+        base_ref = rest[0] if with_base else None
+        outs, (moved, total) = (rest[int(with_base) : -2], rest[-2:])
+        step = pl.program_id(0)
+
+        @pl.when(step == 0)
+        def _():
+            both = two_sides(info_ref[0], mine_ref[...], other_ref[...])
+            fill_moved(moved, both.astype(jnp.float32))
+            total[...] = jnp.zeros_like(total)
+
+        row_off, col_off = tap_of(step, info_ref[1])
+        total[...] += dot(moved[col_off + 1, rows_from(row_off), :], weight_ref[...])
+
+        @pl.when(step == 8)
+        def _():
+            value_out = outs[3] if with_base else None
+            held = base_ref[...] if with_base else None
+            finish_forward(
+                total[...], info_ref[2], held, rows_ref[...], act, *outs[:3], value_out
+            )
+
+    outs = forward_outs(with_base)
+    extra = [base] if with_base else []
+    return pl.pallas_call(
+        body,
+        grid_spec=pltpu.PrefetchScalarGridSpec(
+            num_scalar_prefetch=1,
+            grid=(9,),
+            in_specs=[
+                whole(mine.shape),
+                whole(other.shape),
+                pl.BlockSpec(
+                    (pl.Element(C), pl.Element(HALF)),
+                    lambda i, info_ref: (
+                        pl.multiple_of(at + C * i, 8),
+                        pl.multiple_of(HALF * info_ref[0], HALF),
+                    ),
+                ),
+                whole(rows.shape),
+            ]
+            + [whole(one.shape) for one in extra],
+            out_specs=[whole(one.shape) for one in outs],
+            scratch_shapes=[
+                pltpu.VMEM((3, PADDED, C), jnp.bfloat16),
+                pltpu.VMEM((TOKENS, HALF), jnp.float32),
+            ],
+        ),
+        out_shape=outs,
+        compiler_params=params(),
+        cost_estimate=cost(18 * TOKENS * C * HALF, 9 * C * HALF * 2 + 6 * TOKENS * HALF * 4),
+    )(info, mine, other, table, rows, *extra)
+
+
+def conv_backward(info, grad_mine, grad_other, act_mine, act_other, table, store, at, saved, rows, base):
+    with_base = base is not None
+    old, old_specs, out_spec, out_shape = store_specs(store, at, C)
+
+    def body(info_ref, *refs):
+        refs = refs[len(old) :]
+        gm_ref, go_ref, am_ref, ao_ref, weight_ref, normed_ref, inv_ref, rows_ref = refs[:8]
+        base_ref = refs[8] if with_base else None
+        refs = refs[8 + int(with_base) :]
+        out_ref, low_out, sums_out = refs[:3]
+        moved, turned_act, shifted, total = refs[-4:]
+        step = pl.program_id(0)
+
+        @pl.when(step == 0)
+        def _():
+            both = two_sides(info_ref[0], gm_ref[...], go_ref[...])
+            fill_moved(moved, both.astype(jnp.float32))
+            act = two_sides(info_ref[0], am_ref[...], ao_ref[...]).astype(jnp.float32)
+            for slab in range(3):
+                turned_act[slab] = columns_moved(act, slab - 1).T.astype(jnp.bfloat16)
+            empty = jnp.zeros((FRAME, HALF), jnp.bfloat16)
+            shifted[0:FRAME, :] = empty
+            shifted[FRAME : FRAME + TOKENS, :] = gm_ref[...]
+            shifted[FRAME + TOKENS : PADDED, :] = empty
+            total[...] = jnp.zeros_like(total)
+
+        row_off, col_off = tap_of(step, info_ref[1])
+        out_ref[...] = dot(turned_act[col_off + 1], shifted[rows_from(-row_off), :])
+        total[...] += dot_t(moved[1 - col_off, rows_from(-row_off), :], weight_ref[...])
+
+        @pl.when(step == 8)
+        def _():
+            mask = token_mask(info_ref[2])
+            gain, normed, inv_std = (rows_ref[0:1], normed_ref[...], inv_ref[0:1])
+            norm = normed * gain + rows_ref[1:2]
+            logistic = 1.0 / (1.0 + jnp.exp(-norm))
+            gradient = mask * total[...] * (logistic * (1.0 + norm * (1.0 - logistic)))
+            result, gain_grad, bias_grad = norm_back(
+                gradient, normed, inv_std, mask, info_ref[2], gain
+            )
+            if with_base:
+                result = mask * (result + base_ref[...])
+            low_result = result.astype(jnp.bfloat16)
+            low_out[...] = low_result
+            sums_out[3:4] = column_squares(low_result)
+            sums_out[0:1] = jnp.sum(result, axis=0, keepdims=True)
+            sums_out[1:2] = gain_grad
+            sums_out[2:3] = bias_grad
+
+    extra = [base] if with_base else []
+    operands = [grad_mine, grad_other, act_mine, act_other]
+    result = pl.pallas_call(
+        body,
+        grid_spec=pltpu.PrefetchScalarGridSpec(
+            num_scalar_prefetch=1,
+            grid=(9,),
+            in_specs=old_specs
+            + [whole(one.shape) for one in operands]
+            + [
+                pl.BlockSpec(
+                    (pl.Element(HALF), pl.Element(C)),
+                    lambda i, info_ref: (
+                        pl.multiple_of(at + C * i + HALF * info_ref[0], 8),
+                        0,
+                    ),
+                ),
+                whole((TOKENS, HALF)),
+                whole((8, HALF)),
+                whole(rows.shape),
+            ]
+            + [whole(one.shape) for one in extra],
+            out_specs=[
+                out_spec,
+                whole((TOKENS, HALF)),
+                whole((8, HALF)),
+            ],
+            scratch_shapes=[
+                pltpu.VMEM((3, PADDED, C), jnp.bfloat16),
+                pltpu.VMEM((3, C, TOKENS), jnp.bfloat16),
+                pltpu.VMEM((PADDED, HALF), jnp.bfloat16),
+                pltpu.VMEM((TOKENS, HALF), jnp.float32),
+            ],
+        ),
+        out_shape=[
+            out_shape,
+            jax.ShapeDtypeStruct((TOKENS, HALF), jnp.bfloat16),
+            jax.ShapeDtypeStruct((8, HALF), jnp.float32),
+        ],
+        input_output_aliases={1 + k: k for k in range(len(old))},
+        compiler_params=params(),
+        cost_estimate=cost(36 * TOKENS * C * HALF, 9 * C * HALF * 6 + 6 * TOKENS * HALF * 4),
+    )(info, *old, *operands, table, *saved, rows, *extra)
+    store.write(result[0], None)
+    return (result[1], result[2])
+
+
+def column_squares(values):
+    wide = values.astype(jnp.float32)
+    return jnp.sum(wide * wide, axis=0, keepdims=True)
+
+
+def norm_back(gradient, normed, inv_std, mask, limit, gain):
+    same = group_same()
+    share = 1.0 / (limit.astype(jnp.float32) * (C // GROUPS))
+    scaled = gradient * gain
+    first = spread_in(jnp.sum(scaled * mask, axis=0, keepdims=True), same) * share
+    second = spread_in(jnp.sum(scaled * normed * mask, axis=0, keepdims=True), same) * share
+    result = mask * inv_std * (scaled - first - normed * second)
+    return (
+        result,
+        jnp.sum(gradient * normed, axis=0, keepdims=True),
+        jnp.sum(gradient, axis=0, keepdims=True),
+    )
 
 
 def gather_small(place, value):
@@ -359,15 +766,6 @@
     return jnp.dot(channel_sums, same, precision=lax.Precision.HIGHEST)
 
 
-def group_forward(values, mask, denominator, gain_vec, bias_vec):
-    mean_val = group_spread(jnp.sum(values * mask, axis=0)[None]) / denominator
-    centered = values - mean_val
-    var_val = group_spread(jnp.sum(centered * centered * mask, axis=0)[None]) / denominator
-    inv_std = lax.rsqrt(var_val + eps_group)
-    normed = centered * inv_std
-    return (normed * gain_vec + bias_vec, normed, inv_std)
-
-
 def group_backward(gradient, normed, inv_std, mask, denominator, gain_vec):
     scaled = gradient * gain_vec
     sums = group_spread(
@@ -484,8 +882,8 @@
     return jnp.where(turned, landscape, portrait).reshape(TOKENS, 2 * LC)
 
 
-def train_step(place, mats, vecs, latents, target_noise, label, step_value, orient, extent):
-    grads, bias_grads = ({}, {})
+def train_step(place, store, table, mats, vecs, latents, target_noise, label, step_value, orient, extent):
+    bias_grads = {}
     half, full = (place.half, place.full)
     turned = orient != 1
     seen = lax.iota(jnp.int32, TOKENS) < extent * FRAME
@@ -504,24 +902,40 @@
     time_vec = dot(hidden_two, mats["w_tp"]) + vecs["b_tp"]
     class_vec = lax.dynamic_slice(mats["table"], (label, 0), (1, C)).astype(jnp.float32)
 
+    info = jnp.stack([place.side, turned.astype(jnp.int32), extent * FRAME]).astype(jnp.int32)
+    side_row = lambda name: half(vecs[name])[None]
+    stack = lambda *rows: jnp.concatenate(rows, axis=0)
+    at = store.places
     pad_in = windows(low(noisy), turned, 1)
-    state_zero = mask * (dot(pad_in, half(mats["w_in"])) + half(vecs["b_in"]))
-    norm_one, normed_one, inv_one = group_forward(
-        state_zero, mask, denominator, half(vecs["g1"]), half(vecs["bb1"])
-    )
-    pad_one = windows(full(low(mask * jax.nn.silu(norm_one))), turned, 1)
-    conv_one = mask * (
-        dot(pad_one, half(mats["w_c1"])) + half(vecs["b_c1"]) + half(time_vec)
-    )
-    norm_two, normed_two, inv_two = group_forward(
-        conv_one, mask, denominator, half(vecs["g2"]), half(vecs["bb2"])
-    )
-    pad_two = windows(full(low(mask * jax.nn.silu(norm_two))), turned, 1)
-    state_one = state_zero + mask * (dot(pad_two, half(mats["w_c2"])) + half(vecs["b_c2"]))
-    norm_three, normed_three, inv_three = group_forward(
-        state_one, mask, denominator, half(vecs["g3"]), half(vecs["bb3"])
-    )
-    token_in = full(low(norm_three))
+    act_one, normed_one, inv_one, state_zero = first_forward(
+        info,
+        pad_in,
+        half(mats["w_in"]),
+        stack(side_row("b_in"), side_row("g1"), side_row("bb1")),
+    )
+    act_one_peer = place.swap(act_one)
+    act_two, normed_two, inv_two = conv_forward(
+        info,
+        act_one,
+        act_one_peer,
+        table,
+        at["w_c1"],
+        None,
+        stack(side_row("b_c1") + half(time_vec), side_row("g2"), side_row("bb2")),
+        True,
+    )
+    act_two_peer = place.swap(act_two)
+    token_own, normed_three, inv_three, state_one = conv_forward(
+        info,
+        act_two,
+        act_two_peer,
+        table,
+        at["w_c2"],
+        state_zero,
+        stack(side_row("b_c2"), side_row("g3"), side_row("bb3")),
+        False,
+    )
+    token_in = full(token_own)
     resid_zero = dot(token_in, mats["w_pin"]) + vecs["b_pin"]
     ln_one, normed_ln1, inv_ln1 = layer_forward(resid_zero, vecs["n1g"], vecs["n1b"])
     qkv_own = own_columns(place, mats["w_qkv"])
@@ -566,18 +980,20 @@
     out_grad = 2.0 * mask * residual_err
     bias_grads["b_out"] = jnp.sum(out_grad, axis=0)
     out_low = low(out_grad)
-    grads["w_out"] = half(t_dot(pad_out, out_low).reshape(9 * LC, C))
     w_out_back = jnp.transpose(mats["w_out"].reshape(9, C, LC), (0, 2, 1)).reshape(9 * LC, C)
     state_grad = dot(windows(out_low, turned, -1), w_out_back)
     branch_grad = mask * state_grad
     state_grad = half(state_grad)
     bias_grads["b_pout"] = half(jnp.sum(branch_grad, axis=0))
     grad_low = low(branch_grad)
-    grads["w_pout"] = t_dot(out_in, half(grad_low))
+    store.add("w_pout", out_in, half(grad_low))
+    w_out_grad = half(t_dot(pad_out, out_low).reshape(9 * LC, C))
+    last = store.total - store.places["w_out"] - 9 * LC
+    store.put(store.places["w_out"], jnp.pad(w_out_grad, ((0, last), (0, 0))))
     resid_grad = dot_t(grad_low, mats["w_pout"])
     bias_grads["b_ff2"] = half(jnp.sum(resid_grad, axis=0))
     grad_low = low(resid_grad)
-    grads["w_ff2"] = t_dot(gated, half(grad_low))
+    store.add("w_ff2", gated, half(grad_low))
     ff2_own = pick(mats["w_ff2"].reshape(-1, 2, HALF, C), place.side, 1).reshape(wide, C)
     gated_grad = dot_t(grad_low, ff2_own)
     density = jnp.exp(-0.5 * gate * gate) * (1.0 / math.sqrt(2.0 * math.pi))
@@ -586,7 +1002,7 @@
     )
     bias_grads["b_ff1"] = jnp.sum(proj_grad, axis=0)
     grad_low = low(proj_grad)
-    grads["w_ff1"] = t_dot(ln_three, grad_low)
+    store.add("w_ff1", ln_three, grad_low)
     ln_grad = dot_t(grad_low, ff1_own)
     ln_grad = ln_grad + place.swap(ln_grad)
     ln_grad, gain, bias = layer_backward(ln_grad, normed_ln3, inv_ln3, vecs["n3g"])
@@ -594,12 +1010,12 @@
     resid_grad = resid_grad + ln_grad
     bias_grads["b_co"] = half(jnp.sum(resid_grad, axis=0))
     grad_low = low(resid_grad)
-    grads["w_co"] = t_dot(cross_out, half(grad_low))
+    store.add("w_co", cross_out, half(grad_low))
     cross_grad = heads_of(low(dot_t(grad_low, half(mats["w_co"], 0))))
     query_grad, kv_grad = cross_back(cross_query, context_kv, cross_prob, cross_grad)
     query_low, kv_low = (low(query_grad), low(kv_grad))
-    grads["w_cq"] = t_dot(ln_two, query_low)
-    grads["w_ckv"] = t_dot(context, kv_low)
+    store.add("w_cq", ln_two, query_low)
+    store.add("w_ckv", context, kv_low)
     context_grad = dot_t(kv_low, ckv_own)
     context_grad = context_grad + place.swap(context_grad)
     ln_grad = dot_t(full(query_low), mats["w_cq"])
@@ -608,10 +1024,10 @@
     resid_grad = resid_grad + ln_grad
     bias_grads["b_o"] = half(jnp.sum(resid_grad, axis=0))
     grad_low = low(resid_grad)
-    grads["w_o"] = t_dot(attended, half(grad_low))
+    store.add("w_o", attended, half(grad_low))
     attended_grad = heads_of(low(dot_t(grad_low, half(mats["w_o"], 0))))
     packed_grad = attend_back(query, key, value, seen, log_total, attended_grad)
-    grads["w_qkv"] = t_dot(ln_one, packed_grad)
+    store.add("w_qkv", ln_one, packed_grad)
     ln_grad = dot_t(packed_grad, qkv_own)
     ln_grad = ln_grad + place.swap(ln_grad)
     ln_grad, gain, bias = layer_backward(ln_grad, normed_ln1, inv_ln1, vecs["n1g"])
@@ -619,69 +1035,68 @@
     resid_grad = resid_grad + ln_grad
     bias_grads["b_pin"] = half(jnp.sum(resid_grad, axis=0))
     grad_low = low(resid_grad)
-    grads["w_pin"] = t_dot(token_in, half(grad_low))
+    store.add("w_pin", token_in, half(grad_low))
     token_grad = dot_t(grad_low, half(mats["w_pin"], 0))
     norm_grad, bias_grads["g3"], bias_grads["bb3"] = group_backward(
-        token_grad, normed_three, inv_three, mask, denominator, half(vecs["g3"])
+        token_grad, normed_three, inv_three[0:1], mask, denominator, half(vecs["g3"])
     )
     state_grad = state_grad + norm_grad
 
     conv_grad = mask * state_grad
     bias_grads["b_c2"] = jnp.sum(conv_grad, axis=0)
     conv_low = low(conv_grad)
-    grads["w_c2"] = t_dot(pad_two, conv_low)
-    act_grad = conv_input_grad(place, full(conv_low), mats["w_c2"], turned)
-    conv_grad, bias_grads["g2"], bias_grads["bb2"] = group_backward(
-        mask * act_grad * silu_slope(norm_two),
-        normed_two,
-        inv_two,
-        mask,
-        denominator,
-        half(vecs["g2"]),
-    )
-    conv_sum = jnp.sum(conv_grad, axis=0)
+    c2_squares = column_squares(conv_low)
+    conv_low, sums = conv_backward(
+        info,
+        conv_low,
+        place.swap(conv_low),
+        act_two,
+        act_two_peer,
+        table,
+        store,
+        at["w_c2"],
+        (normed_two, inv_two),
+        stack(side_row("g2"), side_row("bb2")),
+        None,
+    )
+    conv_sum, bias_grads["g2"], bias_grads["bb2"] = (sums[0], sums[1], sums[2])
     bias_grads["b_c1"] = conv_sum
-    conv_low = low(conv_grad)
-    grads["w_c1"] = t_dot(pad_one, conv_low)
-    act_grad = conv_input_grad(place, full(conv_low), mats["w_c1"], turned)
-    norm_grad, bias_grads["g1"], bias_grads["bb1"] = group_backward(
-        mask * act_grad * silu_slope(norm_one),
-        normed_one,
-        inv_one,
-        mask,
-        denominator,
-        half(vecs["g1"]),
-    )
-    in_grad = mask * (state_grad + norm_grad)
-    bias_grads["b_in"] = jnp.sum(in_grad, axis=0)
-    grads["w_in"] = t_dot(pad_in, low(in_grad))
-
     time_grad = full(conv_sum[None]) + context_grad[1:2]
     bias_grads["b_tp"] = half(time_grad[0])
     time_low = low(time_grad)
-    grads["w_tp"] = outer(hidden_two, half(time_low))
+    store.add("w_tp", hidden_two, half(time_low))
     pre_grad = dot_t(time_low, mats["w_tp"]) * silu_slope(pre_two)
     bias_grads["b_t2"] = own_columns(place, pre_grad)[0]
     pre_low = low(pre_grad)
-    grads["w_t2"] = outer(hidden_one, own_columns(place, pre_low))
+    store.add("w_t2", hidden_one, own_columns(place, pre_low))
     pre_grad = dot_t(pre_low, mats["w_t2"]) * silu_slope(pre_one)
     bias_grads["b_t1"] = own_columns(place, pre_grad)[0]
-    grads["w_t1"] = outer(embed_in, own_columns(place, low(pre_grad)))
+    store.add("w_t1", embed_in, own_columns(place, low(pre_grad)))
     rows = lax.iota(jnp.int32, NCLS)[:, None] == label
-    grads["table"] = jnp.where(rows, half(context_grad[0:1]), 0.0)
-    return (grads, bias_grads, loss)
-
-
-def outer(inputs, gradient):
-    return inputs.astype(jnp.float32).reshape(-1, 1) * gradient.astype(jnp.float32)
-
-
-def conv_input_grad(place, gradient, weight, turned):
-    moved = windows(gradient, turned, -1).reshape(TOKENS, 9, C)
-    own = place.half(weight.reshape(9, C, C), 1)
-    return lax.dot_general(
-        moved, own, (((1, 2), (0, 2)), ((), ())), preferred_element_type=jnp.float32
-    )
+    store.put(store.places["table"], jnp.where(rows, half(context_grad[0:1]), 0.0))
+    store.put(0, jnp.zeros((store.places["w_t1"], HALF), jnp.float32))
+
+    squares = [jnp.max(rows_of).reshape(1, 1) for rows_of in (inv_one[1], inv_two[1], c2_squares, sums[3])]
+    tops = largest_of_all(place, jnp.concatenate([store.top] + squares, axis=1))[0]
+    bound = jnp.maximum(tops[0], 1.01 * jnp.sqrt(tops[1] * tops[4]))
+    bound = jnp.maximum(bound, 1.01 * jnp.sqrt(tops[2] * tops[3]))
+    scale = (WIRE_TOP / (place.count // 2)) / jnp.maximum(bound, 1e-30)
+    in_low, sums = conv_backward(
+        info,
+        conv_low,
+        place.swap(conv_low),
+        act_one,
+        act_one_peer,
+        table,
+        store,
+        at["w_c1"],
+        (normed_one, inv_one),
+        stack(side_row("g1"), side_row("bb1")),
+        state_grad,
+    )
+    bias_grads["b_in"], bias_grads["g1"], bias_grads["bb1"] = (sums[0], sums[1], sums[2])
+    w_in_grad = t_dot(pad_in, in_low)
+    return (bias_grads, w_in_grad, scale, loss)
 
 
 def adam_update(params, first_mom, second, gradient, decay_rate):
@@ -730,8 +1145,11 @@
     vec_all = vec_all.reshape(-1).astype(jnp.bfloat16).astype(jnp.float32)
     vecs = unpack(vec_all, vec_layout())
     own = lambda values: pick(values, place.slot, 0)
-    grads, bias_grads, loss = train_step(
+    store = Store(place, rows)
+    bias_grads, w_in_grad, scale, loss = train_step(
         place,
+        store,
+        table,
         mats,
         vecs,
         latents,
@@ -741,26 +1159,23 @@
         own(orient),
         own(extent),
     )
-    pieces = [jnp.zeros((LEAD, HALF), jnp.float32)]
-    pieces += [grads[record[0]].reshape(-1, HALF) for record in mat_layout()]
-    used = sum(piece.shape[0] for piece in pieces)
-    pieces.append(jnp.zeros((place.count * rows - used, HALF), jnp.float32))
-    grad_rows = jnp.concatenate(pieces, axis=0)
-
     small = [bias_grads[record[0]].reshape(-1, HALF) for record in vec_layout()[:-1]]
     count_local = (own(extent) * FRAME).astype(jnp.float32)
     extra = jnp.concatenate([bias_grads["b_out"], jnp.stack([loss, count_local])])
     extra = jnp.pad(extra, (0, HALF - LC - 2))[None]
-    small = jnp.concatenate(small + [extra], axis=0)
+    small = jnp.concatenate(small + [extra, w_in_grad], axis=0)
     small = jnp.pad(small, ((0, -small.shape[0] % 8), (0, 0)))
     small = place.full(place.chip_sum(small))
     body = sum(record[1] for record in vec_layout()[:-1]) // WIDE
     loss_sum, pixel_count = (small[body, LC], small[body, LC + 1])
+    w_in_sum = small[body + 1 : body + 1 + 9 * LC]
     vec_flat = jnp.concatenate([small[:body].reshape(-1), small[body, :LC]])
     vec_flat = jnp.pad(vec_flat, (0, vec_len * place.count - vec_flat.shape[0]))
     shard_vec = lax.dynamic_slice(vec_flat, (vec_len * place.index,), (vec_len,))
 
-    block_grad = scatter_sum(place, grad_rows, rows)
+    block_grad = scatter_sum(place, store.buffer, scale, rows)
+    held = jnp.where(place.index == 0, w_in_sum, block_grad[LEAD : LEAD + 9 * LC])
+    block_grad = lax.dynamic_update_slice(block_grad, held, (LEAD, 0))
     shard_mat = from_blocks(place, block_grad, length)
     square = jnp.sum(block_grad * block_grad).reshape(1, 1)
     square = place.chip_sum(square + place.swap(square))[0, 0]

time: 955 us -> 697 us (0.73)
  starting transfers between devices: 245 us -> 87.2 us
  local copies, waits for them, and re-layouts: 222 us -> 103 us
  Pallas kernels: 0 us -> 63.5 us
  matrix products: 112 us -> 65.9 us
  waiting for transfers between devices: 187 us -> 232 us
  other arithmetic: 117 us -> 89.7 us
  between operations: 58.9 us -> 42.1 us
    ppermute x82 -> x60, starting transfers between devices: 245 us -> 87.2 us  [move(): return lax.ppermute(value, ('dp', 'rows'), pairs)]
    concatenate x2, local copies, waits for them, and re-layouts: 69.8 us -> 3.12 us  [the longest x1 2.77 us: train_step(): jnp.concatenate([store.top] + squares, axis=1)]
    pallas_call x0 -> x17, Pallas kernels: none -> 63.5 us  [the longest x2 22.9 us: conv_backward(): pl.pallas_call(body, grid_spec=pltpu.PrefetchScalarGridSpec(num_scalar_pr...]
    ppermute x82 -> x60, waiting for transfers between devices: 52.5 us -> 101 us  [move(): return lax.ppermute(value, ('dp', 'rows'), pairs)]
    dot_general x13 -> x2, matrix products: 32.3 us -> 3.03 us  [t_dot(): lax.dot_general(left, right, (((0,), (0,)), ((), ())), preferred_element_...]
    slice x2 -> x5, local copies, waits for them, and re-layouts: 19.9 us -> 1.14 us  [the longest x1 0.6 us: train_step(): bound = jnp.maximum(bound, 1.01 * jnp.sqrt(tops[2] * tops[3]))]
    unnamed x42 -> x15, other arithmetic: 25.3 us -> 8.63 us
    concatenate x9 -> x4, local copies, waits for them, and re-layouts: 15.8 us -> 0.73 us  [windows(): return jnp.concatenate(out, axis=1)]
  transfers between devices with their start and end apart: 83 -> 61, of which waited for: 26 -> 29; matrix products, arithmetic and copies ran while one was open for 20% -> 20% of each run, Pallas kernels for 0% -> 5%
where the time goes in v1:
time: 697 us; the launch traced here: 683 us
  waiting for transfers between devices  232 us (33%)
  local copies, waits for them, and re-layouts  103 us (15%)
  other arithmetic  89.7 us (13%)
  starting transfers between devices  87.2 us (13%)
  matrix products  65.9 us (9%)
  Pallas kernels  63.5 us (9%)
  between operations  42.1 us (6%)
    all_gather x1, waiting for transfers between devices, local(): table = lax.all_gather(block, ('dp', 'rows'), axis=0, tiled=True)  131 us
    ppermute x60, waiting for transfers between devices, move(): return lax.ppermute(value, ('dp', 'rows'), pairs)  101 us
    ppermute x60, starting transfers between devices, move(): return lax.ppermute(value, ('dp', 'rows'), pairs)  87.2 us
    unnamed x381, local copies, waits for them, and re-layouts  27.5 us
    convert_element_type x15, other arithmetic, wire(): return values.astype(jnp.float16)  24.2 us
    pallas_call x2, Pallas kernels, conv_backward(): pl.pallas_call(body, grid_spec=pltpu.PrefetchScalarGridSpec(num_scalar_pr...  22.9 us
    pallas_call x12, Pallas kernels, grad_into(): pl.pallas_call(body, grid=(tiles,), in_specs=old_specs + [pl.BlockSpec((t...  21.9 us
    dot_general x11, matrix products, dot_t(): lax.dot_general(left, right, (((1,), (1,)), ((), ())), preferred_element_...  19.3 us
  transfers between devices with their start and end apart: 61, of which 29 were waited for; matrix products, arithmetic and copies ran while one was open for 20% of the time, Pallas kernels for 5%

profile of v1, /device:TPU:4, one launch (start us, length us, event | category | flops | bytes accessed | tf_op | source)
XLA Modules:
  0.0 683.4 jit_solution(8388260391325695167)
XLA Ops:
  11.5 3.5 collective-permute-done.2
  15.0 5.3 concatenate.269
  32.9 3.3 collective-permute-start.4
  37.9 3.6 collective-permute-done.5
  49.6 2.8 collective-permute-done.7
  53.4 130.8 %all-gather.2.cloned.1.call-done.weight_ref.refs_5_ = bf16[25344,512]{1,0:T(8,128)(2,1)} async-done(((bf16[792,512]{1,0:T(8,128)(2,1)}), bf16[25344,512]{1,0:T(8,128)(2,1)}) %all-gather.2.cloned.1.call-update) | async-done | bytes 25952272 | tf_op jit(solution)/shard_map/all_gather | solution.py:1133
  187.2 3.4 fusion.176
  191.0 4.5 fusion.177
  207.4 8.4 %shard_map.222 = (bf16[512,256]{1,0:T(8,128)(2,1)S(1)}, f32[512,256]{1,0:T(8,128)S(1)}, f32[8,256]{1,0:T(8,128)S(1)}) custom-call(s32[3]{0:T(128)S(1)} %pad_add_fusion.info_ref, bf16[512,256]{1,0:T(8,128)(2,1)S(1)} %get-tuple-element.52.mine_ref.refs_3_, bf16[512,256]{1,0:T(8,128)(2,1)S(1)} %collective-permute-done.8.other_ref.refs_4_, ...), custom_call_target="tpu_custom_call" | custom-call | flops 1207959552 | bytes 5505024 | tf_op jit(solution)/shard_map/pallas_call | solution.py:580
  218.9 8.5 %shard_map.223 = (bf16[512,256]{1,0:T(8,128)(2,1)S(1)}, f32[512,256]{1,0:T(8,128)S(1)}, f32[8,256]{1,0:T(8,128)S(1)}, f32[512,256]{1,0:T(8,128)S(1)}) custom-call(s32[3]{0:T(128)S(1)} %pad_add_fusion.info_ref, bf16[512,256]{1,0:T(8,128)(2,1)S(1)} %get-tuple-element.53.mine_ref.refs_3_, bf16[512,256]{1,0:T(8,128)(2,1)S(1)} %collective-permute-done.9.other_ref.refs_4_, ...), custom_call_target="tpu_custom_call" | custom-call | flops 1207959552 | bytes 5505024 | tf_op jit(solution)/shard_map/pallas_call | solution.py:580
  233.0 4.9 copy.203
  266.8 3.4 reshape_reshape.15
  270.2 3.2 reshape.600
  286.8 3.6 fusion.48.refs_0_
  304.1 3.8 multiply_multiply_fusion.2
  316.2 2.9 fusion.207
  319.0 4.0 reshape.602
  329.7 3.1 multiply_reduce_fusion.2
  339.8 3.0 shard_map.225
  343.5 4.3 shard_map.226
  352.4 2.9 fusion.209
  356.7 8.0 %fusion.56 = bf16[4,64,512]{2,1,0:T(8,128)(2,1)S(1)} fusion(bf16[512,4,64]{0,2,1:T(8,128)(2,1)S(1)} %bitcast.321, f32[4,512,512]{1,2,0:T(8,128)} %fusion.209, f32[4,512,512]{1,2,0:T(8,128)} %copy-done.24, f32[4,512]{1,0:T(4,128)S(1)} %copy-done.115), kind=kOutput, calls=%fused_computation.98 | convolution fusion | flops 141691392 | bytes 8921088 | tf_op jit(solution)/shard_map/hqk,khd->qhd/dot_general | solution.py:822
  364.7 8.0 %fusion.59 = bf16[4,64,512]{2,1,0:T(8,128)(2,1)S(1)} fusion(bf16[512,4,64]{0,2,1:T(8,128)(2,1)S(1)} %bitcast.323, f32[4,512,512]{1,2,0:T(8,128)} %fusion.209, f32[4,512,512]{1,2,0:T(8,128)} %copy-done.24, f32[4,512]{1,0:T(4,128)S(1)} %copy-done.115), kind=kOutput, calls=%fused_computation.99 | convolution fusion | flops 141691392 | bytes 8921088 | tf_op jit(solution)/shard_map/hqk,qhd->khd/dot_general | solution.py:823
  375.3 3.0 fusion.166
  397.6 11.5 %shard_map.233 = (f32[25344,256]{1,0:T(8,128)}, bf16[512,256]{1,0:T(8,128)(2,1)S(1)}, f32[8,256]{1,0:T(8,128)S(1)}) custom-call(s32[3]{0:T(128)S(1)} %pad_add_fusion.info_ref, f32[25344,256]{1,0:T(8,128)} %get-tuple-element.65.refs_0_, bf16[512,256]{1,0:T(8,128)(2,1)S(1)} %get-tuple-element.130.refs_1_, ...), custom_call_target="tpu_custom_call", output_to_operand_aliasing={{0}: (1, {})} | custom-call | flops 2415919104 | bytes 10223616 | tf_op jit(solution)/shard_map/pallas_call | solution.py:661
  434.8 3.0 collective-permute-done.23
  438.4 3.0 collective-permute-done.24
  441.4 3.5 collective-permute-done.25
  446.4 2.9 collective-permute-done.26
  453.4 11.4 %shard_map.237 = (f32[25344,256]{1,0:T(8,128)}, bf16[512,256]{1,0:T(8,128)(2,1)S(1)}, f32[8,256]{1,0:T(8,128)S(1)}) custom-call(s32[3]{0:T(128)S(1)} %pad_add_fusion.info_ref, f32[25344,256]{1,0:T(8,128)} %constant_dynamic-update-slice_fusion.4.refs_0_, bf16[512,256]{1,0:T(8,128)(2,1)S(1)} %get-tuple-element.75.refs_1_, ...), custom_call_target="tpu_custom_call", output_to_operand_aliasing={{0}: (1, {})} | custom-call | flops 2415919104 | bytes 10223616 | tf_op jit(solution)/shard_map/pallas_call | solution.py:661
  464.8 4.5 fusion.20
  475.5 6.9 %constant_dynamic-slice_fusion.3 = (f32[4,2,1,616,256]{4,3,2,1,0:T(8,128)S(1)}, f32[4,2,1,616,256]{4,3,2,1,0:T(8,128)}) fusion(f32[4,2,2,1584,256]{4,3,2,1,0:T(8,128)} %bitcast.295, s32[]{:T(128)S(6)} %select_n.677, s32[]{:T(128)S(6)} %select_n.590), kind=kLoop, calls=%fused_computation.279 | loop fusion | bytes 20185096 | tf_op jit(solution)/shard_map/dynamic_slice | solution.py:290
  487.6 5.2 collective-permute-start.41
  506.0 15.9 %collective-permute-done.32 = f16[4,2,616,256]{3,2,1,0:T(8,128)(2,1)} collective-permute-done((f16[4,2,616,256]{3,2,1,0:T(8,128)(2,1)}, f16[4,2,616,256]{3,2,1,0:T(8,128)(2,1)}, u32[]{:S(2)}, u32[]{:S(2)}) %collective-permute-start.32) | collective-permute-done | bytes 2523168 | tf_op jit(solution)/shard_map/ppermute | solution.py:171
  521.9 3.7 fusion.2
  526.9 3.3 collective-permute-start.33
  535.7 8.6 %collective-permute-done.33 = f16[2,616,256]{2,1,0:T(8,128)(2,1)} collective-permute-done((f16[2,616,256]{2,1,0:T(8,128)(2,1)}, f16[2,616,256]{2,1,0:T(8,128)(2,1)}, u32[]{:S(2)}, u32[]{:S(2)}) %collective-permute-start.33) | collective-permute-done | bytes 630816 | tf_op jit(solution)/shard_map/ppermute | solution.py:171
  547.3 4.0 collective-permute-start.34
  551.3 3.8 fusion.5
  557.1 10.1 %collective-permute-done.34 = f16[2,616,256]{2,1,0:T(8,128)(2,1)S(1)} collective-permute-done((f16[2,616,256]{2,1,0:T(8,128)(2,1)S(1)}, f16[2,616,256]{2,1,0:T(8,128)(2,1)S(1)}, u32[]{:S(2)}, u32[]{:S(2)}) %collective-permute-start.34) | collective-permute-done | bytes 630816 | tf_op jit(solution)/shard_map/ppermute | solution.py:171
  573.9 4.2 collective-permute-done.50
  578.5 4.0 collective-permute-done.51
  582.5 9.6 %collective-permute-start.52 = (f32[64,256]{1,0:T(8,128)S(1)}, f32[64,256]{1,0:T(8,128)S(1)}, u32[]{:S(2)}, u32[]{:S(2)}) collective-permute-start(f32[64,256]{1,0:T(8,128)S(1)} %add.805), channel_id=1, source_target_pairs={{0,16},{1,17},{2,18},{3,19},{4,20},{5,21},{6,22},{7,23},{8,24},{9,... | collective-permute-start | bytes 196616 | tf_op jit(solution)/shard_map/ppermute | solution.py:171
  603.3 6.3 collective-permute-done.35
  612.4 9.8 %collective-permute-start.30 = (f16[616,256]{1,0:T(8,128)(2,1)S(1)}, f16[616,256]{1,0:T(8,128)(2,1)S(1)}, u32[]{:S(2)}, u32[]{:S(2)}) collective-permute-start(f16[616,256]{1,0:T(8,128)(2,1)S(1)} %get-tuple-element.173), channel_id=1, source_target_pairs={{0,16},{1,17},{2,18},{3,19},{4,20},{5,21},{6,22},{7,23},{8,24},{9,... | collective-permute-start | bytes 946184 | tf_op jit(solution)/shard_map/ppermute | solution.py:171
  625.4 8.0 %collective-permute-done.30 = f16[616,256]{1,0:T(8,128)(2,1)S(1)} collective-permute-done((f16[616,256]{1,0:T(8,128)(2,1)S(1)}, f16[616,256]{1,0:T(8,128)(2,1)S(1)}, u32[]{:S(2)}, u32[]{:S(2)}) %collective-permute-start.30) | collective-permute-done | bytes 315424 | tf_op jit(solution)/shard_map/ppermute | solution.py:171
  662.2 3.0 collective-permute-done.59
  667.3 7.7 %multiply_add_fusion = (f32[401888]{0:T(1024)}, f32[401888]{0:T(1024)}, f32[401888]{0:T(1024)}, f32[401888]{0:T(1024)}) fusion(f32[401888]{0:T(1024)} %param.23, f32[401888]{0:T(1024)} %param.20, f32[]{:T(128)S(6)} %mul.824, s32[]{:T(128)S(6)} %select_n.703, f32[405504]{0:T(1024)S(1)} %bitcast.308, f32[109568]{0:T(1024)} %collective-permute-done.54, ...), kind=kLoop, calls=%fused_computation.57 | loop fusion | flops 8841536 | bytes 14920712 | tf_op jit(solution)/shard_map/add | solution.py:1193
  (829 shorter events, 255.4 us)
Async XLA Ops:
  7.2 177.0 %all-gather.2.cloned.1.call-start = ((), (), s32[]{:S(2)}) async-start(), calls=%async_computation | async-start | bytes 26763264 | tf_op jit(solution)/shard_map/all_gather | solution.py:1133
  8.8 6.3 collective-permute-start.2
  22.3 10.5 %collective-permute-start.3 = (bf16[1,5,128]{2,0,1:T(2,128)(2,1)S(1)}, bf16[1,5,128]{2,0,1:T(2,128)(2,1)S(1)}, u32[]{:S(2)}, u32[]{:S(2)}) collective-permute-start(bf16[1,5,128]{2,0,1:T(2,128)(2,1)S(1)} %broadcast_in_dim_reshape.3), channel_id=1, source_target_pairs={{0,1},{1,0},{2,3},{3,2},{4,5},{5,4},{6,7},{7,6},{8,9},{9,8},{10,11... | collective-permute-start | bytes 3848 | tf_op jit(solution)/shard_map/ppermute | solution.py:171
  23.3 19.9 %collective-permute-start = (f32[1,2,8,32,6]{3,2,0,4,1:T(8,128)S(1)}, f32[1,2,8,32,6]{3,2,0,4,1:T(8,128)S(1)}, u32[]{:S(2)}, u32[]{:S(2)}) collective-permute-start(f32[1,2,8,32,6]{3,2,0,4,1:T(8,128)S(1)} %maximum_bitcast_fusion), channel_id=1, source_target_pairs={{0,1},{1,0},{2,3},{3,2},{4,5},{5,4},{6,7},{7,6},{8,9},{9,8},{10,11... | collective-permute-start | bytes 36872 | tf_op jit(solution)/shard_map/ppermute | solution.py:171
  32.9 4.9 collective-permute-start.4
  37.8 3.7 collective-permute-start.5
  41.5 4.7 collective-permute-start.6
  43.2 4.9 collective-permute-start.1
  46.2 6.2 collective-permute-start.7
  186.9 20.5 %collective-permute-start.8 = (bf16[512,256]{1,0:T(8,128)(2,1)S(1)}, bf16[512,256]{1,0:T(8,128)(2,1)S(1)}, u32[]{:S(2)}, u32[]{:S(2)}) collective-permute-start(bf16[512,256]{1,0:T(8,128)(2,1)S(1)} %get-tuple-element.52.mine_ref.refs_3_), channel_id=1, source_target_pairs={{0,1},{1,0},{2,3},{3,2},{4,5},{5,4},{6,7},{7,6},{8,9},{9,8},{10,11... | collective-permute-start | bytes 786440 | tf_op jit(solution)/shard_map/ppermute | solution.py:171
  228.3 9.6 %collective-permute-start.10 = (bf16[512,256]{1,0:T(8,128)(2,1)S(1)}, bf16[512,256]{1,0:T(8,128)(2,1)S(1)}, u32[]{:S(2)}, u32[]{:S(2)}) collective-permute-start(bf16[512,256]{1,0:T(8,128)(2,1)S(1)} %get-tuple-element.55), channel_id=1, source_target_pairs={{0,1},{1,0},{2,3},{3,2},{4,5},{5,4},{6,7},{7,6},{8,9},{9,8},{10,11... | collective-permute-start | bytes 786440 | tf_op jit(solution)/shard_map/ppermute | solution.py:171
  263.2 15.1 %collective-permute-start.13 = (bf16[512,1024]{1,0:T(8,128)(2,1)S(1)}, bf16[512,1024]{1,0:T(8,128)(2,1)}, u32[]{:S(2)}, u32[]{:S(2)}) collective-permute-start(bf16[512,1024]{1,0:T(8,128)(2,1)S(1)} %multiply_convert_fusion.1), channel_id=1, source_target_pairs={{0,1},{1,0},{2,3},{3,2},{4,5},{5,4},{6,7},{7,6},{8,9},{9,8},{10,11... | collective-permute-start | bytes 3145736 | tf_op jit(solution)/shard_map/ppermute | solution.py:171
  313.3 16.3 %collective-permute-start.15 = (f32[512,512]{1,0:T(8,128)}, f32[512,512]{1,0:T(8,128)}, u32[]{:S(2)}, u32[]{:S(2)}) collective-permute-start(f32[512,512]{1,0:T(8,128)} %fusion.208), channel_id=1, source_target_pairs={{0,1},{1,0},{2,3},{3,2},{4,5},{5,4},{6,7},{7,6},{8,9},{9,8},{10,11... | collective-permute-start | bytes 3145736 | tf_op jit(solution)/shard_map/ppermute | solution.py:171
  337.0 10.9 %collective-permute-start.16 = (bf16[512,256]{1,0:T(8,128)(2,1)S(1)}, bf16[512,256]{1,0:T(8,128)(2,1)S(1)}, u32[]{:S(2)}, u32[]{:S(2)}) collective-permute-start(bf16[512,256]{1,0:T(8,128)(2,1)S(1)} %copy.176.refs_2_), channel_id=1, source_target_pairs={{0,1},{1,0},{2,3},{3,2},{4,5},{5,4},{6,7},{7,6},{8,9},{9,8},{10,11... | collective-permute-start | bytes 786440 | tf_op jit(solution)/shard_map/ppermute | solution.py:171
  378.3 10.8 %collective-permute-start.17 = (f32[512,512]{1,0:T(8,128)}, f32[512,512]{1,0:T(8,128)}, u32[]{:S(2)}, u32[]{:S(2)}) collective-permute-start(f32[512,512]{1,0:T(8,128)} %fusion.166), channel_id=1, source_target_pairs={{0,1},{1,0},{2,3},{3,2},{4,5},{5,4},{6,7},{7,6},{8,9},{9,8},{10,11... | collective-permute-start | bytes 3145736 | tf_op jit(solution)/shard_map/ppermute | solution.py:171
  383.6 28.2 %collective-permute-start.20 = (f32[2,512]{1,0:T(2,128)S(1)}, f32[2,512]{1,0:T(2,128)S(1)}, u32[]{:S(2)}, u32[]{:S(2)}) collective-permute-start(f32[2,512]{1,0:T(2,128)S(1)} %fusion.210), channel_id=1, source_target_pairs={{0,1},{1,0},{2,3},{3,2},{4,5},{5,4},{6,7},{7,6},{8,9},{9,8},{10,11... | collective-permute-start | bytes 12296 | tf_op jit(solution)/shard_map/ppermute | solution.py:171
  393.5 4.1 collective-permute-start.18
  409.1 5.6 collective-permute-start.19
  414.4 38.9 %collective-permute-start.21 = (bf16[512,256]{1,0:T(8,128)(2,1)S(1)}, bf16[512,256]{1,0:T(8,128)(2,1)S(1)}, u32[]{:S(2)}, u32[]{:S(2)}) collective-permute-start(bf16[512,256]{1,0:T(8,128)(2,1)S(1)} %get-tuple-element.75.refs_1_), channel_id=1, source_target_pairs={{0,1},{1,0},{2,3},{3,2},{4,5},{5,4},{6,7},{7,6},{8,9},{9,8},{10,11... | collective-permute-start | bytes 786440 | tf_op jit(solution)/shard_map/ppermute | solution.py:171
  444.9 4.4 collective-permute-start.26
  469.2 52.7 %collective-permute-start.32 = (f16[4,2,616,256]{3,2,1,0:T(8,128)(2,1)}, f16[4,2,616,256]{3,2,1,0:T(8,128)(2,1)}, u32[]{:S(2)}, u32[]{:S(2)}) collective-permute-start(f16[4,2,616,256]{3,2,1,0:T(8,128)(2,1)} %fusion.20), channel_id=1, source_target_pairs={{0,4},{1,5},{2,6},{3,7},{4,0},{5,1},{6,2},{7,3},{8,12},{9,13},{10,... | collective-permute-start | bytes 7569416 | tf_op jit(solution)/shard_map/ppermute | solution.py:171
  471.9 13.1 %collective-permute-start.40 = (f16[2,2,352,256]{3,2,1,0:T(8,128)(2,1)S(1)}, f16[2,2,352,256]{3,2,1,0:T(8,128)(2,1)S(1)}, u32[]{:S(2)}, u32[]{:S(2)}) collective-permute-start(f16[2,2,352,256]{3,2,1,0:T(8,128)(2,1)S(1)} %get-tuple-element.153), channel_id=1, source_target_pairs={{0,8},{1,9},{2,10},{3,11},{4,12},{5,13},{6,14},{7,15}} | collective-permute-start | bytes 2162696 | tf_op jit(solution)/shard_map/ppermute | solution.py:171
  473.9 26.0 %collective-permute-start.43 = (f16[2,2,352,256]{3,2,1,0:T(8,128)(2,1)S(1)}, f16[2,2,352,256]{3,2,1,0:T(8,128)(2,1)}, u32[]{:S(2)}, u32[]{:S(2)}) collective-permute-start(f16[2,2,352,256]{3,2,1,0:T(8,128)(2,1)S(1)} %get-tuple-element.154), channel_id=1, source_target_pairs={{24,16},{25,17},{26,18},{27,19},{28,20},{29,21},{30,22},{31,23}} | collective-permute-start | bytes 2162696 | tf_op jit(solution)/shard_map/ppermute | solution.py:171
  487.6 15.1 %collective-permute-start.41 = (f16[2,2,352,256]{3,2,1,0:T(8,128)(2,1)}, f16[2,2,352,256]{3,2,1,0:T(8,128)(2,1)}, u32[]{:S(2)}, u32[]{:S(2)}) collective-permute-start(f16[2,2,352,256]{3,2,1,0:T(8,128)(2,1)} %fusion.42), channel_id=1, source_target_pairs={{0,8},{1,9},{2,10},{3,11},{4,12},{5,13},{6,14},{7,15},{8,16},{9,17... | collective-permute-start | bytes 2162696 | tf_op jit(solution)/shard_map/ppermute | solution.py:171
  495.0 52.3 %collective-permute-start.27 = (f16[4,2,616,256]{3,2,0,1:T(8,128)(2,1)}, f16[4,2,616,256]{3,2,0,1:T(8,128)(2,1)}, u32[]{:S(2)}, u32[]{:S(2)}) collective-permute-start(f16[4,2,616,256]{3,2,0,1:T(8,128)(2,1)} %fusion.21), channel_id=1, source_target_pairs={{0,2},{1,3},{2,0},{3,1},{4,6},{5,7},{6,4},{7,5},{8,10},{9,11},{10,... | collective-permute-start | bytes 7569416 | tf_op jit(solution)/shard_map/ppermute | solution.py:171
  505.3 27.4 %collective-permute-start.44 = (f16[2,2,352,256]{3,2,1,0:T(8,128)(2,1)S(1)}, f16[2,2,352,256]{3,2,1,0:T(8,128)(2,1)S(1)}, u32[]{:S(2)}, u32[]{:S(2)}) collective-permute-start(f16[2,2,352,256]{3,2,1,0:T(8,128)(2,1)S(1)} %get-tuple-element.152), channel_id=1, source_target_pairs={{16,8},{17,9},{18,10},{19,11},{20,12},{21,13},{22,14},{23,15},{24,... | collective-permute-start | bytes 2162696 | tf_op jit(solution)/shard_map/ppermute | solution.py:171
  526.9 17.4 %collective-permute-start.33 = (f16[2,616,256]{2,1,0:T(8,128)(2,1)}, f16[2,616,256]{2,1,0:T(8,128)(2,1)}, u32[]{:S(2)}, u32[]{:S(2)}) collective-permute-start(f16[2,616,256]{2,1,0:T(8,128)(2,1)} %get-tuple-element.169), channel_id=1, source_target_pairs={{0,8},{1,9},{2,10},{3,11},{4,12},{5,13},{6,14},{7,15}} | collective-permute-start | bytes 1892360 | tf_op jit(solution)/shard_map/ppermute | solution.py:171
  530.8 38.6 %collective-permute-start.49 = (f32[64,256]{1,0:T(8,128)S(1)}, f32[64,256]{1,0:T(8,128)S(1)}, u32[]{:S(2)}, u32[]{:S(2)}) collective-permute-start(f32[64,256]{1,0:T(8,128)S(1)} %pad.83), channel_id=1, source_target_pairs={{0,2},{1,3},{2,0},{3,1},{4,6},{5,7},{6,4},{7,5},{8,10},{9,11},{10,... | collective-permute-start | bytes 196616 | tf_op jit(solution)/shard_map/ppermute | solution.py:171
  531.4 38.6 %collective-permute-start.42 = (f16[2,2,352,256]{3,2,1,0:T(8,128)(2,1)S(1)}, f16[2,2,352,256]{3,2,1,0:T(8,128)(2,1)S(1)}, u32[]{:S(2)}, u32[]{:S(2)}) collective-permute-start(f16[2,2,352,256]{3,2,1,0:T(8,128)(2,1)S(1)} %get-tuple-element.151), channel_id=1, source_target_pairs={{0,8},{1,9},{2,10},{3,11},{4,12},{5,13},{6,14},{7,15},{8,16},{9,17... | collective-permute-start | bytes 2162696 | tf_op jit(solution)/shard_map/ppermute | solution.py:171
  534.4 35.6 %collective-permute-start.45 = (f16[2,2,352,256]{3,2,1,0:T(8,128)(2,1)S(1)}, f16[2,2,352,256]{3,2,1,0:T(8,128)(2,1)S(1)}, u32[]{:S(2)}, u32[]{:S(2)}) collective-permute-start(f16[2,2,352,256]{3,2,1,0:T(8,128)(2,1)S(1)} %fusion.41), channel_id=1, source_target_pairs={{8,0},{9,1},{10,2},{11,3},{12,4},{13,5},{14,6},{15,7},{16,8},{17,9... | collective-permute-start | bytes 2162696 | tf_op jit(solution)/shard_map/ppermute | solution.py:171
  544.3 12.3 %collective-permute-start.36 = (f16[2,616,256]{2,1,0:T(8,128)(2,1)S(1)}, f16[2,616,256]{2,1,0:T(8,128)(2,1)S(1)}, u32[]{:S(2)}, u32[]{:S(2)}) collective-permute-start(f16[2,616,256]{2,1,0:T(8,128)(2,1)S(1)} %get-tuple-element.170), channel_id=1, source_target_pairs={{24,16},{25,17},{26,18},{27,19},{28,20},{29,21},{30,22},{31,23}} | collective-permute-start | bytes 1892360 | tf_op jit(solution)/shard_map/ppermute | solution.py:171
  547.3 19.9 %collective-permute-start.34 = (f16[2,616,256]{2,1,0:T(8,128)(2,1)S(1)}, f16[2,616,256]{2,1,0:T(8,128)(2,1)S(1)}, u32[]{:S(2)}, u32[]{:S(2)}) collective-permute-start(f16[2,616,256]{2,1,0:T(8,128)(2,1)S(1)} %fusion.52), channel_id=1, source_target_pairs={{0,8},{1,9},{2,10},{3,11},{4,12},{5,13},{6,14},{7,15},{8,16},{9,17... | collective-permute-start | bytes 1892360 | tf_op jit(solution)/shard_map/ppermute | solution.py:171
  556.6 43.5 %collective-permute-start.28 = (f16[4,616,256]{2,1,0:T(8,128)(2,1)}, f16[4,616,256]{2,1,0:T(8,128)(2,1)S(1)}, u32[]{:S(2)}, u32[]{:S(2)}) collective-permute-start(f16[4,616,256]{2,1,0:T(8,128)(2,1)} %fusion.49), channel_id=1, source_target_pairs={{0,4},{1,5},{2,6},{3,7},{4,0},{5,1},{6,2},{7,3},{8,12},{9,13},{10,... | collective-permute-start | bytes 3784712 | tf_op jit(solution)/shard_map/ppermute | solution.py:171
  568.7 26.0 %collective-permute-start.37 = (f16[2,616,256]{2,1,0:T(8,128)(2,1)}, f16[2,616,256]{2,1,0:T(8,128)(2,1)S(1)}, u32[]{:S(2)}, u32[]{:S(2)}) collective-permute-start(f16[2,616,256]{2,1,0:T(8,128)(2,1)} %get-tuple-element.168), channel_id=1, source_target_pairs={{16,8},{17,9},{18,10},{19,11},{20,12},{21,13},{22,14},{23,15},{24,... | collective-permute-start | bytes 1892360 | tf_op jit(solution)/shard_map/ppermute | solution.py:171
  569.4 8.8 %collective-permute-start.50 = (f32[64,256]{1,0:T(8,128)S(1)}, f32[64,256]{1,0:T(8,128)S(1)}, u32[]{:S(2)}, u32[]{:S(2)}) collective-permute-start(f32[64,256]{1,0:T(8,128)S(1)} %pad_add_fusion.1), channel_id=1, source_target_pairs={{0,4},{1,5},{2,6},{3,7},{4,0},{5,1},{6,2},{7,3},{8,12},{9,13},{10,... | collective-permute-start | bytes 196616 | tf_op jit(solution)/shard_map/ppermute | solution.py:171
  572.5 25.0 %collective-permute-start.46 = (f16[2,352,256]{2,1,0:T(8,128)(2,1)}, f16[2,352,256]{2,1,0:T(8,128)(2,1)}, u32[]{:S(2)}, u32[]{:S(2)}) collective-permute-start(f16[2,352,256]{2,1,0:T(8,128)(2,1)} %fusion.91), channel_id=1, source_target_pairs={{0,2},{1,3},{2,0},{3,1},{4,6},{5,7},{6,4},{7,5},{8,10},{9,11},{10,... | collective-permute-start | bytes 1081352 | tf_op jit(solution)/shard_map/ppermute | solution.py:171
  578.2 4.3 collective-permute-start.51
  582.5 51.5 %collective-permute-start.52 = (f32[64,256]{1,0:T(8,128)S(1)}, f32[64,256]{1,0:T(8,128)S(1)}, u32[]{:S(2)}, u32[]{:S(2)}) collective-permute-start(f32[64,256]{1,0:T(8,128)S(1)} %add.805), channel_id=1, source_target_pairs={{0,16},{1,17},{2,18},{3,19},{4,20},{5,21},{6,22},{7,23},{8,24},{9,... | collective-permute-start | bytes 196616 | tf_op jit(solution)/shard_map/ppermute | solution.py:171
  592.2 17.4 %collective-permute-start.35 = (f16[2,616,256]{2,1,0:T(8,128)(2,1)}, f16[2,616,256]{2,1,0:T(8,128)(2,1)S(1)}, u32[]{:S(2)}, u32[]{:S(2)}) collective-permute-start(f16[2,616,256]{2,1,0:T(8,128)(2,1)} %get-tuple-element.167), channel_id=1, source_target_pairs={{0,8},{1,9},{2,10},{3,11},{4,12},{5,13},{6,14},{7,15},{8,16},{9,17... | collective-permute-start | bytes 1892360 | tf_op jit(solution)/shard_map/ppermute | solution.py:171
  596.2 16.3 %collective-permute-start.38 = (f16[2,616,256]{2,1,0:T(8,128)(2,1)S(1)}, f16[2,616,256]{2,1,0:T(8,128)(2,1)S(1)}, u32[]{:S(2)}, u32[]{:S(2)}) collective-permute-start(f16[2,616,256]{2,1,0:T(8,128)(2,1)S(1)} %fusion.51), channel_id=1, source_target_pairs={{8,0},{9,1},{10,2},{11,3},{12,4},{13,5},{14,6},{15,7},{16,8},{17,9... | collective-permute-start | bytes 1892360 | tf_op jit(solution)/shard_map/ppermute | solution.py:171
  598.6 25.2 %collective-permute-start.47 = (f16[352,256]{1,0:T(8,128)(2,1)S(1)}, f16[352,256]{1,0:T(8,128)(2,1)S(1)}, u32[]{:S(2)}, u32[]{:S(2)}) collective-permute-start(f16[352,256]{1,0:T(8,128)(2,1)S(1)} %fusion.105), channel_id=1, source_target_pairs={{0,4},{1,5},{2,6},{3,7},{4,0},{5,1},{6,2},{7,3},{8,12},{9,13},{10,... | collective-permute-start | bytes 540680 | tf_op jit(solution)/shard_map/ppermute | solution.py:171
  600.6 24.8 %collective-permute-start.29 = (f16[616,256]{1,0:T(8,128)(2,1)S(1)}, f16[616,256]{1,0:T(8,128)(2,1)S(1)}, u32[]{:S(2)}, u32[]{:S(2)}) collective-permute-start(f16[616,256]{1,0:T(8,128)(2,1)S(1)} %get-tuple-element.171), channel_id=1, source_target_pairs={{0,8},{1,9},{2,10},{3,11},{4,12},{5,13},{6,14},{7,15},{8,16},{9,17... | collective-permute-start | bytes 946184 | tf_op jit(solution)/shard_map/ppermute | solution.py:171
  609.6 15.8 %collective-permute-start.31 = (f16[616,256]{1,0:T(8,128)(2,1)S(1)}, f16[616,256]{1,0:T(8,128)(2,1)S(1)}, u32[]{:S(2)}, u32[]{:S(2)}) collective-permute-start(f16[616,256]{1,0:T(8,128)(2,1)S(1)} %get-tuple-element.172), channel_id=1, source_target_pairs={{0,24},{1,25},{2,26},{3,27},{4,28},{5,29},{6,30},{7,31},{8,0},{9,1... | collective-permute-start | bytes 946184 | tf_op jit(solution)/shard_map/ppermute | solution.py:171
  612.4 21.0 %collective-permute-start.30 = (f16[616,256]{1,0:T(8,128)(2,1)S(1)}, f16[616,256]{1,0:T(8,128)(2,1)S(1)}, u32[]{:S(2)}, u32[]{:S(2)}) collective-permute-start(f16[616,256]{1,0:T(8,128)(2,1)S(1)} %get-tuple-element.173), channel_id=1, source_target_pairs={{0,16},{1,17},{2,18},{3,19},{4,20},{5,21},{6,22},{7,23},{8,24},{9,... | collective-permute-start | bytes 946184 | tf_op jit(solution)/shard_map/ppermute | solution.py:171
  623.8 9.8 %collective-permute-start.39 = (f16[616,256]{1,0:T(8,128)(2,1)S(1)}, f16[616,256]{1,0:T(8,128)(2,1)S(1)}, u32[]{:S(2)}, u32[]{:S(2)}) collective-permute-start(f16[616,256]{1,0:T(8,128)(2,1)S(1)} %fusion.95), channel_id=1, source_target_pairs={{0,2},{1,3},{2,0},{3,1},{4,6},{5,7},{6,4},{7,5},{8,10},{9,11},{10,... | collective-permute-start | bytes 946184 | tf_op jit(solution)/shard_map/ppermute | solution.py:171
  633.9 4.7 collective-permute-start.48
  640.4 27.0 %collective-permute-start.54 = (f32[109568]{0:T(1024)}, f32[109568]{0:T(1024)}, u32[]{:S(2)}, u32[]{:S(2)}) collective-permute-start(f32[109568]{0:T(1024)} %slice.448), channel_id=1, source_target_pairs={{0,1},{1,2},{2,3},{3,4},{4,5},{5,6},{6,7},{7,8},{8,9},{9,10},{10,1... | collective-permute-start | bytes 1314824 | tf_op jit(solution)/shard_map/ppermute | solution.py:171
  660.8 4.5 collective-permute-start.59
  (202 other events, 1746.8 us)
Sparse Core Ops, SparseCore 0:
  22.4 161.7 all-gather.1

commit v2 on v1

--- a/solution.py
+++ b/solution.py
@@ -269,12 +269,34 @@
     return values.astype(jnp.float32)
 
 
-def largest_of_all(place, top):
-    stride = 1
-    while stride < place.count:
-        top = jnp.maximum(top, place.swap(top, stride))
-        stride *= 2
-    return top
+def lane_row(values):
+    lane = lax.broadcasted_iota(jnp.int32, (1, 128), 1)
+    row = jnp.zeros((1, 128), jnp.float32)
+    for i, value in enumerate(values):
+        row = jnp.where(lane == i, value, row)
+    return row
+
+
+SQUARE_AT = 8
+
+
+class Largest:
+    def __init__(self, place, values):
+        self.place, self.values, self.stride = (place, values, 1)
+
+    def exchange(self, beside=None):
+        if self.stride < self.place.count:
+            got = self.place.swap(self.values, self.stride)
+            if beside is not None:
+                got, beside = lax.optimization_barrier((got, beside))
+            self.values = jnp.maximum(self.values, got)
+            self.stride *= 2
+        return beside
+
+    def finish(self):
+        while self.stride < self.place.count:
+            self.exchange()
+        return self.values
 
 
 def scatter_part(place, grads, low_row, rows, order, scale):
@@ -327,10 +349,13 @@
     for i in range(3):
         order = axes[i:] + axes[:i]
         parts.append(scatter_part(place, held, cuts[i], cuts[i + 1] - cuts[i], order, scale))
-    chip = jnp.concatenate(parts, axis=0).reshape(2, rows, HALF) * (1.0 / scale)
+    unit = 1.0 / scale
+    parts = [part * unit for part in parts]
+    square = sum(jnp.sum(part * part) for part in parts).reshape(1, 1)
+    chip = jnp.concatenate(parts, axis=0).reshape(2, rows, HALF)
     mine = pick(chip, place.side, 0)
     other = place.swap(pick(chip, 1 - place.side, 0))
-    return place.join(mine, other)
+    return (place.join(mine, other), square)
 
 
 class Store:
@@ -355,7 +380,6 @@
         grad_into(self, inputs, gradient, self.places[name])
 
     def put(self, at, values):
-        self.top = jnp.maximum(self.top, jnp.max(jnp.abs(values)).reshape(1, 1))
         self.buffer = lax.dynamic_update_slice(self.buffer, values, (at, 0))
 
 
@@ -564,10 +588,14 @@
             fill_moved(moved, both.astype(jnp.float32))
             total[...] = jnp.zeros_like(total)
 
-        row_off, col_off = tap_of(step, info_ref[1])
-        total[...] += dot(moved[col_off + 1, rows_from(row_off), :], weight_ref[...])
-
-        @pl.when(step == 8)
+        part = None
+        for j in range(3):
+            row_off, col_off = tap_of(3 * step + j, info_ref[1])
+            one = dot(moved[col_off + 1, rows_from(row_off), :], weight_ref[C * j : C * (j + 1), :])
+            part = one if part is None else part + one
+        total[...] += part
+
+        @pl.when(step == 2)
         def _():
             value_out = outs[3] if with_base else None
             held = base_ref[...] if with_base else None
@@ -581,14 +609,14 @@
         body,
         grid_spec=pltpu.PrefetchScalarGridSpec(
             num_scalar_prefetch=1,
-            grid=(9,),
+            grid=(3,),
             in_specs=[
                 whole(mine.shape),
                 whole(other.shape),
                 pl.BlockSpec(
-                    (pl.Element(C), pl.Element(HALF)),
+                    (pl.Element(3 * C), pl.Element(HALF)),
                     lambda i, info_ref: (
-                        pl.multiple_of(at + C * i, 8),
+                        pl.multiple_of(at + 3 * C * i, 8),
                         pl.multiple_of(HALF * info_ref[0], HALF),
                     ),
                 ),
@@ -609,13 +637,14 @@
 
 def conv_backward(info, grad_mine, grad_other, act_mine, act_other, table, store, at, saved, rows, base):
     with_base = base is not None
-    old, old_specs, out_spec, out_shape = store_specs(store, at, C)
+    old, old_specs, out_spec, out_shape = store_specs(store, at, 3 * C)
 
     def body(info_ref, *refs):
         refs = refs[len(old) :]
-        gm_ref, go_ref, am_ref, ao_ref, weight_ref, normed_ref, inv_ref, rows_ref = refs[:8]
-        base_ref = refs[8] if with_base else None
-        refs = refs[8 + int(with_base) :]
+        gm_ref, go_ref, am_ref, ao_ref = refs[:4]
+        weight_refs, (normed_ref, inv_ref, rows_ref) = (refs[4:7], refs[7:10])
+        base_ref = refs[10] if with_base else None
+        refs = refs[10 + int(with_base) :]
         out_ref, low_out, sums_out = refs[:3]
         moved, turned_act, shifted, total = refs[-4:]
         step = pl.program_id(0)
@@ -633,11 +662,16 @@
             shifted[FRAME + TOKENS : PADDED, :] = empty
             total[...] = jnp.zeros_like(total)
 
-        row_off, col_off = tap_of(step, info_ref[1])
-        out_ref[...] = dot(turned_act[col_off + 1], shifted[rows_from(-row_off), :])
-        total[...] += dot_t(moved[1 - col_off, rows_from(-row_off), :], weight_ref[...])
-
-        @pl.when(step == 8)
+        part = None
+        for j in range(3):
+            row_off, col_off = tap_of(3 * step + j, info_ref[1])
+            rows_at = rows_from(-row_off)
+            out_ref[C * j : C * (j + 1), :] = dot(turned_act[col_off + 1], shifted[rows_at, :])
+            one = dot_t(moved[1 - col_off, rows_at, :], weight_refs[j][...])
+            part = one if part is None else part + one
+        total[...] += part
+
+        @pl.when(step == 2)
         def _():
             mask = token_mask(info_ref[2])
             gain, normed, inv_std = (rows_ref[0:1], normed_ref[...], inv_ref[0:1])
@@ -656,23 +690,25 @@
             sums_out[1:2] = gain_grad
             sums_out[2:3] = bias_grad
 
+    def tap_rows(j):
+        return pl.BlockSpec(
+            (pl.Element(HALF), pl.Element(C)),
+            lambda i, info_ref: (pl.multiple_of(at + C * (3 * i + j) + HALF * info_ref[0], 8), 0),
+        )
+
     extra = [base] if with_base else []
     operands = [grad_mine, grad_other, act_mine, act_other]
     result = pl.pallas_call(
         body,
         grid_spec=pltpu.PrefetchScalarGridSpec(
             num_scalar_prefetch=1,
-            grid=(9,),
+            grid=(3,),
             in_specs=old_specs
             + [whole(one.shape) for one in operands]
             + [
-                pl.BlockSpec(
-                    (pl.Element(HALF), pl.Element(C)),
-                    lambda i, info_ref: (
-                        pl.multiple_of(at + C * i + HALF * info_ref[0], 8),
-                        0,
-                    ),
-                ),
+                tap_rows(j) for j in range(3)
+            ]
+            + [
                 whole((TOKENS, HALF)),
                 whole((8, HALF)),
                 whole(rows.shape),
@@ -698,7 +734,7 @@
         input_output_aliases={1 + k: k for k in range(len(old))},
         compiler_params=params(),
         cost_estimate=cost(36 * TOKENS * C * HALF, 9 * C * HALF * 6 + 6 * TOKENS * HALF * 4),
-    )(info, *old, *operands, table, *saved, rows, *extra)
+    )(info, *old, *operands, table, table, table, *saved, rows, *extra)
     store.write(result[0], None)
     return (result[1], result[2])
 
@@ -720,6 +756,439 @@
         jnp.sum(gradient * normed, axis=0, keepdims=True),
         jnp.sum(gradient, axis=0, keepdims=True),
     )
+
+
+def unmix(info, table, at, depth, pieces, columns):
+    tile = min(depth, 128 if pieces > 4 else 256)
+
+    def body(info_ref, rows_ref, out_ref, mixed):
+        for side in range(columns // 128):
+            mixed[...] = rows_ref[:, side * 128 : (side + 1) * 128].astype(jnp.float32)
+            for j in range(pieces):
+                column = j * columns + side * 128
+                out_ref[:, column : column + 128] = low(mixed[pl.ds(j, tile, stride=pieces), :])
+
+    return pl.pallas_call(
+        body,
+        grid_spec=pltpu.PrefetchScalarGridSpec(
+            num_scalar_prefetch=1,
+            grid=(depth // tile,),
+            in_specs=[
+                pl.BlockSpec(
+                    (pl.Element(tile * pieces), pl.Element(columns)),
+                    lambda i, info_ref: (
+                        pl.multiple_of(at + tile * pieces * i, 8),
+                        pl.multiple_of(HALF * info_ref[0] * int(columns == HALF), HALF),
+                    ),
+                )
+            ],
+            out_specs=pl.BlockSpec((tile, pieces * columns), lambda i, info_ref: (i, 0)),
+            scratch_shapes=[pltpu.VMEM((tile * pieces, 128), jnp.float32)],
+        ),
+        out_shape=jax.ShapeDtypeStruct((depth, pieces * columns), jnp.bfloat16),
+        compiler_params=params(),
+        cost_estimate=cost(0, 4 * depth * pieces * columns),
+    )(info, table)
+
+
+class Rows:
+    def __init__(self, at, count, side_columns=False, side_rows=False):
+        self.at, self.count = (at, count)
+        self.side_columns, self.side_rows = (side_columns, side_rows)
+
+    def spec(self):
+        at, columns, rows = (self.at, int(self.side_columns), int(self.side_rows))
+        return pl.BlockSpec(
+            (pl.Element(self.count), pl.Element(HALF if columns else WIDE)),
+            lambda i, info_ref: (
+                pl.multiple_of(at + HALF * info_ref[0] * rows, 8),
+                pl.multiple_of(HALF * info_ref[0] * columns, HALF),
+            ),
+        )
+
+
+def one_step(body, info, table, operands, outs, flops):
+    arrays = [table if isinstance(one, Rows) else one for one in operands]
+    specs = [one.spec() if isinstance(one, Rows) else whole(one.shape) for one in operands]
+    shapes = [jax.ShapeDtypeStruct(shape, kind) for shape, kind in outs]
+    nbytes = sum(math.prod(one.shape) * one.dtype.itemsize for one in shapes)
+    return pl.pallas_call(
+        body,
+        grid_spec=pltpu.PrefetchScalarGridSpec(
+            num_scalar_prefetch=1,
+            grid=(1,),
+            in_specs=specs,
+            out_specs=[whole(one.shape) for one in shapes],
+        ),
+        out_shape=shapes,
+        compiler_params=params(),
+        cost_estimate=cost(flops, 2 * nbytes),
+    )(info, *arrays)
+
+
+f32, bf16 = (jnp.float32, jnp.bfloat16)
+
+
+def side_of(side, values):
+    return jnp.where(side == 0, values[:, :HALF], values[:, HALF:])
+
+
+def layer_parts(values):
+    centered = values - jnp.mean(values, axis=-1, keepdims=True)
+    var_val = jnp.mean(centered * centered, axis=-1, keepdims=True)
+    inv_std = lax.rsqrt(var_val + eps_layer)
+    return (centered * inv_std, inv_std)
+
+
+def layer_back(gradient, values, gain, base, side, sums_ref):
+    normed, inv_std = layer_parts(values)
+    scaled = gradient * gain
+    first = jnp.mean(scaled, axis=-1, keepdims=True)
+    second = jnp.mean(scaled * normed, axis=-1, keepdims=True)
+    result = base + inv_std * (scaled - first - normed * second)
+    sums_ref[0:1] = side_of(side, jnp.sum(result, axis=0, keepdims=True))
+    sums_ref[1:2] = side_of(side, jnp.sum(gradient * normed, axis=0, keepdims=True))
+    sums_ref[2:3] = side_of(side, jnp.sum(gradient, axis=0, keepdims=True))
+    return result
+
+
+def head_lanes(head):
+    return lax.broadcasted_iota(jnp.int32, (1, HALF), 1) // DHEAD == head
+
+
+def head_probs(query, key, head, limit):
+    mine = jnp.where(head_lanes(head), query, jnp.zeros((), bf16))
+    scores = dot_t(mine, key) * 0.125
+    seen = lax.broadcasted_iota(jnp.int32, (1, TOKENS), 1) < limit
+    scores = jnp.where(seen, scores, -1e30)
+    exponent = jnp.exp(scores - jnp.max(scores, axis=-1, keepdims=True))
+    return exponent / jnp.sum(exponent, axis=-1, keepdims=True)
+
+
+def self_front(info, table, mine, other, weight, rows, qkv):
+    def body(info_ref, mine_ref, other_ref, weight_ref, rows_ref, qkv_ref, *outs):
+        token_ref, resid_ref, ln_ref, packed_ref, out_ref = outs
+        token = two_sides(info_ref[0], mine_ref[...], other_ref[...])
+        token_ref[...] = token
+        resid = dot(token, weight_ref[...]) + rows_ref[0:1]
+        resid_ref[...] = resid
+        ln = low(layer_parts(resid)[0] * rows_ref[1:2] + rows_ref[2:3])
+        ln_ref[...] = ln
+        packed_ref[...] = low(dot(ln, qkv_ref[...]))
+        query, key = (packed_ref[:, 0:HALF], packed_ref[:, HALF : 2 * HALF])
+        value = packed_ref[:, 2 * HALF : 3 * HALF]
+        total = jnp.zeros((TOKENS, HALF), f32)
+        for head in range(LOCAL_HEADS):
+            probs = head_probs(query, key, head, info_ref[2])
+            total = jnp.where(head_lanes(head), dot(low(probs), value), total)
+        out_ref[...] = low(total)
+
+    outs = [
+        ((TOKENS, C), bf16),
+        ((TOKENS, C), f32),
+        ((TOKENS, C), bf16),
+        ((TOKENS, 3 * HALF), bf16),
+        ((TOKENS, HALF), bf16),
+    ]
+    flops = 2 * TOKENS * C * (C + 3 * HALF) + 4 * LOCAL_HEADS * TOKENS * TOKENS * HALF
+    return one_step(body, info, table, [mine, other, weight, rows, qkv], outs, flops)
+
+
+def same_head():
+    left = lax.broadcasted_iota(jnp.int32, (HALF, HALF), 0) // DHEAD
+    right = lax.broadcasted_iota(jnp.int32, (HALF, HALF), 1) // DHEAD
+    return (left == right).astype(f32)
+
+
+def head_sums(values, same):
+    return jnp.dot(values, same, precision=lax.Precision.HIGHEST, preferred_element_type=f32)
+
+
+def cross_probs(query, context, same):
+    first = head_sums(query * context[0:1, :HALF], same) * 0.125
+    second = head_sums(query * context[1:2, :HALF], same) * 0.125
+    top = jnp.maximum(first, second)
+    first, second = (jnp.exp(first - top), jnp.exp(second - top))
+    total = first + second
+    return (first / total, second / total)
+
+
+def cross_front(info, table, mine, other, weight, rows, resid, query_weight, context):
+    def body(info_ref, mine_ref, other_ref, weight_ref, rows_ref, old_ref, qw_ref, kv_ref, *outs):
+        full_ref, resid_ref, ln_ref, query_ref, out_ref = outs
+        joined = two_sides(info_ref[0], mine_ref[...], other_ref[...])
+        full_ref[...] = joined
+        resid_now = old_ref[...] + dot(joined, weight_ref[...]) + rows_ref[0:1]
+        resid_ref[...] = resid_now
+        ln = low(layer_parts(resid_now)[0] * rows_ref[1:2] + rows_ref[2:3])
+        ln_ref[...] = ln
+        query = low(dot(ln, qw_ref[...]))
+        query_ref[...] = query
+        both = kv_ref[...].astype(f32)
+        first, second = cross_probs(query.astype(f32), both, same_head())
+        out_ref[...] = low(first * both[0:1, HALF:] + second * both[1:2, HALF:])
+
+    outs = [
+        ((TOKENS, C), bf16),
+        ((TOKENS, C), f32),
+        ((TOKENS, C), bf16),
+        ((TOKENS, HALF), bf16),
+        ((TOKENS, HALF), bf16),
+    ]
+    operands = [mine, other, weight, rows, resid, query_weight, context]
+    return one_step(body, info, table, operands, outs, 2 * TOKENS * C * (C + 13 * HALF))
+
+
+def gelu_parts(gate):
+    return 0.5 * (1.0 + lax.erf(gate * math.sqrt(0.5)))
+
+
+WIDE_FF = FFI // 2
+
+
+def ff_front(info, table, mine, other, weight, rows, resid, ff_weight, ff_bias):
+    def body(info_ref, mine_ref, other_ref, weight_ref, rows_ref, old_ref, fw_ref, fb_ref, *outs):
+        full_ref, resid_ref, ln_ref, proj_ref, out_ref = outs
+        joined = two_sides(info_ref[0], mine_ref[...], other_ref[...])
+        full_ref[...] = joined
+        resid_now = old_ref[...] + dot(joined, weight_ref[...]) + rows_ref[0:1]
+        resid_ref[...] = resid_now
+        ln = low(layer_parts(resid_now)[0] * rows_ref[1:2] + rows_ref[2:3])
+        ln_ref[...] = ln
+        for at in range(0, WIDE_FF, HALF):
+            gate_at = WIDE_FF + at
+            lift = dot(ln, fw_ref[:, at : at + HALF]) + fb_ref[:, at : at + HALF]
+            gate = dot(ln, fw_ref[:, gate_at : gate_at + HALF]) + fb_ref[:, gate_at : gate_at + HALF]
+            proj_ref[:, at : at + HALF] = lift
+            proj_ref[:, gate_at : gate_at + HALF] = gate
+            out_ref[:, at : at + HALF] = low(lift * gate * gelu_parts(gate))
+
+    outs = [
+        ((TOKENS, C), bf16),
+        ((TOKENS, C), f32),
+        ((TOKENS, C), bf16),
+        ((TOKENS, FFI), f32),
+        ((TOKENS, WIDE_FF), bf16),
+    ]
+    operands = [mine, other, weight, rows, resid, ff_weight, ff_bias]
+    return one_step(body, info, table, operands, outs, 2 * TOKENS * C * (C + FFI))
+
+
+def ff_finish(info, table, mine, other, weight, rows, resid, out_weight, out_bias, state):
+    def body(info_ref, mine_ref, other_ref, weight_ref, rows_ref, old_ref, ow_ref, ob_ref, state_ref, *outs):
+        full_ref, resid_ref, out_ref = outs
+        side = info_ref[0]
+        for at in range(0, WIDE_FF, HALF):
+            own, peer = (mine_ref[:, at : at + HALF], other_ref[:, at : at + HALF])
+            full_ref[:, 2 * at : 2 * at + WIDE] = two_sides(side, own, peer)
+        resid_now = old_ref[...] + dot(full_ref[...], weight_ref[...]) + rows_ref[0:1]
+        inner = low(resid_now)
+        resid_ref[...] = inner
+        branch = dot(inner, ow_ref[...]) + ob_ref[0:1]
+        out_ref[...] = low(state_ref[...] + token_mask(info_ref[2]) * branch)
+
+    outs = [((TOKENS, FFI), bf16), ((TOKENS, C), bf16), ((TOKENS, HALF), bf16)]
+    operands = [mine, other, weight, rows, resid, out_weight, out_bias, state]
+    return one_step(body, info, table, operands, outs, 2 * TOKENS * C * (FFI + HALF))
+
+
+def lanes_moved(values, row_off, col_off):
+    token = lax.broadcasted_iota(jnp.int32, (1, TOKENS), 1)
+    row, col = (token // FRAME + row_off, token % FRAME + col_off)
+    keep = (row >= 0) & (row < SIDE) & (col >= 0) & (col < FRAME)
+    away = FRAME * row_off + col_off
+    return jnp.where(keep, pltpu.roll(values, lax.rem(TOKENS - away, TOKENS), 1), 0.0)
+
+
+OUT_ROWS = 8
+
+
+def loss_back(info, table, mine, other, out_weight, noise, bias, pout, ff2, projected, ff1):
+    def body(info_ref, *refs):
+        mine_ref, other_ref, ow_ref, noise_ref, bias_ref, pout_ref, ff2_ref, proj_ref, ff1_ref = refs[:9]
+        ow_grad, small_out, state_out, pout_low, ff2_low, resid_out, proj_low, ln_out, sums, ff_sums = refs[9:]
+        side, turned, limit = (info_ref[0], info_ref[1], info_ref[2])
+        state = two_sides(side, mine_ref[...], other_ref[...])
+        raw = dot_t(ow_ref[...], state)
+        predicted = bias_ref[:, 0:1]
+        for tap in range(9):
+            row_off, col_off = tap_of(tap, turned)
+            part = raw[tap * OUT_ROWS : (tap + 1) * OUT_ROWS]
+            predicted = predicted + lanes_moved(part, row_off, col_off)
+        token = lax.broadcasted_iota(jnp.int32, (OUT_ROWS, TOKENS), 1)
+        channel = lax.broadcasted_iota(jnp.int32, (OUT_ROWS, TOKENS), 0)
+        error = jnp.where((token < limit) & (channel < LC), predicted - noise_ref[...], 0.0)
+        loss = jnp.sum(jnp.sum(error * error, axis=1, keepdims=True), axis=0, keepdims=True)
+        gradient = 2.0 * error
+        small_out[:, 0:128] = jnp.broadcast_to(jnp.sum(gradient, axis=1, keepdims=True), (OUT_ROWS, 128))
+        small_out[:, 128:256] = jnp.broadcast_to(loss, (OUT_ROWS, 128))
+        gradient = low(gradient).astype(f32)
+        moved = []
+        for tap in range(9):
+            row_off, col_off = tap_of(tap, turned)
+            moved.append(lanes_moved(gradient, -row_off, -col_off))
+        moved = low(jnp.concatenate(moved, axis=0))
+        ow_grad[...] = dot(moved, state)
+        state_grad = t_dot(moved, ow_ref[...])
+        state_out[...] = side_of(side, state_grad)
+        branch = token_mask(limit) * state_grad
+        sums[1:2] = side_of(side, jnp.sum(branch, axis=0, keepdims=True))
+        branch = low(branch)
+        pout_low[...] = side_of(side, branch)
+        resid_grad = dot_t(branch, pout_ref[...])
+        resid_out[...] = resid_grad
+        sums[0:1] = side_of(side, jnp.sum(resid_grad, axis=0, keepdims=True))
+        resid_low = low(resid_grad)
+        ff2_low[...] = side_of(side, resid_low)
+        total = jnp.zeros((TOKENS, C), f32)
+        for j in range(WIDE_FF // HALF):
+            at, gate_at = (j * HALF, WIDE_FF + j * HALF)
+            own = pl.ds(pl.multiple_of(WIDE * j + HALF * side, HALF), HALF)
+            gated_grad = dot_t(resid_low, ff2_ref[own, :])
+            lift, gate = (proj_ref[:, at : at + HALF], proj_ref[:, gate_at : gate_at + HALF])
+            cdf = gelu_parts(gate)
+            density = jnp.exp(-0.5 * gate * gate) * (1.0 / math.sqrt(2.0 * math.pi))
+            lift_grad = gated_grad * gate * cdf
+            gate_grad = gated_grad * lift * (cdf + gate * density)
+            ff_sums[j : j + 1] = jnp.sum(lift_grad, axis=0, keepdims=True)
+            ff_sums[4 + j : 5 + j] = jnp.sum(gate_grad, axis=0, keepdims=True)
+            lift_grad, gate_grad = (low(lift_grad), low(gate_grad))
+            proj_low[:, at : at + HALF] = lift_grad
+            proj_low[:, gate_at : gate_at + HALF] = gate_grad
+            total = total + dot_t(lift_grad, ff1_ref[:, at : at + HALF])
+            total = total + dot_t(gate_grad, ff1_ref[:, gate_at : gate_at + HALF])
+        ln_out[...] = total
+
+    outs = [
+        ((9 * OUT_ROWS, C), f32),
+        ((OUT_ROWS, HALF), f32),
+        ((TOKENS, HALF), f32),
+        ((TOKENS, HALF), bf16),
+        ((TOKENS, HALF), bf16),
+        ((TOKENS, C), f32),
+        ((TOKENS, FFI), bf16),
+        ((TOKENS, C), f32),
+        ((8, HALF), f32),
+        ((8, HALF), f32),
+    ]
+    operands = [mine, other, out_weight, noise, bias, pout, ff2, projected, ff1]
+    return one_step(body, info, table, operands, outs, 2 * TOKENS * C * (C + FFI + WIDE_FF))
+
+
+def cross_back(info, table, mine, other, resid, gain, base, weight, query, context):
+    def body(info_ref, mine_ref, other_ref, resid_ref, gain_ref, base_ref, weight_ref, query_ref, kv_ref, *outs):
+        resid_out, co_low, query_low, kv_grad, sums = outs
+        side = info_ref[0]
+        result = layer_back(
+            mine_ref[...] + other_ref[...], resid_ref[...], gain_ref[0:1], base_ref[...], side, sums
+        )
+        resid_out[...] = result
+        result = low(result)
+        co_low[...] = side_of(side, result)
+        out_grad = low(dot_t(result, weight_ref[...])).astype(f32)
+        same, both, query_now = (same_head(), kv_ref[...].astype(f32), query_ref[...].astype(f32))
+        first, second = cross_probs(query_now, both, same)
+        first_grad = head_sums(out_grad * both[0:1, HALF:], same)
+        second_grad = head_sums(out_grad * both[1:2, HALF:], same)
+        inner = first * first_grad + second * second_grad
+        first_grad = first * (first_grad - inner) * 0.125
+        second_grad = second * (second_grad - inner) * 0.125
+        query_low[...] = low(first_grad * both[0:1, :HALF] + second_grad * both[1:2, :HALF])
+        for row, (prob, score) in enumerate(((first, first_grad), (second, second_grad))):
+            kv_grad[row : row + 1, :HALF] = jnp.sum(score * query_now, axis=0, keepdims=True)
+            kv_grad[row : row + 1, HALF:] = jnp.sum(prob * out_grad, axis=0, keepdims=True)
+
+    outs = [
+        ((TOKENS, C), f32),
+        ((TOKENS, HALF), bf16),
+        ((TOKENS, HALF), bf16),
+        ((8, WIDE), f32),
+        ((8, HALF), f32),
+    ]
+    operands = [mine, other, resid, gain, base, weight, query, context]
+    return one_step(body, info, table, operands, outs, 2 * TOKENS * C * 14 * HALF)
+
+
+def self_back(info, table, mine, other, query_weight, resid, gain, base, weight, packed, qkv):
+    def body(info_ref, mine_ref, other_ref, qw_ref, resid_ref, gain_ref, base_ref, weight_ref, packed_ref, qkv_ref, *outs):
+        resid_out, o_low, packed_low, ln_out, sums = outs
+        side, limit = (info_ref[0], info_ref[2])
+        joined = two_sides(side, mine_ref[...], other_ref[...])
+        result = layer_back(
+            dot_t(joined, qw_ref[...]), resid_ref[...], gain_ref[0:1], base_ref[...], side, sums
+        )
+        resid_out[...] = result
+        result = low(result)
+        o_low[...] = side_of(side, result)
+        out_grad = low(dot_t(result, weight_ref[...]))
+        query, key = (packed_ref[:, 0:HALF], packed_ref[:, HALF : 2 * HALF])
+        value = packed_ref[:, 2 * HALF : 3 * HALF]
+        parts = [jnp.zeros((TOKENS, HALF), f32) for _ in range(3)]
+        for head in range(LOCAL_HEADS):
+            lanes = head_lanes(head)
+            probs = head_probs(query, key, head, limit)
+            mine_grad = jnp.where(lanes, out_grad, jnp.zeros((), bf16))
+            prob_grad = dot_t(mine_grad, value)
+            inner = jnp.sum(probs * prob_grad, axis=-1, keepdims=True)
+            score_grad = low(probs * (prob_grad - inner) * 0.125)
+            parts[0] = jnp.where(lanes, dot(score_grad, key), parts[0])
+            parts[1] = jnp.where(lanes, t_dot(score_grad, query), parts[1])
+            parts[2] = jnp.where(lanes, t_dot(low(probs), out_grad), parts[2])
+        joined = low(jnp.concatenate(parts, axis=1))
+        packed_low[...] = joined
+        ln_out[...] = dot_t(joined, qkv_ref[...])
+
+    outs = [
+        ((TOKENS, C), f32),
+        ((TOKENS, HALF), bf16),
+        ((TOKENS, 3 * HALF), bf16),
+        ((TOKENS, C), f32),
+        ((8, HALF), f32),
+    ]
+    operands = [mine, other, query_weight, resid, gain, base, weight, packed, qkv]
+    flops = 2 * TOKENS * C * 6 * HALF + 10 * LOCAL_HEADS * TOKENS * TOKENS * HALF
+    return one_step(body, info, table, operands, outs, flops)
+
+
+def token_back(info, table, mine, other, resid, gain, base, weight, normed, rows, gain_three, state):
+    def body(info_ref, mine_ref, other_ref, resid_ref, gain_ref, base_ref, weight_ref, normed_ref, inv_ref, g3_ref, state_ref, *outs):
+        pin_low, state_out, conv_low, sums, sums_three = outs
+        side, limit = (info_ref[0], info_ref[2])
+        result = layer_back(
+            mine_ref[...] + other_ref[...], resid_ref[...], gain_ref[0:1], base_ref[...], side, sums
+        )
+        result = low(result)
+        pin_low[...] = side_of(side, result)
+        token_grad = dot_t(result, weight_ref[...])
+        mask = token_mask(limit)
+        norm_grad, gain_grad, bias_grad = norm_back(
+            token_grad, normed_ref[...], inv_ref[0:1], mask, limit, g3_ref[0:1]
+        )
+        state_now = state_ref[...] + norm_grad
+        state_out[...] = state_now
+        conv_grad = mask * state_now
+        low_grad = low(conv_grad)
+        conv_low[...] = low_grad
+        sums_three[0:1] = jnp.sum(conv_grad, axis=0, keepdims=True)
+        sums_three[1:2] = gain_grad
+        sums_three[2:3] = bias_grad
+        sums_three[3:4] = column_squares(low_grad)
+
+    outs = [
+        ((TOKENS, HALF), bf16),
+        ((TOKENS, HALF), f32),
+        ((TOKENS, HALF), bf16),
+        ((8, HALF), f32),
+        ((8, HALF), f32),
+    ]
+    operands = [mine, other, resid, gain, base, weight, normed, rows, gain_three, state]
+    return one_step(body, info, table, operands, outs, 2 * TOKENS * C * HALF)
+
+
+def channel_mix():
+    flat = lax.iota(jnp.int32, LC * C)[:, None]
+    split = lax.iota(jnp.int32, LC * C)[None]
+    return flat == LC * (split % C) + split // C
 
 
 def gather_small(place, value):
@@ -760,110 +1229,6 @@
     return jnp.concatenate(out, axis=1)
 
 
-def group_spread(channel_sums):
-    at = lax.iota(jnp.int32, HALF) // (C // GROUPS)
-    same = (at[:, None] == at[None, :]).astype(jnp.float32)
-    return jnp.dot(channel_sums, same, precision=lax.Precision.HIGHEST)
-
-
-def group_backward(gradient, normed, inv_std, mask, denominator, gain_vec):
-    scaled = gradient * gain_vec
-    sums = group_spread(
-        jnp.stack([jnp.sum(scaled * mask, axis=0), jnp.sum(scaled * normed * mask, axis=0)])
-    )
-    input_grad = mask * inv_std * (
-        scaled - sums[0:1] / denominator - normed * (sums[1:2] / denominator)
-    )
-    return (input_grad, jnp.sum(gradient * normed, axis=0), jnp.sum(gradient, axis=0))
-
-
-def layer_forward(values, gain_vec, bias_vec):
-    mean_val = jnp.mean(values, axis=-1, keepdims=True)
-    centered = values - mean_val
-    var_val = jnp.mean(centered * centered, axis=-1, keepdims=True)
-    inv_std = lax.rsqrt(var_val + eps_layer)
-    normed = centered * inv_std
-    return (low(normed * gain_vec + bias_vec), normed, inv_std)
-
-
-def layer_backward(gradient, normed, inv_std, gain_vec):
-    scaled = gradient * gain_vec
-    first = jnp.mean(scaled, axis=-1, keepdims=True)
-    second = jnp.mean(scaled * normed, axis=-1, keepdims=True)
-    input_grad = inv_std * (scaled - first - normed * second)
-    return (input_grad, jnp.sum(gradient * normed, axis=0), jnp.sum(gradient, axis=0))
-
-
-def heads_of(value):
-    return value.reshape(value.shape[0], LOCAL_HEADS, DHEAD)
-
-
-def head_scores(query, key, key_mask):
-    scores = jnp.einsum("qhd,khd->hqk", query, key, preferred_element_type=jnp.float32) * 0.125
-    return jnp.where(key_mask, scores, -1e30)
-
-
-def attend(query, key, value, key_mask):
-    scores = head_scores(query, key, key_mask)
-    row_max = jnp.max(scores, axis=-1, keepdims=True)
-    exponent = jnp.exp(scores - row_max)
-    totals = jnp.sum(exponent, axis=-1, keepdims=True)
-    out = jnp.einsum(
-        "hqk,khd->qhd", low(exponent / totals), value, preferred_element_type=jnp.float32
-    )
-    return (low(out).reshape(TOKENS, HALF), row_max + jnp.log(totals))
-
-
-def attend_back(query, key, value, key_mask, log_total, out_grad):
-    probs = jnp.exp(head_scores(query, key, key_mask) - log_total)
-    prob_grad = jnp.einsum("qhd,khd->hqk", out_grad, value, preferred_element_type=jnp.float32)
-    inner = jnp.sum(probs * prob_grad, axis=-1, keepdims=True)
-    score_grad = low(probs * (prob_grad - inner) * 0.125)
-    query_grad = jnp.einsum("hqk,khd->qhd", score_grad, key, preferred_element_type=jnp.float32)
-    key_grad = jnp.einsum("hqk,qhd->khd", score_grad, query, preferred_element_type=jnp.float32)
-    value_grad = jnp.einsum(
-        "hqk,qhd->khd", low(probs), out_grad, preferred_element_type=jnp.float32
-    )
-    return low(
-        jnp.concatenate(
-            [part.reshape(TOKENS, HALF) for part in (query_grad, key_grad, value_grad)], axis=1
-        )
-    )
-
-
-def cross_split(context_kv):
-    return (
-        context_kv[:, :HALF].reshape(2, LOCAL_HEADS, DHEAD),
-        context_kv[:, HALF:].reshape(2, LOCAL_HEADS, DHEAD),
-    )
-
-
-def cross_attend(query, context_kv):
-    key, value = cross_split(context_kv)
-    scores = jnp.einsum("thd,jhd->thj", query, key, preferred_element_type=jnp.float32) * 0.125
-    probs = jax.nn.softmax(scores, axis=-1)
-    out = jnp.einsum("thj,jhd->thd", probs, value.astype(jnp.float32))
-    return (probs, low(out).reshape(TOKENS, HALF))
-
-
-def cross_back(query, context_kv, probs, out_grad):
-    key, value = cross_split(context_kv)
-    prob_grad = jnp.einsum("thd,jhd->thj", out_grad, value, preferred_element_type=jnp.float32)
-    score_grad = probs * (prob_grad - jnp.sum(probs * prob_grad, axis=-1, keepdims=True)) * 0.125
-    query_grad = jnp.einsum("thj,jhd->thd", score_grad, key.astype(jnp.float32))
-    key_grad = jnp.einsum("thj,thd->jhd", score_grad, query.astype(jnp.float32))
-    value_grad = jnp.einsum("thj,thd->jhd", probs, out_grad.astype(jnp.float32))
-    return (
-        query_grad.reshape(TOKENS, HALF),
-        jnp.concatenate([key_grad.reshape(2, HALF), value_grad.reshape(2, HALF)], axis=1),
-    )
-
-
-def own_columns(place, weight):
-    split = weight.reshape(weight.shape[0], -1, 2, HALF)
-    return pick(split, place.side, 2).reshape(weight.shape[0], -1)
-
-
 def frame_of(place, latents, target_noise, turned):
     both = jnp.concatenate([latents, target_noise], axis=-1)
     stride, joined = (1, both[None])
@@ -882,221 +1247,250 @@
     return jnp.where(turned, landscape, portrait).reshape(TOKENS, 2 * LC)
 
 
-def train_step(place, store, table, mats, vecs, latents, target_noise, label, step_value, orient, extent):
-    bias_grads = {}
-    half, full = (place.half, place.full)
+def train_step(place, store, table, vecs, latents, target_noise, label, step_value, orient, extent):
+    half, at = (place.half, store.places)
     turned = orient != 1
-    seen = lax.iota(jnp.int32, TOKENS) < extent * FRAME
-    mask = seen.astype(jnp.float32)[:, None]
-    denominator = (extent * FRAME * (C // GROUPS)).astype(jnp.float32)
+    info = jnp.stack([place.side, turned.astype(jnp.int32), extent * FRAME]).astype(jnp.int32)
+    mask = (lax.iota(jnp.int32, TOKENS) < extent * FRAME).astype(jnp.float32)[:, None]
     frame = frame_of(place, latents, target_noise, turned)
-    noise_img = frame[:, LC:]
     share = noise_level(step_value)
-    noisy = mask * (jnp.sqrt(share) * frame[:, :LC] + jnp.sqrt(1.0 - share) * noise_img)
-
+    noisy = mask * (jnp.sqrt(share) * frame[:, :LC] + jnp.sqrt(1.0 - share) * frame[:, LC:])
+    pad_in = windows(low(noisy), turned, 1)
+    noise_rows = jnp.pad(frame[:, LC:].T, ((0, OUT_ROWS - LC), (0, 0)))
     embed_in = low(time_embed(step_value))[None]
-    pre_one = dot(embed_in, mats["w_t1"]) + vecs["b_t1"]
+    mix = channel_mix()
+    row = lambda *names: jnp.stack([vecs[name] for name in names])
+    side_rows = lambda *names: half(row(*names))
+
+    def part(name, depth=C, **kind):
+        return Rows(at[name], depth, **kind)
+
+    def own_rows(name):
+        return Rows(at[name], HALF, side_rows=True)
+
+    w_t1 = unmix(info, table, at["w_t1"], TE, TD // WIDE, C)
+    w_t2 = unmix(info, table, at["w_t2"], TD, TD // WIDE, C)
+    qkv = unmix(info, table, at["w_qkv"], C, 3, HALF)
+    ckv = unmix(info, table, at["w_ckv"], C, 2, HALF)
+    ff1 = unmix(info, table, at["w_ff1"], C, 2 * FFI // WIDE, HALF)
+    w_tp = table[at["w_tp"] : at["w_tp"] + TD]
+    w_in = half(table[at["w_in"] : at["w_in"] + 9 * LC])
+    w_out = dot(table[at["w_out"] : at["w_out"] + 9 * LC].reshape(9, LC * C), low(mix))
+    w_out = low(jnp.pad(w_out.reshape(9, LC, C), ((0, 0), (0, OUT_ROWS - LC), (0, 0))))
+    w_out = w_out.reshape(9 * OUT_ROWS, C)
+
+    pre_one = dot(embed_in, w_t1) + vecs["b_t1"]
     hidden_one = low(jax.nn.silu(pre_one))
-    pre_two = dot(hidden_one, mats["w_t2"]) + vecs["b_t2"]
+    pre_two = dot(hidden_one, w_t2) + vecs["b_t2"]
     hidden_two = low(jax.nn.silu(pre_two))
-    time_vec = dot(hidden_two, mats["w_tp"]) + vecs["b_tp"]
-    class_vec = lax.dynamic_slice(mats["table"], (label, 0), (1, C)).astype(jnp.float32)
-
-    info = jnp.stack([place.side, turned.astype(jnp.int32), extent * FRAME]).astype(jnp.int32)
-    side_row = lambda name: half(vecs[name])[None]
-    stack = lambda *rows: jnp.concatenate(rows, axis=0)
-    at = store.places
-    pad_in = windows(low(noisy), turned, 1)
+    time_vec = dot(hidden_two, w_tp) + vecs["b_tp"]
+    class_vec = lax.dynamic_slice(table, (at["table"] + label, 0), (1, C)).astype(jnp.float32)
+    context = low(jnp.concatenate([class_vec, time_vec], axis=0))
+    context_kv = jnp.pad(low(dot(context, ckv)), ((0, 6), (0, 0)))
+
     act_one, normed_one, inv_one, state_zero = first_forward(
-        info,
-        pad_in,
-        half(mats["w_in"]),
-        stack(side_row("b_in"), side_row("g1"), side_row("bb1")),
+        info, pad_in, w_in, side_rows("b_in", "g1", "bb1")
     )
     act_one_peer = place.swap(act_one)
+    rows_two = side_rows("b_c1", "g2", "bb2")
+    rows_two = jnp.concatenate([rows_two[0:1] + half(time_vec), rows_two[1:]], axis=0)
     act_two, normed_two, inv_two = conv_forward(
-        info,
-        act_one,
-        act_one_peer,
-        table,
-        at["w_c1"],
-        None,
-        stack(side_row("b_c1") + half(time_vec), side_row("g2"), side_row("bb2")),
-        True,
+        info, act_one, act_one_peer, table, at["w_c1"], None, rows_two, True
     )
     act_two_peer = place.swap(act_two)
     token_own, normed_three, inv_three, state_one = conv_forward(
+        info, act_two, act_two_peer, table, at["w_c2"], state_zero, side_rows("b_c2", "g3", "bb3"), False
+    )
+    token_in, resid_zero, ln_one, packed, attended_own = self_front(
+        info, table, token_own, place.swap(token_own), part("w_pin"), row("b_pin", "n1g", "n1b"), qkv
+    )
+    attended, resid_one, ln_two, cross_query, cross_own = cross_front(
         info,
-        act_two,
-        act_two_peer,
         table,
-        at["w_c2"],
-        state_zero,
-        stack(side_row("b_c2"), side_row("g3"), side_row("bb3")),
-        False,
-    )
-    token_in = full(token_own)
-    resid_zero = dot(token_in, mats["w_pin"]) + vecs["b_pin"]
-    ln_one, normed_ln1, inv_ln1 = layer_forward(resid_zero, vecs["n1g"], vecs["n1b"])
-    qkv_own = own_columns(place, mats["w_qkv"])
-    packed = low(dot(ln_one, qkv_own))
-    query, key, value = [heads_of(packed[:, i * HALF : (i + 1) * HALF]) for i in range(3)]
-    attended_own, log_total = attend(query, key, value, seen)
-    attended = full(attended_own)
-    resid_one = resid_zero + dot(attended, mats["w_o"]) + vecs["b_o"]
-    ln_two, normed_ln2, inv_ln2 = layer_forward(resid_one, vecs["n2g"], vecs["n2b"])
-    cq_own = half(mats["w_cq"])
-    cross_query = heads_of(low(dot(ln_two, cq_own)))
-    context = low(jnp.concatenate([class_vec, time_vec], axis=0))
-    ckv_own = own_columns(place, mats["w_ckv"])
-    context_kv = low(dot(context, ckv_own))
-    cross_prob, cross_own = cross_attend(cross_query, context_kv)
-    cross_out = full(cross_own)
-    resid_two = resid_one + dot(cross_out, mats["w_co"]) + vecs["b_co"]
-    ln_three, normed_ln3, inv_ln3 = layer_forward(resid_two, vecs["n3g"], vecs["n3b"])
-    ff1_own = own_columns(place, mats["w_ff1"])
-    projected = dot(ln_three, ff1_own) + own_columns(place, vecs["b_ff1"][None])
-    wide = FFI // 2
-    lift, gate = (projected[:, :wide], projected[:, wide:])
-    cdf = 0.5 * (1.0 + lax.erf(gate * math.sqrt(0.5)))
-    gated_own = low(lift * gate * cdf)
-    gated_peer = place.swap(gated_own)
-    gated = jnp.concatenate(
-        [
-            place.join(gated_own[:, i * HALF : (i + 1) * HALF], gated_peer[:, i * HALF : (i + 1) * HALF])
-            for i in range(FFI // WIDE)
-        ],
-        axis=1,
-    )
-    resid_three = resid_two + dot(gated, mats["w_ff2"]) + vecs["b_ff2"]
-    out_in = low(resid_three)
-    branch = dot(out_in, half(mats["w_pout"])) + half(vecs["b_pout"])
-    state_two = state_one + mask * branch
-    pad_out = windows(full(low(state_two)), turned, 1)
-    predicted = dot(pad_out, mats["w_out"]) + vecs["b_out"]
-    residual_err = predicted - noise_img
-    loss = jnp.sum(mask * residual_err * residual_err)
-
-    out_grad = 2.0 * mask * residual_err
-    bias_grads["b_out"] = jnp.sum(out_grad, axis=0)
-    out_low = low(out_grad)
-    w_out_back = jnp.transpose(mats["w_out"].reshape(9, C, LC), (0, 2, 1)).reshape(9 * LC, C)
-    state_grad = dot(windows(out_low, turned, -1), w_out_back)
-    branch_grad = mask * state_grad
-    state_grad = half(state_grad)
-    bias_grads["b_pout"] = half(jnp.sum(branch_grad, axis=0))
-    grad_low = low(branch_grad)
-    store.add("w_pout", out_in, half(grad_low))
-    w_out_grad = half(t_dot(pad_out, out_low).reshape(9 * LC, C))
-    last = store.total - store.places["w_out"] - 9 * LC
-    store.put(store.places["w_out"], jnp.pad(w_out_grad, ((0, last), (0, 0))))
-    resid_grad = dot_t(grad_low, mats["w_pout"])
-    bias_grads["b_ff2"] = half(jnp.sum(resid_grad, axis=0))
-    grad_low = low(resid_grad)
-    store.add("w_ff2", gated, half(grad_low))
-    ff2_own = pick(mats["w_ff2"].reshape(-1, 2, HALF, C), place.side, 1).reshape(wide, C)
-    gated_grad = dot_t(grad_low, ff2_own)
-    density = jnp.exp(-0.5 * gate * gate) * (1.0 / math.sqrt(2.0 * math.pi))
-    proj_grad = jnp.concatenate(
-        [gated_grad * gate * cdf, gated_grad * lift * (cdf + gate * density)], axis=1
-    )
-    bias_grads["b_ff1"] = jnp.sum(proj_grad, axis=0)
-    grad_low = low(proj_grad)
-    store.add("w_ff1", ln_three, grad_low)
-    ln_grad = dot_t(grad_low, ff1_own)
-    ln_grad = ln_grad + place.swap(ln_grad)
-    ln_grad, gain, bias = layer_backward(ln_grad, normed_ln3, inv_ln3, vecs["n3g"])
-    bias_grads["n3g"], bias_grads["n3b"] = (half(gain), half(bias))
-    resid_grad = resid_grad + ln_grad
-    bias_grads["b_co"] = half(jnp.sum(resid_grad, axis=0))
-    grad_low = low(resid_grad)
-    store.add("w_co", cross_out, half(grad_low))
-    cross_grad = heads_of(low(dot_t(grad_low, half(mats["w_co"], 0))))
-    query_grad, kv_grad = cross_back(cross_query, context_kv, cross_prob, cross_grad)
-    query_low, kv_low = (low(query_grad), low(kv_grad))
+        attended_own,
+        place.swap(attended_own),
+        part("w_o"),
+        row("b_o", "n2g", "n2b"),
+        resid_zero,
+        part("w_cq", side_columns=True),
+        context_kv,
+    )
+    b_ff1 = half(vecs["b_ff1"].reshape(-1, WIDE)).reshape(1, FFI)
+    cross_out, resid_two, ln_three, projected, gated_own = ff_front(
+        info,
+        table,
+        cross_own,
+        place.swap(cross_own),
+        part("w_co"),
+        row("b_co", "n3g", "n3b"),
+        resid_one,
+        ff1,
+        b_ff1,
+    )
+    gated, out_in, state_own = ff_finish(
+        info,
+        table,
+        gated_own,
+        place.swap(gated_own),
+        part("w_ff2", FFI),
+        row("b_ff2"),
+        resid_two,
+        part("w_pout", side_columns=True),
+        side_rows("b_pout"),
+        state_one,
+    )
+    b_out = jnp.broadcast_to(jnp.pad(vecs["b_out"], (0, OUT_ROWS - LC))[:, None], (OUT_ROWS, 128))
+    (
+        w_out_grad,
+        small_out,
+        state_grad,
+        pout_low,
+        ff2_low,
+        resid_grad,
+        proj_low,
+        ln_part,
+        sums_out,
+        sums_ff,
+    ) = loss_back(
+        info,
+        table,
+        state_own,
+        place.swap(state_own),
+        w_out,
+        noise_rows,
+        b_out,
+        part("w_pout"),
+        part("w_ff2", FFI),
+        projected,
+        ff1,
+    )
+    ln_peer = place.swap(ln_part)
+    store.add("w_pout", out_in, pout_low)
+    store.add("w_ff2", gated, ff2_low)
+    store.add("w_ff1", ln_three, proj_low)
+    w_out_grad = w_out_grad.reshape(9, OUT_ROWS, C)[:, :LC].reshape(9, LC * C)
+    w_out_grad = lax.dot_general(
+        w_out_grad,
+        mix.astype(jnp.float32),
+        (((1,), (1,)), ((), ())),
+        precision=lax.Precision.HIGHEST,
+        preferred_element_type=jnp.float32,
+    )
+    w_out_grad = half(w_out_grad.reshape(9 * LC, C))
+    store.put(at["w_out"], jnp.zeros((store.total - at["w_out"], HALF), jnp.float32))
+    resid_grad, co_low, query_low, kv_grad, sums_co = cross_back(
+        info,
+        table,
+        ln_part,
+        ln_peer,
+        resid_two,
+        row("n3g"),
+        resid_grad,
+        own_rows("w_co"),
+        cross_query,
+        context_kv,
+    )
+    query_peer = place.swap(query_low)
+    kv_low = low(kv_grad[:2])
+    context_grad = dot_t(kv_low, ckv)
+    context_grad = context_grad + place.swap(context_grad)
+    store.add("w_co", cross_out, co_low)
     store.add("w_cq", ln_two, query_low)
     store.add("w_ckv", context, kv_low)
-    context_grad = dot_t(kv_low, ckv_own)
-    context_grad = context_grad + place.swap(context_grad)
-    ln_grad = dot_t(full(query_low), mats["w_cq"])
-    ln_grad, gain, bias = layer_backward(ln_grad, normed_ln2, inv_ln2, vecs["n2g"])
-    bias_grads["n2g"], bias_grads["n2b"] = (half(gain), half(bias))
-    resid_grad = resid_grad + ln_grad
-    bias_grads["b_o"] = half(jnp.sum(resid_grad, axis=0))
-    grad_low = low(resid_grad)
-    store.add("w_o", attended, half(grad_low))
-    attended_grad = heads_of(low(dot_t(grad_low, half(mats["w_o"], 0))))
-    packed_grad = attend_back(query, key, value, seen, log_total, attended_grad)
-    store.add("w_qkv", ln_one, packed_grad)
-    ln_grad = dot_t(packed_grad, qkv_own)
-    ln_grad = ln_grad + place.swap(ln_grad)
-    ln_grad, gain, bias = layer_backward(ln_grad, normed_ln1, inv_ln1, vecs["n1g"])
-    bias_grads["n1g"], bias_grads["n1b"] = (half(gain), half(bias))
-    resid_grad = resid_grad + ln_grad
-    bias_grads["b_pin"] = half(jnp.sum(resid_grad, axis=0))
-    grad_low = low(resid_grad)
-    store.add("w_pin", token_in, half(grad_low))
-    token_grad = dot_t(grad_low, half(mats["w_pin"], 0))
-    norm_grad, bias_grads["g3"], bias_grads["bb3"] = group_backward(
-        token_grad, normed_three, inv_three[0:1], mask, denominator, half(vecs["g3"])
-    )
-    state_grad = state_grad + norm_grad
-
-    conv_grad = mask * state_grad
-    bias_grads["b_c2"] = jnp.sum(conv_grad, axis=0)
-    conv_low = low(conv_grad)
-    c2_squares = column_squares(conv_low)
-    conv_low, sums = conv_backward(
+    resid_grad, o_low, packed_low, ln_part, sums_o = self_back(
+        info,
+        table,
+        query_low,
+        query_peer,
+        part("w_cq"),
+        resid_one,
+        row("n2g"),
+        resid_grad,
+        own_rows("w_o"),
+        packed,
+        qkv,
+    )
+    ln_peer = place.swap(ln_part)
+    store.add("w_o", attended, o_low)
+    store.add("w_qkv", ln_one, packed_low)
+    pin_low, state_grad, conv_low, sums_pin, sums_two = token_back(
+        info,
+        table,
+        ln_part,
+        ln_peer,
+        resid_zero,
+        row("n1g"),
+        resid_grad,
+        own_rows("w_pin"),
+        normed_three,
+        inv_three,
+        side_rows("g3"),
+        state_grad,
+    )
+    conv_peer = place.swap(conv_low)
+    store.add("w_pin", token_in, pin_low)
+    conv_low, sums_one = conv_backward(
         info,
         conv_low,
-        place.swap(conv_low),
+        conv_peer,
         act_two,
         act_two_peer,
         table,
         store,
         at["w_c2"],
         (normed_two, inv_two),
-        stack(side_row("g2"), side_row("bb2")),
+        side_rows("g2", "bb2"),
         None,
     )
-    conv_sum, bias_grads["g2"], bias_grads["bb2"] = (sums[0], sums[1], sums[2])
-    bias_grads["b_c1"] = conv_sum
-    time_grad = full(conv_sum[None]) + context_grad[1:2]
-    bias_grads["b_tp"] = half(time_grad[0])
+    conv_peer = place.swap(conv_low)
+    time_grad = place.full(sums_one[0:1]) + context_grad[1:2]
+    b_tp = half(time_grad)
     time_low = low(time_grad)
+    pre_grad = dot_t(time_low, w_tp) * silu_slope(pre_two)
+    b_t2 = half(pre_grad.reshape(-1, WIDE))
+    two_low = low(pre_grad)
+    pre_grad = dot_t(two_low, w_t2) * silu_slope(pre_one)
+    b_t1 = half(pre_grad.reshape(-1, WIDE))
+    one_low = low(pre_grad)
+    size = lambda one: jnp.max(jnp.abs(one.astype(jnp.float32)))
+    local = jnp.maximum(store.top[0, 0], size(context_grad[0]))
+    for left, right in ((hidden_two, time_low), (hidden_one, two_low), (embed_in, one_low)):
+        local = jnp.maximum(local, 1.01 * size(left) * size(right))
+    squares = [size(one) for one in (inv_one[1], inv_two[1], sums_two[3], sums_one[3])]
+    largest = Largest(place, lane_row([local] + squares))
     store.add("w_tp", hidden_two, half(time_low))
-    pre_grad = dot_t(time_low, mats["w_tp"]) * silu_slope(pre_two)
-    bias_grads["b_t2"] = own_columns(place, pre_grad)[0]
-    pre_low = low(pre_grad)
-    store.add("w_t2", hidden_one, own_columns(place, pre_low))
-    pre_grad = dot_t(pre_low, mats["w_t2"]) * silu_slope(pre_one)
-    bias_grads["b_t1"] = own_columns(place, pre_grad)[0]
-    store.add("w_t1", embed_in, own_columns(place, low(pre_grad)))
-    rows = lax.iota(jnp.int32, NCLS)[:, None] == label
-    store.put(store.places["table"], jnp.where(rows, half(context_grad[0:1]), 0.0))
-    store.put(0, jnp.zeros((store.places["w_t1"], HALF), jnp.float32))
-
-    squares = [jnp.max(rows_of).reshape(1, 1) for rows_of in (inv_one[1], inv_two[1], c2_squares, sums[3])]
-    tops = largest_of_all(place, jnp.concatenate([store.top] + squares, axis=1))[0]
-    bound = jnp.maximum(tops[0], 1.01 * jnp.sqrt(tops[1] * tops[4]))
-    bound = jnp.maximum(bound, 1.01 * jnp.sqrt(tops[2] * tops[3]))
-    scale = (WIRE_TOP / (place.count // 2)) / jnp.maximum(bound, 1e-30)
-    in_low, sums = conv_backward(
+    store.buffer = largest.exchange(store.buffer)
+    store.add("w_t2", hidden_one, half(two_low.reshape(-1, WIDE)).reshape(1, -1))
+    store.buffer = largest.exchange(store.buffer)
+    store.add("w_t1", embed_in, half(one_low.reshape(-1, WIDE)).reshape(1, -1))
+    chosen = lax.iota(jnp.int32, NCLS)[:, None] == label
+    store.put(at["table"], jnp.where(chosen, half(context_grad[0:1]), 0.0))
+    store.put(0, jnp.zeros((at["w_t1"], HALF), jnp.float32))
+    store.buffer = largest.exchange(store.buffer)
+    in_low, sums_in = conv_backward(
         info,
         conv_low,
-        place.swap(conv_low),
+        conv_peer,
         act_one,
         act_one_peer,
         table,
         store,
         at["w_c1"],
         (normed_one, inv_one),
-        stack(side_row("g1"), side_row("bb1")),
+        side_rows("g1", "bb1"),
         state_grad,
     )
-    bias_grads["b_in"], bias_grads["g1"], bias_grads["bb1"] = (sums[0], sums[1], sums[2])
+    store.buffer = largest.exchange(store.buffer)
+    tops = largest.finish()[0]
+    bound = jnp.maximum(tops[0], 1.01 * jnp.sqrt(tops[1] * tops[4]))
+    bound = jnp.maximum(bound, 1.01 * jnp.sqrt(tops[2] * tops[3]))
+    scale = (WIRE_TOP / (place.count // 2)) / jnp.maximum(bound, 1e-30)
     w_in_grad = t_dot(pad_in, in_low)
-    return (bias_grads, w_in_grad, scale, loss)
+    small = [b_t1, b_t2, b_tp, sums_in[:3], sums_one[:3], sums_two[:3], sums_pin[:3], sums_o[:3]]
+    small += [sums_co[:3], sums_ff, sums_out[:2]]
+    extra = [small_out[:LC, 0], small_out[0:1, 128], (extent * FRAME).astype(jnp.float32)[None]]
+    extra = jnp.pad(jnp.concatenate(extra), (0, HALF - LC - 2))[None]
+    return (jnp.concatenate(small + [extra, w_in_grad, w_out_grad], axis=0), scale)
 
 
 def adam_update(params, first_mom, second, gradient, decay_rate):
@@ -1131,13 +1525,6 @@
     rows = shard_rows(length * place.count, place.count)
     block = to_blocks(place, mat_params.astype(jnp.bfloat16), rows)
     table = lax.all_gather(block, ("dp", "rows"), axis=0, tiled=True)
-    mats, at = ({}, LEAD)
-    for name, depth, width in mat_layout():
-        count = depth * width // WIDE
-        mats[name] = table[at : at + count].reshape(depth, width)
-        if name == "w_in":
-            mats[name] = table[at : at + count]
-        at += count
     vec_len = vec_params.shape[0]
     vec_wide = -(-vec_len // 128) * 128
     padded = jnp.pad(vec_params, (0, vec_wide - vec_len)).reshape(-1, 128)
@@ -1146,11 +1533,10 @@
     vecs = unpack(vec_all, vec_layout())
     own = lambda values: pick(values, place.slot, 0)
     store = Store(place, rows)
-    bias_grads, w_in_grad, scale, loss = train_step(
+    small, scale = train_step(
         place,
         store,
         table,
-        mats,
         vecs,
         latents,
         target_noise,
@@ -1159,27 +1545,26 @@
         own(orient),
         own(extent),
     )
-    small = [bias_grads[record[0]].reshape(-1, HALF) for record in vec_layout()[:-1]]
-    count_local = (own(extent) * FRAME).astype(jnp.float32)
-    extra = jnp.concatenate([bias_grads["b_out"], jnp.stack([loss, count_local])])
-    extra = jnp.pad(extra, (0, HALF - LC - 2))[None]
-    small = jnp.concatenate(small + [extra, w_in_grad], axis=0)
+    block_grad, square = scatter_sum(place, store.buffer, scale, rows)
     small = jnp.pad(small, ((0, -small.shape[0] % 8), (0, 0)))
+    body = sum(record[1] for record in vec_layout()[:-1]) // WIDE
+    lane = lax.broadcasted_iota(jnp.int32, small.shape, 1)
+    line = lax.broadcasted_iota(jnp.int32, small.shape, 0)
+    small = jnp.where((lane == SQUARE_AT) & (line == body), square, small)
     small = place.full(place.chip_sum(small))
-    body = sum(record[1] for record in vec_layout()[:-1]) // WIDE
     loss_sum, pixel_count = (small[body, LC], small[body, LC + 1])
-    w_in_sum = small[body + 1 : body + 1 + 9 * LC]
     vec_flat = jnp.concatenate([small[:body].reshape(-1), small[body, :LC]])
     vec_flat = jnp.pad(vec_flat, (0, vec_len * place.count - vec_flat.shape[0]))
     shard_vec = lax.dynamic_slice(vec_flat, (vec_len * place.index,), (vec_len,))
-
-    block_grad = scatter_sum(place, store.buffer, scale, rows)
-    held = jnp.where(place.index == 0, w_in_sum, block_grad[LEAD : LEAD + 9 * LC])
-    block_grad = lax.dynamic_update_slice(block_grad, held, (LEAD, 0))
+    square = small[body, SQUARE_AT] + small[body, HALF + SQUARE_AT] + jnp.sum(vec_flat * vec_flat)
     shard_mat = from_blocks(place, block_grad, length)
-    square = jnp.sum(block_grad * block_grad).reshape(1, 1)
-    square = place.chip_sum(square + place.swap(square))[0, 0]
-    square = square + jnp.sum(vec_flat * vec_flat)
+    for i, name in enumerate(("w_in", "w_out")):
+        values = small[body + 1 + 9 * LC * i : body + 1 + 9 * LC * (i + 1)]
+        square = square + jnp.sum(values * values)
+        owner, offset = divmod((store.places[name] - LEAD) * WIDE, length)
+        old = lax.dynamic_slice(shard_mat, (offset,), (9 * LC * C,))
+        new = jnp.where(place.index == owner, values.reshape(-1), old)
+        shard_mat = lax.dynamic_update_slice(shard_mat, new, (offset,))
     inverse = 1.0 / pixel_count
     grad_norm = jnp.sqrt(square) * inverse
     factor = clip_norm / jnp.maximum(grad_norm, clip_norm) * inverse

time: 697 us -> 630 us (0.904)
  matrix products: 65.9 us -> 10.3 us
  Pallas kernels: 63.5 us -> 112 us
  local copies, waits for them, and re-layouts: 103 us -> 56.6 us
  starting transfers between devices: 87.2 us -> 72.4 us
  waiting for transfers between devices: 232 us -> 243 us
    pallas_call x0 -> x13, Pallas kernels: none -> 60.4 us  [the longest x8 48 us: one_step(): pl.pallas_call(body, grid_spec=pltpu.PrefetchScalarGridSpec(num_scalar_pr...]
    dot_general x13 -> x1, matrix products: 25.6 us -> 4.22 us  [train_step(): lax.dot_general(w_out_grad, mix.astype(jnp.float32), (((1,), (1,)), ((),...]
    dot_general x11 -> x3, matrix products: 19.3 us -> 2.46 us  [dot_t(): lax.dot_general(left, right, (((1,), (1,)), ((), ())), preferred_element_...]
    ppermute x60 -> x55, starting transfers between devices: 87.2 us -> 72.4 us  [move(): return lax.ppermute(value, ('dp', 'rows'), pairs)]
    dot_general x14 -> x5, matrix products: 18 us -> 3.52 us  [dot(): return jnp.dot(left, right, preferred_element_type=jnp.float32)]
    reshape x19 -> x10, local copies, waits for them, and re-layouts: 14.4 us -> 0.88 us  [the longest x1 0.78 us: train_step(): table[at['w_out']:at['w_out'] + 9 * LC].reshape(9, LC * C)]
    reduce_sum x15 -> x5, other arithmetic: 13.8 us -> 3.57 us  [the longest x3 2.33 us: scatter_sum(): square = sum((jnp.sum(part * part) for part in parts)).reshape(1, 1)]
    slice x24 -> x15, local copies, waits for them, and re-layouts: 13.5 us -> 4.71 us  [the longest x1 1.41 us: train_step(): table[at['w_out']:at['w_out'] + 9 * LC].reshape(9, LC * C)]
  transfers between devices with their start and end apart: 61 -> 56, of which waited for: 29 -> 27; matrix products, arithmetic and copies ran while one was open for 20% -> 16% of each run, Pallas kernels for 5% -> 6%
where the time goes in v2:
time: 630 us; the launch traced here: 620 us
  waiting for transfers between devices  243 us (39%)
  Pallas kernels  112 us (18%)
  other arithmetic  84.1 us (13%)
  starting transfers between devices  72.4 us (11%)
  local copies, waits for them, and re-layouts  56.6 us (9%)
  between operations  41.6 us (7%)
  matrix products  10.3 us (2%)
    all_gather x1, waiting for transfers between devices, local(): table = lax.all_gather(block, ('dp', 'rows'), axis=0, tiled=True)  136 us
    ppermute x55, waiting for transfers between devices, move(): return lax.ppermute(value, ('dp', 'rows'), pairs)  107 us
    ppermute x55, starting transfers between devices, move(): return lax.ppermute(value, ('dp', 'rows'), pairs)  72.4 us
    pallas_call x8, Pallas kernels, one_step(): pl.pallas_call(body, grid_spec=pltpu.PrefetchScalarGridSpec(num_scalar_pr...  48 us
    convert_element_type x15, other arithmetic, wire(): return values.astype(jnp.float16)  29.7 us
    unnamed x233, local copies, waits for them, and re-layouts  28.4 us
    pallas_call x12, Pallas kernels, grad_into(): pl.pallas_call(body, grid=(tiles,), in_specs=old_specs + [pl.BlockSpec((t...  21.7 us
    pallas_call x2, Pallas kernels, conv_backward(): pl.pallas_call(body, grid_spec=pltpu.PrefetchScalarGridSpec(num_scalar_pr...  17.5 us
  transfers between devices with their start and end apart: 56, of which 27 were waited for; matrix products, arithmetic and copies ran while one was open for 16% of the time, Pallas kernels for 6%

profile of v2, /device:TPU:4, one launch (start us, length us, event | category | flops | bytes accessed | tf_op | source)
XLA Modules:
  0.0 620.3 jit_solution(4158083704892770445)
XLA Ops:
  11.5 3.5 collective-permute-done.2
  15.0 5.3 concatenate.173
  29.6 3.3 collective-permute-start.4
  34.6 3.7 collective-permute-done.5
  48.2 136.0 %all-gather.2.cloned.1.call-done.rows_ref.weight_ref.qw_ref.ow_ref.refs_5_.refs_6_.refs_7_ = bf16[25344,512]{1,0:T(8,128)(2,1)} async-done(((bf16[792,512]{1,0:T(8,128)(2,1)}), bf16[25344,512]{1,0:T(8,128)(2,1)}) %all-gather.2.cloned.1.call-update) | async-done | bytes 25952272 | tf_op jit(solution)/shard_map/all_gather | solution.py:1527
  186.8 3.3 shard_map.223
  199.1 5.5 shard_map.224
  207.8 5.5 shard_map.225
  218.2 4.8 shard_map.227
  226.2 4.2 shard_map.229
  234.0 3.5 shard_map.230.fw_ref.refs_8_
  238.9 6.5 %shard_map.231 = (bf16[512,512]{1,0:T(8,128)(2,1)S(1)}, f32[512,512]{1,0:T(8,128)S(1)}, bf16[512,512]{1,0:T(8,128)(2,1)S(1)}, f32[512,2048]{1,0:T(8,128)}, bf16[512,1024]{1,0:T(8,128)(2,1)S(1)}) custom-call(s32[3]{0:T(128)S(1)} %pad_add_fusion.info_ref, bf16[512,256]{1,0:T(8,128)(2,1)S(1)} %get-tuple-element.106.mine_ref, ...), custom_call_target="tpu_custom_call" | custom-call | flops 1342177280 | bytes 14680064 | tf_op jit(solution)/shard_map/pallas_call | solution.py:815
  248.3 3.2 iota_compare_fusion.1
  254.2 4.9 shard_map.232
  260.8 8.7 %shard_map.233 = (f32[72,512]{1,0:T(8,128)S(1)}, f32[8,256]{1,0:T(8,128)S(1)}, f32[512,256]{1,0:T(8,128)S(1)}, bf16[512,256]{1,0:T(8,128)(2,1)S(1)}, bf16[512,25...) custom-call(s32[3]{0:T(128)S(1)} %pad_add_fusion.info_ref, ...), custom_call_target="tpu_custom_call" | custom-call | flops 1879048192 | bytes 10829824 | tf_op jit(solution)/shard_map/pallas_call | solution.py:815
  276.5 5.2 shard_map.237
  288.7 9.3 %shard_map.241 = (f32[512,512]{1,0:T(8,128)}, bf16[512,256]{1,0:T(8,128)(2,1)S(1)}, bf16[512,768]{1,0:T(8,128)(2,1)S(1)}, f32[512,512]{1,0:T(8,128)}, f32[8,256]{1,0:T(8,128)S(1)}) custom-call(s32[3]{0:T(128)S(1)} %pad_add_fusion.info_ref, bf16[512,256]{1,0:T(8,128)(2,1)S(1)} %copy-done.16, bf16[512,256]{1,0:T(8,128)(2,1)S(1)} %copy-done.58, ...), custom_call_target="tpu_custom_call" | custom-call | flops 3489660928 | bytes 6307840 | tf_op jit(solution)/shard_map/pallas_call | solution.py:815
  310.8 2.9 shard_map.235
  314.4 4.1 shard_map.236
  319.9 4.4 shard_map.244
  337.0 8.8 %shard_map.246 = (f32[25344,256]{1,0:T(8,128)}, bf16[512,256]{1,0:T(8,128)(2,1)S(1)}, f32[8,256]{1,0:T(8,128)S(1)}) custom-call(s32[3]{0:T(128)S(1)} %pad_add_fusion.info_ref, f32[25344,256]{1,0:T(8,128)} %get-tuple-element.148.refs_0_, bf16[512,256]{1,0:T(8,128)(2,1)S(1)} %get-tuple-element.149.refs_1_, ...), custom_call_target="tpu_custom_call", output_to_operand_aliasing={{0}: (1, {})} | custom-call | flops 2415919104 | bytes 10223616 | tf_op jit(solution)/shard_map/pallas_call | solution.py:701
  374.6 8.7 %shard_map.250 = (f32[25344,256]{1,0:T(8,128)}, bf16[512,256]{1,0:T(8,128)(2,1)S(1)}, f32[8,256]{1,0:T(8,128)S(1)}) custom-call(s32[3]{0:T(128)S(1)} %pad_add_fusion.info_ref, f32[25344,256]{1,0:T(8,128)} %broadcast_dynamic-update-slice_fusion.1.refs_0_, bf16[512,256]{1,0:T(8,128)(2,1)S(1)} %get-tuple-element.174.refs_1_, ...), custom_call_target="tpu_custom_call", output_to_operand_aliasing={{0}: (1, {})} | custom-call | flops 2415919104 | bytes 10223616 | tf_op jit(solution)/shard_map/pallas_call | solution.py:701
  391.7 4.6 fusion.8
  397.2 3.2 fusion.28
  400.5 4.8 collective-permute-start.40
  405.3 6.8 %constant_dynamic-slice_fusion.11 = (f32[4,2,1,616,256]{4,3,2,1,0:T(8,128)S(1)}, f32[4,2,1,616,256]{4,3,2,1,0:T(8,128)}) fusion(f32[4,2,2,1584,256]{4,3,2,1,0:T(8,128)} %bitcast.241, s32[]{:T(128)S(6)} %select_n.523, s32[]{:T(128)S(6)} %select_n.468), kind=kLoop, calls=%fused_computation.156 | loop fusion | bytes 20185096 | tf_op jit(solution)/shard_map/dynamic_slice | solution.py:312
  413.6 4.2 collective-permute-done.40
  420.5 5.5 collective-permute-start.41
  431.9 4.2 fusion
  437.4 3.7 fusion.16
  442.7 9.0 %collective-permute-done.32 = f16[4,2,616,256]{3,2,1,0:T(8,128)(2,1)S(1)} collective-permute-done((f16[4,2,616,256]{3,2,1,0:T(8,128)(2,1)}, f16[4,2,616,256]{3,2,1,0:T(8,128)(2,1)S(1)}, u32[]{:S(2)}, u32[]{:S(2)}) %collective-permute-start.32) | collective-permute-done | bytes 2523168 | tf_op jit(solution)/shard_map/ppermute | solution.py:171
  451.7 5.2 fusion.2
  459.6 3.7 collective-permute-start.33
  470.6 7.3 %collective-permute-done.33 = f16[2,616,256]{2,1,0:T(8,128)(2,1)S(1)} collective-permute-done((f16[2,616,256]{2,1,0:T(8,128)(2,1)S(1)}, f16[2,616,256]{2,1,0:T(8,128)(2,1)S(1)}, u32[]{:S(2)}, u32[]{:S(2)}) %collective-permute-start.33) | collective-permute-done | bytes 630816 | tf_op jit(solution)/shard_map/ppermute | solution.py:171
  479.4 4.4 collective-permute-start.34
  483.9 3.8 fusion.5
  489.7 13.5 %collective-permute-done.34 = f16[2,616,256]{2,1,0:T(8,128)(2,1)S(1)} collective-permute-done((f16[2,616,256]{2,1,0:T(8,128)(2,1)S(1)}, f16[2,616,256]{2,1,0:T(8,128)(2,1)S(1)}, u32[]{:S(2)}, u32[]{:S(2)}) %collective-permute-start.34) | collective-permute-done | bytes 630816 | tf_op jit(solution)/shard_map/ppermute | solution.py:171
  503.2 3.1 fusion.22
  511.7 4.2 collective-permute-start.35
  523.1 6.8 %collective-permute-start.29 = (f16[616,256]{1,0:T(8,128)(2,1)S(1)}, f16[616,256]{1,0:T(8,128)(2,1)S(1)}, u32[]{:S(2)}, u32[]{:S(2)}) collective-permute-start(f16[616,256]{1,0:T(8,128)(2,1)S(1)} %get-tuple-element.241), channel_id=1, source_target_pairs={{0,8},{1,9},{2,10},{3,11},{4,12},{5,13},{6,14},{7,15},{8,16},{9,17... | collective-permute-start | bytes 946184 | tf_op jit(solution)/shard_map/ppermute | solution.py:171
  533.6 12.6 %collective-permute-done.38 = f16[2,616,256]{2,1,0:T(8,128)(2,1)S(1)} collective-permute-done((f16[2,616,256]{2,1,0:T(8,128)(2,1)S(1)}, f16[2,616,256]{2,1,0:T(8,128)(2,1)S(1)}, u32[]{:S(2)}, u32[]{:S(2)}) %collective-permute-start.38) | collective-permute-done | bytes 630816 | tf_op jit(solution)/shard_map/ppermute | solution.py:171
  551.9 13.6 %collective-permute-done.30 = f16[616,256]{1,0:T(8,128)(2,1)S(1)} collective-permute-done((f16[616,256]{1,0:T(8,128)(2,1)S(1)}, f16[616,256]{1,0:T(8,128)(2,1)S(1)}, u32[]{:S(2)}, u32[]{:S(2)}) %collective-permute-start.30) | collective-permute-done | bytes 315424 | tf_op jit(solution)/shard_map/ppermute | solution.py:171
  569.3 4.5 collective-permute-done.50
  574.1 4.4 collective-permute-done.51
  578.6 4.5 collective-permute-done.52
  583.3 5.7 collective-permute-done.53
  601.8 4.3 collective-permute-done.49
  608.0 3.8 multiply_add_fusion
  (535 shorter events, 181.9 us)
Async XLA Ops:
  7.2 177.0 %all-gather.2.cloned.1.call-start = ((), (), s32[]{:S(2)}) async-start(), calls=%async_computation | async-start | bytes 26763264 | tf_op jit(solution)/shard_map/all_gather | solution.py:1527
  8.8 6.3 %collective-permute-start.2 = (bf16[113664]{0:T(1024)(128)(2,1)S(1)}, bf16[113664]{0:T(1024)(128)(2,1)S(1)}, u32[]{:S(2)}, u32[]{:S(2)}) collective-permute-start(bf16[113664]{0:T(1024)(128)(2,1)S(1)} %slice.333), channel_id=1, source_target_pairs={{1,0},{2,1},{3,2},{4,3},{5,4},{6,5},{7,6},{8,7},{9,8},{10,9},{11,1... | collective-permute-start | bytes 681992 | tf_op jit(solution)/shard_map/ppermute | solution.py:171
  22.3 7.2 %collective-permute-start.3 = (bf16[1,5,128]{2,0,1:T(2,128)(2,1)S(1)}, bf16[1,5,128]{2,0,1:T(2,128)(2,1)S(1)}, u32[]{:S(2)}, u32[]{:S(2)}) collective-permute-start(bf16[1,5,128]{2,0,1:T(2,128)(2,1)S(1)} %broadcast_in_dim_reshape.3), channel_id=1, source_target_pairs={{0,1},{1,0},{2,3},{3,2},{4,5},{5,4},{6,7},{7,6},{8,9},{9,8},{10,11... | collective-permute-start | bytes 3848 | tf_op jit(solution)/shard_map/ppermute | solution.py:171
  23.3 16.6 %collective-permute-start = (f32[1,2,8,32,6]{3,2,0,4,1:T(8,128)S(1)}, f32[1,2,8,32,6]{3,2,0,4,1:T(8,128)S(1)}, u32[]{:S(2)}, u32[]{:S(2)}) collective-permute-start(f32[1,2,8,32,6]{3,2,0,4,1:T(8,128)S(1)} %maximum_bitcast_fusion), channel_id=1, source_target_pairs={{0,1},{1,0},{2,3},{3,2},{4,5},{5,4},{6,7},{7,6},{8,9},{9,8},{10,11... | collective-permute-start | bytes 36872 | tf_op jit(solution)/shard_map/ppermute | solution.py:171
  29.6 4.9 collective-permute-start.4
  34.5 3.8 collective-permute-start.5
  38.3 4.0 collective-permute-start.6
  40.0 4.9 collective-permute-start.1
  42.3 5.7 collective-permute-start.7
  213.3 4.9 collective-permute-start.10
  233.7 5.2 collective-permute-start.12
  248.0 5.1 collective-permute-start.13
  273.8 2.7 collective-permute-start.15
  299.6 20.3 %collective-permute-start.17 = (f32[512,512]{1,0:T(8,128)}, f32[512,512]{1,0:T(8,128)}, u32[]{:S(2)}, u32[]{:S(2)}) collective-permute-start(f32[512,512]{1,0:T(8,128)} %get-tuple-element.142.mine_ref), channel_id=1, source_target_pairs={{0,1},{1,0},{2,3},{3,2},{4,5},{5,4},{6,7},{7,6},{8,9},{9,8},{10,11... | collective-permute-start | bytes 3145736 | tf_op jit(solution)/shard_map/ppermute | solution.py:171
  324.3 12.6 %collective-permute-start.18 = (bf16[512,256]{1,0:T(8,128)(2,1)S(1)}, bf16[512,256]{1,0:T(8,128)(2,1)S(1)}, u32[]{:S(2)}, u32[]{:S(2)}) collective-permute-start(bf16[512,256]{1,0:T(8,128)(2,1)S(1)} %get-tuple-element.149.refs_1_), channel_id=1, source_target_pairs={{0,1},{1,0},{2,3},{3,2},{4,5},{5,4},{6,7},{7,6},{8,9},{9,8},{10,11... | collective-permute-start | bytes 786440 | tf_op jit(solution)/shard_map/ppermute | solution.py:171
  324.9 6.2 collective-permute-start.19
  347.4 27.2 %collective-permute-start.25 = (bf16[512,256]{1,0:T(8,128)(2,1)S(1)}, bf16[512,256]{1,0:T(8,128)(2,1)S(1)}, u32[]{:S(2)}, u32[]{:S(2)}) collective-permute-start(bf16[512,256]{1,0:T(8,128)(2,1)S(1)} %get-tuple-element.174.refs_1_), channel_id=1, source_target_pairs={{0,1},{1,0},{2,3},{3,2},{4,5},{5,4},{6,7},{7,6},{8,9},{9,8},{10,11... | collective-permute-start | bytes 786440 | tf_op jit(solution)/shard_map/ppermute | solution.py:171
  364.2 3.6 collective-permute-start.22
  370.5 4.0 collective-permute-start.23
  374.5 8.7 %collective-permute-start.24 = (f32[1,128]{1,0:T(1,128)S(1)}, f32[1,128]{1,0:T(1,128)S(1)}, u32[]{:S(2)}, u32[]{:S(2)}) collective-permute-start(f32[1,128]{1,0:T(1,128)S(1)} %max.80), channel_id=1, source_target_pairs={{0,8},{1,9},{2,10},{3,11},{4,12},{5,13},{6,14},{7,15},{8,0},{9,1},... | collective-permute-start | bytes 1544 | tf_op jit(solution)/shard_map/ppermute | solution.py:171
  383.2 4.5 collective-permute-start.26
  396.3 55.4 %collective-permute-start.32 = (f16[4,2,616,256]{3,2,1,0:T(8,128)(2,1)}, f16[4,2,616,256]{3,2,1,0:T(8,128)(2,1)S(1)}, u32[]{:S(2)}, u32[]{:S(2)}) collective-permute-start(f16[4,2,616,256]{3,2,1,0:T(8,128)(2,1)} %fusion.8), channel_id=1, source_target_pairs={{0,4},{1,5},{2,6},{3,7},{4,0},{5,1},{6,2},{7,3},{8,12},{9,13},{10,... | collective-permute-start | bytes 7569416 | tf_op jit(solution)/shard_map/ppermute | solution.py:171
  400.5 17.4 %collective-permute-start.40 = (f16[2,2,352,256]{3,2,1,0:T(8,128)(2,1)}, f16[2,2,352,256]{3,2,1,0:T(8,128)(2,1)}, u32[]{:S(2)}, u32[]{:S(2)}) collective-permute-start(f16[2,2,352,256]{3,2,1,0:T(8,128)(2,1)} %get-tuple-element.233), channel_id=1, source_target_pairs={{0,8},{1,9},{2,10},{3,11},{4,12},{5,13},{6,14},{7,15}} | collective-permute-start | bytes 2162696 | tf_op jit(solution)/shard_map/ppermute | solution.py:171
  412.1 24.9 %collective-permute-start.43 = (f16[2,2,352,256]{3,2,1,0:T(8,128)(2,1)}, f16[2,2,352,256]{3,2,1,0:T(8,128)(2,1)}, u32[]{:S(2)}, u32[]{:S(2)}) collective-permute-start(f16[2,2,352,256]{3,2,1,0:T(8,128)(2,1)} %get-tuple-element.234), channel_id=1, source_target_pairs={{24,16},{25,17},{26,18},{27,19},{28,20},{29,21},{30,22},{31,23}} | collective-permute-start | bytes 2162696 | tf_op jit(solution)/shard_map/ppermute | solution.py:171
  420.5 16.9 %collective-permute-start.41 = (f16[2,2,352,256]{3,2,1,0:T(8,128)(2,1)}, f16[2,2,352,256]{3,2,1,0:T(8,128)(2,1)}, u32[]{:S(2)}, u32[]{:S(2)}) collective-permute-start(f16[2,2,352,256]{3,2,1,0:T(8,128)(2,1)} %fusion.15), channel_id=1, source_target_pairs={{0,8},{1,9},{2,10},{3,11},{4,12},{5,13},{6,14},{7,15},{8,16},{9,17... | collective-permute-start | bytes 2162696 | tf_op jit(solution)/shard_map/ppermute | solution.py:171
  428.1 55.8 %collective-permute-start.27 = (f16[4,2,616,256]{3,2,0,1:T(8,128)(2,1)}, f16[4,2,616,256]{3,2,0,1:T(8,128)(2,1)}, u32[]{:S(2)}, u32[]{:S(2)}) collective-permute-start(f16[4,2,616,256]{3,2,0,1:T(8,128)(2,1)} %fusion.9), channel_id=1, source_target_pairs={{0,2},{1,3},{2,0},{3,1},{4,6},{5,7},{6,4},{7,5},{8,10},{9,11},{10,... | collective-permute-start | bytes 7569416 | tf_op jit(solution)/shard_map/ppermute | solution.py:171
  441.2 25.6 %collective-permute-start.44 = (f16[2,2,352,256]{3,2,1,0:T(8,128)(2,1)}, f16[2,2,352,256]{3,2,1,0:T(8,128)(2,1)}, u32[]{:S(2)}, u32[]{:S(2)}) collective-permute-start(f16[2,2,352,256]{3,2,1,0:T(8,128)(2,1)} %get-tuple-element.232), channel_id=1, source_target_pairs={{16,8},{17,9},{18,10},{19,11},{20,12},{21,13},{22,14},{23,15},{24,... | collective-permute-start | bytes 2162696 | tf_op jit(solution)/shard_map/ppermute | solution.py:171
  459.6 18.3 %collective-permute-start.33 = (f16[2,616,256]{2,1,0:T(8,128)(2,1)S(1)}, f16[2,616,256]{2,1,0:T(8,128)(2,1)S(1)}, u32[]{:S(2)}, u32[]{:S(2)}) collective-permute-start(f16[2,616,256]{2,1,0:T(8,128)(2,1)S(1)} %get-tuple-element.239), channel_id=1, source_target_pairs={{0,8},{1,9},{2,10},{3,11},{4,12},{5,13},{6,14},{7,15}} | collective-permute-start | bytes 1892360 | tf_op jit(solution)/shard_map/ppermute | solution.py:171
  465.4 42.7 %collective-permute-start.42 = (f16[2,2,352,256]{3,2,1,0:T(8,128)(2,1)S(1)}, f16[2,2,352,256]{3,2,1,0:T(8,128)(2,1)S(1)}, u32[]{:S(2)}, u32[]{:S(2)}) collective-permute-start(f16[2,2,352,256]{3,2,1,0:T(8,128)(2,1)S(1)} %copy-done.73), channel_id=1, source_target_pairs={{0,8},{1,9},{2,10},{3,11},{4,12},{5,13},{6,14},{7,15},{8,16},{9,17... | collective-permute-start | bytes 2162696 | tf_op jit(solution)/shard_map/ppermute | solution.py:171
  468.6 39.5 %collective-permute-start.45 = (f16[2,2,352,256]{3,2,1,0:T(8,128)(2,1)S(1)}, f16[2,2,352,256]{3,2,1,0:T(8,128)(2,1)S(1)}, u32[]{:S(2)}, u32[]{:S(2)}) collective-permute-start(f16[2,2,352,256]{3,2,1,0:T(8,128)(2,1)S(1)} %fusion.14), channel_id=1, source_target_pairs={{8,0},{9,1},{10,2},{11,3},{12,4},{13,5},{14,6},{15,7},{16,8},{17,9... | collective-permute-start | bytes 2162696 | tf_op jit(solution)/shard_map/ppermute | solution.py:171
  469.9 19.8 %collective-permute-start.36 = (f16[2,616,256]{2,1,0:T(8,128)(2,1)}, f16[2,616,256]{2,1,0:T(8,128)(2,1)S(1)}, u32[]{:S(2)}, u32[]{:S(2)}) collective-permute-start(f16[2,616,256]{2,1,0:T(8,128)(2,1)} %get-tuple-element.240), channel_id=1, source_target_pairs={{24,16},{25,17},{26,18},{27,19},{28,20},{29,21},{30,22},{31,23}} | collective-permute-start | bytes 1892360 | tf_op jit(solution)/shard_map/ppermute | solution.py:171
  479.4 23.8 %collective-permute-start.34 = (f16[2,616,256]{2,1,0:T(8,128)(2,1)S(1)}, f16[2,616,256]{2,1,0:T(8,128)(2,1)S(1)}, u32[]{:S(2)}, u32[]{:S(2)}) collective-permute-start(f16[2,616,256]{2,1,0:T(8,128)(2,1)S(1)} %fusion.21), channel_id=1, source_target_pairs={{0,8},{1,9},{2,10},{3,11},{4,12},{5,13},{6,14},{7,15},{8,16},{9,17... | collective-permute-start | bytes 1892360 | tf_op jit(solution)/shard_map/ppermute | solution.py:171
  489.1 31.8 %collective-permute-start.28 = (f16[4,616,256]{2,1,0:T(8,128)(2,1)}, f16[4,616,256]{2,1,0:T(8,128)(2,1)S(1)}, u32[]{:S(2)}, u32[]{:S(2)}) collective-permute-start(f16[4,616,256]{2,1,0:T(8,128)(2,1)} %fusion.18), channel_id=1, source_target_pairs={{0,4},{1,5},{2,6},{3,7},{4,0},{5,1},{6,2},{7,3},{8,12},{9,13},{10,... | collective-permute-start | bytes 3784712 | tf_op jit(solution)/shard_map/ppermute | solution.py:171
  506.4 9.5 %collective-permute-start.37 = (f16[2,616,256]{2,1,0:T(8,128)(2,1)}, f16[2,616,256]{2,1,0:T(8,128)(2,1)}, u32[]{:S(2)}, u32[]{:S(2)}) collective-permute-start(f16[2,616,256]{2,1,0:T(8,128)(2,1)} %get-tuple-element.238), channel_id=1, source_target_pairs={{16,8},{17,9},{18,10},{19,11},{20,12},{21,13},{22,14},{23,15},{24,... | collective-permute-start | bytes 1892360 | tf_op jit(solution)/shard_map/ppermute | solution.py:171
  510.6 8.3 %collective-permute-start.46 = (f16[2,352,256]{2,1,0:T(8,128)(2,1)}, f16[2,352,256]{2,1,0:T(8,128)(2,1)S(1)}, u32[]{:S(2)}, u32[]{:S(2)}) collective-permute-start(f16[2,352,256]{2,1,0:T(8,128)(2,1)} %fusion.37), channel_id=1, source_target_pairs={{0,2},{1,3},{2,0},{3,1},{4,6},{5,7},{6,4},{7,5},{8,10},{9,11},{10,... | collective-permute-start | bytes 1081352 | tf_op jit(solution)/shard_map/ppermute | solution.py:171
  511.7 19.1 %collective-permute-start.35 = (f16[2,616,256]{2,1,0:T(8,128)(2,1)}, f16[2,616,256]{2,1,0:T(8,128)(2,1)S(1)}, u32[]{:S(2)}, u32[]{:S(2)}) collective-permute-start(f16[2,616,256]{2,1,0:T(8,128)(2,1)} %get-tuple-element.237), channel_id=1, source_target_pairs={{0,8},{1,9},{2,10},{3,11},{4,12},{5,13},{6,14},{7,15},{8,16},{9,17... | collective-permute-start | bytes 1892360 | tf_op jit(solution)/shard_map/ppermute | solution.py:171
  517.5 28.7 %collective-permute-start.38 = (f16[2,616,256]{2,1,0:T(8,128)(2,1)S(1)}, f16[2,616,256]{2,1,0:T(8,128)(2,1)S(1)}, u32[]{:S(2)}, u32[]{:S(2)}) collective-permute-start(f16[2,616,256]{2,1,0:T(8,128)(2,1)S(1)} %fusion.20), channel_id=1, source_target_pairs={{8,0},{9,1},{10,2},{11,3},{12,4},{13,5},{14,6},{15,7},{16,8},{17,9... | collective-permute-start | bytes 1892360 | tf_op jit(solution)/shard_map/ppermute | solution.py:171
  519.0 29.0 %collective-permute-start.47 = (f16[352,256]{1,0:T(8,128)(2,1)S(1)}, f16[352,256]{1,0:T(8,128)(2,1)S(1)}, u32[]{:S(2)}, u32[]{:S(2)}) collective-permute-start(f16[352,256]{1,0:T(8,128)(2,1)S(1)} %fusion.43), channel_id=1, source_target_pairs={{0,4},{1,5},{2,6},{3,7},{4,0},{5,1},{6,2},{7,3},{8,12},{9,13},{10,... | collective-permute-start | bytes 540680 | tf_op jit(solution)/shard_map/ppermute | solution.py:171
  523.1 26.7 %collective-permute-start.29 = (f16[616,256]{1,0:T(8,128)(2,1)S(1)}, f16[616,256]{1,0:T(8,128)(2,1)S(1)}, u32[]{:S(2)}, u32[]{:S(2)}) collective-permute-start(f16[616,256]{1,0:T(8,128)(2,1)S(1)} %get-tuple-element.241), channel_id=1, source_target_pairs={{0,8},{1,9},{2,10},{3,11},{4,12},{5,13},{6,14},{7,15},{8,16},{9,17... | collective-permute-start | bytes 946184 | tf_op jit(solution)/shard_map/ppermute | solution.py:171
  529.9 22.0 %collective-permute-start.31 = (f16[616,256]{1,0:T(8,128)(2,1)S(1)}, f16[616,256]{1,0:T(8,128)(2,1)S(1)}, u32[]{:S(2)}, u32[]{:S(2)}) collective-permute-start(f16[616,256]{1,0:T(8,128)(2,1)S(1)} %get-tuple-element.242), channel_id=1, source_target_pairs={{0,24},{1,25},{2,26},{3,27},{4,28},{5,29},{6,30},{7,31},{8,0},{9,1... | collective-permute-start | bytes 946184 | tf_op jit(solution)/shard_map/ppermute | solution.py:171
  530.7 34.8 %collective-permute-start.30 = (f16[616,256]{1,0:T(8,128)(2,1)S(1)}, f16[616,256]{1,0:T(8,128)(2,1)S(1)}, u32[]{:S(2)}, u32[]{:S(2)}) collective-permute-start(f16[616,256]{1,0:T(8,128)(2,1)S(1)} %get-tuple-element.243), channel_id=1, source_target_pairs={{0,16},{1,17},{2,18},{3,19},{4,20},{5,21},{6,22},{7,23},{8,24},{9,... | collective-permute-start | bytes 946184 | tf_op jit(solution)/shard_map/ppermute | solution.py:171
  547.9 18.5 %collective-permute-start.39 = (f16[616,256]{1,0:T(8,128)(2,1)S(1)}, f16[616,256]{1,0:T(8,128)(2,1)S(1)}, u32[]{:S(2)}, u32[]{:S(2)}) collective-permute-start(f16[616,256]{1,0:T(8,128)(2,1)S(1)} %fusion.42), channel_id=1, source_target_pairs={{0,2},{1,3},{2,0},{3,1},{4,6},{5,7},{6,4},{7,5},{8,10},{9,11},{10,... | collective-permute-start | bytes 946184 | tf_op jit(solution)/shard_map/ppermute | solution.py:171
  569.2 4.6 collective-permute-start.50
  573.9 4.6 collective-permute-start.51
  578.5 4.6 collective-permute-start.52
  583.1 5.9 collective-permute-start.53
  589.2 5.1 collective-permute-start.48
  595.6 10.5 %collective-permute-start.49 = (f32[109568]{0:T(1024)S(1)}, f32[109568]{0:T(1024)S(1)}, u32[]{:S(2)}, u32[]{:S(2)}) collective-permute-start(f32[109568]{0:T(1024)S(1)} %slice.302), channel_id=1, source_target_pairs={{0,1},{1,2},{2,3},{3,4},{4,5},{5,6},{6,7},{7,8},{8,9},{9,10},{10,1... | collective-permute-start | bytes 1314824 | tf_op jit(solution)/shard_map/ppermute | solution.py:171
  (119 other events, 1033.7 us)
Sparse Core Ops, SparseCore 0:
  22.4 161.7 all-gather.1

commit v3 on v2

--- a/solution.py
+++ b/solution.py
@@ -2,6 +2,8 @@
 
 import jax
 import jax.numpy as jnp
+import ml_dtypes
+import numpy as np
 from jax import lax
 from jax.experimental import pallas as pl
 from jax.experimental.pallas import tpu as pltpu
@@ -269,14 +271,6 @@
     return values.astype(jnp.float32)
 
 
-def lane_row(values):
-    lane = lax.broadcasted_iota(jnp.int32, (1, 128), 1)
-    row = jnp.zeros((1, 128), jnp.float32)
-    for i, value in enumerate(values):
-        row = jnp.where(lane == i, value, row)
-    return row
-
-
 SQUARE_AT = 8
 
 
@@ -289,7 +283,7 @@
             got = self.place.swap(self.values, self.stride)
             if beside is not None:
                 got, beside = lax.optimization_barrier((got, beside))
-            self.values = jnp.maximum(self.values, got)
+            self.values = lax.optimization_barrier(jnp.maximum(self.values, got))
             self.stride *= 2
         return beside
 
@@ -316,7 +310,7 @@
         dim = left.index(axis)
         me, size = (place.coords[axis], place.digits[axis])
         total = part_of(dim, me)
-        if size == 2 or axis == order[-1]:
+        if size == 2 or axis != order[0]:
             for away in range(1, size):
                 sent = wire(part_of(dim, (me + away) % size))
                 total = total + plain(place.rotate(sent, axis, away))
@@ -337,7 +331,7 @@
     return held
 
 
-SHARES = (0.39, 0.39)
+SHARES = (0.42, 0.33)
 
 
 def scatter_sum(place, grads, scale, rows):
@@ -1075,9 +1069,9 @@
     return one_step(body, info, table, operands, outs, 2 * TOKENS * C * (C + FFI + WIDE_FF))
 
 
-def cross_back(info, table, mine, other, resid, gain, base, weight, query, context):
-    def body(info_ref, mine_ref, other_ref, resid_ref, gain_ref, base_ref, weight_ref, query_ref, kv_ref, *outs):
-        resid_out, co_low, query_low, kv_grad, sums = outs
+def cross_back(info, table, mine, other, resid, gain, base, weight, query, context, ckv):
+    def body(info_ref, mine_ref, other_ref, resid_ref, gain_ref, base_ref, weight_ref, query_ref, kv_ref, ckv_ref, *outs):
+        resid_out, co_low, query_low, kv_grad, sums, context_out = outs
         side = info_ref[0]
         result = layer_back(
             mine_ref[...] + other_ref[...], resid_ref[...], gain_ref[0:1], base_ref[...], side, sums
@@ -1097,6 +1091,9 @@
         for row, (prob, score) in enumerate(((first, first_grad), (second, second_grad))):
             kv_grad[row : row + 1, :HALF] = jnp.sum(score * query_now, axis=0, keepdims=True)
             kv_grad[row : row + 1, HALF:] = jnp.sum(prob * out_grad, axis=0, keepdims=True)
+        kv_grad[2:8, :] = jnp.zeros((6, WIDE), f32)
+        halves = [low(kv_grad[:, HALF * j : HALF * (j + 1)]) for j in range(2)]
+        context_out[...] = unstuffed([dot_t(one, ckv_ref[...]) for one in halves])
 
     outs = [
         ((TOKENS, C), f32),
@@ -1104,8 +1101,9 @@
         ((TOKENS, HALF), bf16),
         ((8, WIDE), f32),
         ((8, HALF), f32),
+        ((8, WIDE), f32),
     ]
-    operands = [mine, other, resid, gain, base, weight, query, context]
+    operands = [mine, other, resid, gain, base, weight, query, context, ckv]
     return one_step(body, info, table, operands, outs, 2 * TOKENS * C * 14 * HALF)
 
 
@@ -1185,10 +1183,131 @@
     return one_step(body, info, table, operands, outs, 2 * TOKENS * C * HALF)
 
 
+class LabelRows(Rows):
+    def spec(self):
+        at = self.at
+        return pl.BlockSpec(
+            (pl.Element(8), pl.Element(WIDE)),
+            lambda i, info_ref: (pl.multiple_of(at + info_ref[3] // 8 * 8, 8), 0),
+        )
+
+
+def stuffing(parity, kind):
+    row = lax.broadcasted_iota(jnp.int32, (WIDE, 2 * WIDE), 0)
+    column = lax.broadcasted_iota(jnp.int32, (WIDE, 2 * WIDE), 1)
+    return (column == 2 * row + parity).astype(f32).astype(kind)
+
+
+def unstuffed(parts):
+    total = None
+    for parity, part in enumerate(parts):
+        thirds, left = ([], part)
+        for _ in range(3):
+            thirds.append(low(left).astype(f32))
+            left = left - thirds[-1]
+        one = dot_t(low(jnp.concatenate(thirds, axis=0)), stuffing(parity, bf16))
+        one = one[0:8] + one[8:16] + one[16:24]
+        total = one if total is None else total + one
+    return total
+
+
+def first_row(values):
+    row = lax.broadcasted_iota(jnp.int32, values.shape, 0)
+    return jnp.where(row == 0, values, 0.0)
+
+
+def time_front(info, table, at, embed, biases):
+    def body(info_ref, embed_ref, bias_ref, one_ref, two_ref, out_ref, class_ref, kv_ref, *outs):
+        inner, both, context_kv = outs
+        spread = [stuffing(parity, bf16) for parity in range(2)]
+        inner[...] = jnp.zeros_like(inner)
+        hidden = []
+        for j in range(2):
+            pre = dot(low(embed_ref[8 * j : 8 * j + 8, :]), one_ref[...]) + bias_ref[j : j + 1]
+            act = low(silu_in(pre))
+            inner[0:1, WIDE * j : WIDE * (j + 1)] = pre[0:1]
+            inner[2:3, WIDE * j : WIDE * (j + 1)] = act.astype(f32)[0:1]
+            hidden.append(act)
+        last = []
+        for j in range(2):
+            pre = bias_ref[2 + j : 3 + j]
+            for p in range(2):
+                wide = low(dot(hidden[p], spread[j]))
+                pre = pre + dot(wide, two_ref[2 * WIDE * p : 2 * WIDE * (p + 1), :])
+            act = low(silu_in(pre))
+            inner[1:2, WIDE * j : WIDE * (j + 1)] = pre[0:1]
+            inner[3:4, WIDE * j : WIDE * (j + 1)] = act.astype(f32)[0:1]
+            last.append(act)
+        time_vec = bias_ref[4:5]
+        for p in range(2):
+            time_vec = time_vec + dot(last[p], out_ref[WIDE * p : WIDE * (p + 1), :])
+        row = lax.broadcasted_iota(jnp.int32, (8, WIDE), 0)
+        rows = class_ref[...].astype(f32)
+        class_vec = jnp.sum(jnp.where(row == lax.rem(info_ref[3], 8), rows, 0.0), axis=0, keepdims=True)
+        context = jnp.where(row == 0, class_vec, jnp.where(row == 1, time_vec[0:1], 0.0))
+        both[...] = context
+        context = low(context)
+        for j in range(2):
+            wide = low(dot(context, spread[j]))
+            context_kv[:, HALF * j : HALF * (j + 1)] = low(dot(wide, kv_ref[...]))
+
+    operands = [
+        embed,
+        biases,
+        Rows(at["w_t1"], 2 * TE),
+        Rows(at["w_t2"], 2 * TD),
+        Rows(at["w_tp"], TD),
+        LabelRows(at["table"], 8),
+        Rows(at["w_ckv"], 2 * C, side_columns=True),
+    ]
+    outs = [((8, 2 * WIDE), f32), ((8, WIDE), f32), ((8, WIDE), bf16)]
+    return one_step(body, info, table, operands, outs, 2 * 8 * 4096 * WIDE)
+
+
+def time_back(info, table, at, time_grad, inner, top, context_grad, squares):
+    def body(info_ref, grad_ref, inner_ref, two_ref, out_ref, top_ref, context_ref, *rest):
+        square_refs, (outs, bound_out) = (rest[:-2], rest[-2:])
+        time_low = low(grad_ref[...])
+        largest = lambda value: jnp.max(jnp.max(jnp.abs(value), axis=1, keepdims=True), axis=0, keepdims=True)
+
+        def slope(values):
+            logistic = 1.0 / (1.0 + jnp.exp(-values))
+            return logistic * (1.0 + values * (1.0 - logistic))
+
+        outs[...] = jnp.zeros_like(outs)
+        two = []
+        for p in range(2):
+            cols = slice(WIDE * p, WIDE * (p + 1))
+            grad = dot_t(time_low, out_ref[WIDE * p : WIDE * (p + 1), :])
+            grad = first_row(grad * slope(inner_ref[1:2, cols]))
+            outs[0:1, cols] = grad[0:1]
+            two.append(low(grad))
+        for p in range(2):
+            cols = slice(WIDE * p, WIDE * (p + 1))
+            rows = two_ref[2 * WIDE * p : 2 * WIDE * (p + 1), :]
+            grad = unstuffed([dot_t(two[j], rows) for j in range(2)])
+            outs[1:2, cols] = grad[0:1] * slope(inner_ref[0:1, cols])
+        bound = largest(inner_ref[3:4, :]) * largest(time_low.astype(f32))
+        bound = jnp.maximum(bound, largest(inner_ref[2:3, :]) * largest(outs[0:1, :]))
+        bound = jnp.maximum(bound, largest(outs[1:2, :]))
+        bound = jnp.maximum(1.02 * bound, largest(context_ref[0:1, :]))
+        bound = jnp.maximum(bound, top_ref[...])
+        lane = lax.broadcasted_iota(jnp.int32, (8, 128), 1)
+        row = jnp.broadcast_to(bound, (8, 128))
+        for i, (ref, (_, at_row)) in enumerate(zip(square_refs, squares)):
+            row = jnp.where(lane == i + 1, largest(ref[at_row : at_row + 1, :]), row)
+        bound_out[...] = row
+
+    operands = [time_grad, inner, Rows(at["w_t2"], 2 * TD), Rows(at["w_tp"], TD), top, context_grad]
+    operands += [one for one, _ in squares]
+    outs = [((8, 2 * WIDE), f32), ((8, 128), f32)]
+    return one_step(body, info, table, operands, outs, 2 * 8 * 3072 * WIDE)
+
+
 def channel_mix():
-    flat = lax.iota(jnp.int32, LC * C)[:, None]
-    split = lax.iota(jnp.int32, LC * C)[None]
-    return flat == LC * (split % C) + split // C
+    flat = np.arange(LC * C)[:, None]
+    split = np.arange(LC * C)[None]
+    return jnp.asarray((flat == LC * (split % C) + split // C).astype(ml_dtypes.bfloat16))
 
 
 def gather_small(place, value):
@@ -1250,7 +1369,7 @@
 def train_step(place, store, table, vecs, latents, target_noise, label, step_value, orient, extent):
     half, at = (place.half, store.places)
     turned = orient != 1
-    info = jnp.stack([place.side, turned.astype(jnp.int32), extent * FRAME]).astype(jnp.int32)
+    info = jnp.stack([place.side, turned.astype(jnp.int32), extent * FRAME, label]).astype(jnp.int32)
     mask = (lax.iota(jnp.int32, TOKENS) < extent * FRAME).astype(jnp.float32)[:, None]
     frame = frame_of(place, latents, target_noise, turned)
     share = noise_level(step_value)
@@ -1268,25 +1387,21 @@
     def own_rows(name):
         return Rows(at[name], HALF, side_rows=True)
 
-    w_t1 = unmix(info, table, at["w_t1"], TE, TD // WIDE, C)
-    w_t2 = unmix(info, table, at["w_t2"], TD, TD // WIDE, C)
     qkv = unmix(info, table, at["w_qkv"], C, 3, HALF)
-    ckv = unmix(info, table, at["w_ckv"], C, 2, HALF)
     ff1 = unmix(info, table, at["w_ff1"], C, 2 * FFI // WIDE, HALF)
-    w_tp = table[at["w_tp"] : at["w_tp"] + TD]
     w_in = half(table[at["w_in"] : at["w_in"] + 9 * LC])
-    w_out = dot(table[at["w_out"] : at["w_out"] + 9 * LC].reshape(9, LC * C), low(mix))
+    w_out = dot(table[at["w_out"] : at["w_out"] + 9 * LC].reshape(9, LC * C), mix)
     w_out = low(jnp.pad(w_out.reshape(9, LC, C), ((0, 0), (0, OUT_ROWS - LC), (0, 0))))
     w_out = w_out.reshape(9 * OUT_ROWS, C)
 
-    pre_one = dot(embed_in, w_t1) + vecs["b_t1"]
-    hidden_one = low(jax.nn.silu(pre_one))
-    pre_two = dot(hidden_one, w_t2) + vecs["b_t2"]
-    hidden_two = low(jax.nn.silu(pre_two))
-    time_vec = dot(hidden_two, w_tp) + vecs["b_tp"]
-    class_vec = lax.dynamic_slice(table, (at["table"] + label, 0), (1, C)).astype(jnp.float32)
-    context = low(jnp.concatenate([class_vec, time_vec], axis=0))
-    context_kv = jnp.pad(low(dot(context, ckv)), ((0, 6), (0, 0)))
+    twice = jnp.repeat(embed_in.astype(jnp.float32), 2, axis=1)
+    parity = lax.iota(jnp.int32, 2 * TE)[None] % 2
+    stuffed = [jnp.pad(jnp.where(parity == j, twice, 0.0), ((0, 7), (0, 0))) for j in range(2)]
+    biases = [vecs["b_t1"].reshape(2, WIDE), vecs["b_t2"].reshape(2, WIDE), vecs["b_tp"][None]]
+    biases = jnp.pad(jnp.concatenate(biases, axis=0), ((0, 3), (0, 0)))
+    inner, both, context_kv = time_front(info, table, at, jnp.concatenate(stuffed, axis=0), biases)
+    context, time_vec = (low(both[:2]), both[1:2])
+    hidden_one, hidden_two = (low(inner[2:3]), low(inner[3:4]))
 
     act_one, normed_one, inv_one, state_zero = first_forward(
         info, pad_in, w_in, side_rows("b_in", "g1", "bb1")
@@ -1369,16 +1484,15 @@
     store.add("w_ff2", gated, ff2_low)
     store.add("w_ff1", ln_three, proj_low)
     w_out_grad = w_out_grad.reshape(9, OUT_ROWS, C)[:, :LC].reshape(9, LC * C)
-    w_out_grad = lax.dot_general(
-        w_out_grad,
-        mix.astype(jnp.float32),
-        (((1,), (1,)), ((), ())),
-        precision=lax.Precision.HIGHEST,
-        preferred_element_type=jnp.float32,
-    )
+    thirds, left = ([], w_out_grad)
+    for _ in range(3):
+        thirds.append(lax.reduce_precision(left, 8, 7))
+        left = left - thirds[-1]
+    thirds = dot_t(low(jnp.concatenate(thirds, axis=0)), mix)
+    w_out_grad = thirds[:9] + thirds[9:18] + thirds[18:]
     w_out_grad = half(w_out_grad.reshape(9 * LC, C))
     store.put(at["w_out"], jnp.zeros((store.total - at["w_out"], HALF), jnp.float32))
-    resid_grad, co_low, query_low, kv_grad, sums_co = cross_back(
+    resid_grad, co_low, query_low, kv_grad, sums_co, context_grad = cross_back(
         info,
         table,
         ln_part,
@@ -1389,10 +1503,10 @@
         own_rows("w_co"),
         cross_query,
         context_kv,
+        Rows(at["w_ckv"], 2 * C, side_columns=True),
     )
     query_peer = place.swap(query_low)
     kv_low = low(kv_grad[:2])
-    context_grad = dot_t(kv_low, ckv)
     context_grad = context_grad + place.swap(context_grad)
     store.add("w_co", cross_out, co_low)
     store.add("w_cq", ln_two, query_low)
@@ -1446,23 +1560,24 @@
     time_grad = place.full(sums_one[0:1]) + context_grad[1:2]
     b_tp = half(time_grad)
     time_low = low(time_grad)
-    pre_grad = dot_t(time_low, w_tp) * silu_slope(pre_two)
-    b_t2 = half(pre_grad.reshape(-1, WIDE))
-    two_low = low(pre_grad)
-    pre_grad = dot_t(two_low, w_t2) * silu_slope(pre_one)
-    b_t1 = half(pre_grad.reshape(-1, WIDE))
-    one_low = low(pre_grad)
-    size = lambda one: jnp.max(jnp.abs(one.astype(jnp.float32)))
-    local = jnp.maximum(store.top[0, 0], size(context_grad[0]))
-    for left, right in ((hidden_two, time_low), (hidden_one, two_low), (embed_in, one_low)):
-        local = jnp.maximum(local, 1.01 * size(left) * size(right))
-    squares = [size(one) for one in (inv_one[1], inv_two[1], sums_two[3], sums_one[3])]
-    largest = Largest(place, lane_row([local] + squares))
+    outer, bounds = time_back(
+        info,
+        table,
+        at,
+        jnp.pad(time_grad, ((0, 7), (0, 0))),
+        inner,
+        store.top,
+        context_grad,
+        ((inv_one, 1), (inv_two, 1), (sums_two, 3), (sums_one, 3)),
+    )
+    b_t2, b_t1 = (half(outer[0].reshape(-1, WIDE)), half(outer[1].reshape(-1, WIDE)))
+    two_low, one_low = (low(b_t2), low(b_t1))
+    largest = Largest(place, bounds)
     store.add("w_tp", hidden_two, half(time_low))
     store.buffer = largest.exchange(store.buffer)
-    store.add("w_t2", hidden_one, half(two_low.reshape(-1, WIDE)).reshape(1, -1))
+    store.add("w_t2", hidden_one, two_low.reshape(1, -1))
     store.buffer = largest.exchange(store.buffer)
-    store.add("w_t1", embed_in, half(one_low.reshape(-1, WIDE)).reshape(1, -1))
+    store.add("w_t1", embed_in, one_low.reshape(1, -1))
     chosen = lax.iota(jnp.int32, NCLS)[:, None] == label
     store.put(at["table"], jnp.where(chosen, half(context_grad[0:1]), 0.0))
     store.put(0, jnp.zeros((at["w_t1"], HALF), jnp.float32))

time: 630 us -> 613 us (0.973)
  other arithmetic: 84.1 us -> 54 us
  waiting for transfers between devices: 243 us -> 257 us
  Pallas kernels: 112 us -> 125 us
  local copies, waits for them, and re-layouts: 56.6 us -> 45.6 us
  starting transfers between devices: 72.4 us -> 79.6 us
    pallas_call x8 -> x10, Pallas kernels: 48 us -> 67.6 us  [one_step(): pl.pallas_call(body, grid_spec=pltpu.PrefetchScalarGridSpec(num_scalar_pr...]
    ppermute x55 -> x52, waiting for transfers between devices: 107 us -> 123 us  [move(): return lax.ppermute(value, ('dp', 'rows'), pairs)]
    convert_element_type x15 -> x12, other arithmetic: 29.7 us -> 20.6 us  [wire(): return values.astype(jnp.float16)]
    dynamic_slice x2 -> x0, local copies, waits for them, and re-layouts: 7.57 us -> none  [the longest x1 6.83 us: part_of(): out = lax.dynamic_slice(held, starts + [first, 0], sizes + [rows, HALF])]
    ppermute x55 -> x52, starting transfers between devices: 72.4 us -> 79.6 us  [move(): return lax.ppermute(value, ('dp', 'rows'), pairs)]
    reduce_max x9 -> x0, other arithmetic: 7.18 us -> none  [train_step(): size = lambda one: jnp.max(jnp.abs(one.astype(jnp.float32)))]
    pallas_call x5 -> x2, Pallas kernels: 12.4 us -> 5.64 us  [unmix(): pl.pallas_call(body, grid_spec=pltpu.PrefetchScalarGridSpec(num_scalar_pr...]
    unnamed x233 -> x209, local copies, waits for them, and re-layouts: 28.4 us -> 23.5 us
  transfers between devices with their start and end apart: 56 -> 53, of which waited for: 27 -> 28; matrix products, arithmetic and copies ran while one was open for 16% -> 10% of each run, Pallas kernels for 6% -> 8%
where the time goes in v3:
time: 613 us; the launch traced here: 602 us
  waiting for transfers between devices  257 us (42%)
  Pallas kernels  125 us (20%)
  starting transfers between devices  79.6 us (13%)
  other arithmetic  54 us (9%)
  local copies, waits for them, and re-layouts  45.6 us (7%)
  between operations  35.4 us (6%)
    all_gather x1, waiting for transfers between devices, local(): table = lax.all_gather(block, ('dp', 'rows'), axis=0, tiled=True)  134 us
    ppermute x52, waiting for transfers between devices, move(): return lax.ppermute(value, ('dp', 'rows'), pairs)  123 us
    ppermute x52, starting transfers between devices, move(): return lax.ppermute(value, ('dp', 'rows'), pairs)  79.6 us
    pallas_call x10, Pallas kernels, one_step(): pl.pallas_call(body, grid_spec=pltpu.PrefetchScalarGridSpec(num_scalar_pr...  67.6 us
    unnamed x209, local copies, waits for them, and re-layouts  23.5 us
    pallas_call x12, Pallas kernels, grad_into(): pl.pallas_call(body, grid=(tiles,), in_specs=old_specs + [pl.BlockSpec((t...  21.9 us
    convert_element_type x12, other arithmetic, wire(): return values.astype(jnp.float16)  20.6 us
    pallas_call x2, Pallas kernels, conv_backward(): pl.pallas_call(body, grid_spec=pltpu.PrefetchScalarGridSpec(num_scalar_pr...  17.4 us
  transfers between devices with their start and end apart: 53, of which 28 were waited for; matrix products, arithmetic and copies ran while one was open for 10% of the time, Pallas kernels for 8%

profile of v3, /device:TPU:4, one launch (start us, length us, event | category | flops | bytes accessed | tf_op | source)
XLA Modules:
  0.0 601.7 jit_solution(1787967206995615696)
XLA Ops:
  8.8 2.8 collective-permute-start.2
  11.5 3.5 collective-permute-done.2
  15.0 5.3 concatenate.176
  31.1 3.3 collective-permute-start.4
  36.1 3.7 collective-permute-done.5
  50.3 133.9 %all-gather.2.cloned.1.call-done.one_ref.two_ref.out_ref.class_ref.kv_ref.weight_ref.rows_ref.qw_ref.ow_ref.refs_5_.refs_6_.ckv_ref.refs_7_ = bf16[25344,512]{1,0:T(8,128)(2,1)} async-done(((bf16[792,512]{1,0:T(8,128)(2,1)}), bf16[25344,512]{1,0:T(8,128)(2,1)}) %all-gather.2.cloned.1.call-update) | async-done | bytes 25952272 | tf_op jit(solution)/shard_map/all_gather | solution.py:1642
  184.2 5.1 shard_map.231
  194.1 5.5 shard_map.232
  202.0 5.5 shard_map.233
  210.5 4.8 shard_map.235
  219.4 4.2 shard_map.236
  227.1 3.5 shard_map.237.fw_ref.refs_8_
  232.0 6.5 %shard_map.238 = (bf16[512,512]{1,0:T(8,128)(2,1)S(1)}, f32[512,512]{1,0:T(8,128)S(1)}, bf16[512,512]{1,0:T(8,128)(2,1)S(1)}, f32[512,2048]{1,0:T(8,128)}, bf16[512,1024]{1,0:T(8,128)(2,1)S(1)}) custom-call(s32[4]{0:T(128)S(1)} %pad_add_fusion.info_ref, bf16[512,256]{1,0:T(8,128)(2,1)S(1)} %get-tuple-element.114.mine_ref, ...), custom_call_target="tpu_custom_call" | custom-call | flops 1342177280 | bytes 14680064 | tf_op jit(solution)/shard_map/pallas_call | solution.py:809
  244.7 4.8 shard_map.239
  249.8 3.6 convolution_convert_fusion
  253.6 8.7 %shard_map.240 = (f32[72,512]{1,0:T(8,128)S(1)}, f32[8,256]{1,0:T(8,128)S(1)}, f32[512,256]{1,0:T(8,128)S(1)}, bf16[512,256]{1,0:T(8,128)(2,1)S(1)}, bf16[512,25...) custom-call(s32[4]{0:T(128)S(1)} %pad_add_fusion.info_ref, ...), custom_call_target="tpu_custom_call" | custom-call | flops 1879048192 | bytes 10829824 | tf_op jit(solution)/shard_map/pallas_call | solution.py:809
  268.4 6.5 %shard_map.244 = (f32[512,512]{1,0:T(8,128)S(1)}, bf16[512,256]{1,0:T(8,128)(2,1)S(1)}, bf16[512,256]{1,0:T(8,128)(2,1)S(1)}, f32[8,512]{1,0:T(8,128)S(1)}, f32[8,256]{1,0:T(8,128)S(1)}, /*index=5*/f32[8,512]{1,0:T(8,128)S(1)}) custom-call(s32[4]{0:T(128)S(1)} %pad_add_fusion.info_ref, f32[512,512]{1,0:T(8,128)S(1)} %get-tuple-element.131.mine_ref, ...), custom_call_target="tpu_custom_call" | custom-call | flops 1879048192 | bytes 3227648 | tf_op jit(solution)/shard_map/pallas_call | solution.py:809
  279.9 17.2 %shard_map.248 = (f32[512,512]{1,0:T(8,128)}, bf16[512,256]{1,0:T(8,128)(2,1)S(1)}, bf16[512,768]{1,0:T(8,128)(2,1)S(1)}, f32[512,512]{1,0:T(8,128)}, f32[8,256]{1,0:T(8,128)S(1)}) custom-call(s32[4]{0:T(128)S(1)} %pad_add_fusion.info_ref, bf16[512,256]{1,0:T(8,128)(2,1)S(1)} %get-tuple-element.137.refs_2_.mine_ref, bf16[512,256]{1,0:T(8,128)(2,1)S(1)} %copy-done.43, ...), custom_call_target="tpu_custom_call" | custom-call | flops 3489660928 | bytes 6307840 | tf_op jit(solution)/shard_map/pallas_call | solution.py:809
  302.6 3.0 shard_map.242
  306.6 4.6 shard_map.251
  311.6 4.2 shard_map.243
  325.8 8.7 %shard_map.253 = (f32[25344,256]{1,0:T(8,128)}, bf16[512,256]{1,0:T(8,128)(2,1)S(1)}, f32[8,256]{1,0:T(8,128)S(1)}) custom-call(s32[4]{0:T(128)S(1)} %pad_add_fusion.info_ref, f32[25344,256]{1,0:T(8,128)} %get-tuple-element.156.refs_0_, bf16[512,256]{1,0:T(8,128)(2,1)S(1)} %get-tuple-element.157.refs_1_, ...), custom_call_target="tpu_custom_call", output_to_operand_aliasing={{0}: (1, {})} | custom-call | flops 2415919104 | bytes 10223616 | tf_op jit(solution)/shard_map/pallas_call | solution.py:695
  340.4 5.3 shard_map.254
  348.3 2.7 shard_map.256
  355.5 8.7 %shard_map.258 = (f32[25344,256]{1,0:T(8,128)}, bf16[512,256]{1,0:T(8,128)(2,1)S(1)}, f32[8,256]{1,0:T(8,128)S(1)}) custom-call(s32[4]{0:T(128)S(1)} %pad_add_fusion.info_ref, f32[25344,256]{1,0:T(8,128)} %broadcast_dynamic-update-slice_fusion.1.refs_0_, bf16[512,256]{1,0:T(8,128)(2,1)S(1)} %get-tuple-element.186.refs_1_, ...), custom_call_target="tpu_custom_call", output_to_operand_aliasing={{0}: (1, {})} | custom-call | flops 2415919104 | bytes 10223616 | tf_op jit(solution)/shard_map/pallas_call | solution.py:695
  375.0 4.0 collective-permute-start.37
  379.0 4.8 fusion.6
  384.6 4.5 fusion.7
  390.8 3.6 collective-permute-done.37
  396.2 4.7 collective-permute-start.38
  402.4 12.9 %collective-permute-done.38 = f16[2,2,392,256]{3,2,1,0:T(8,128)(2,1)S(1)} collective-permute-done((f16[2,2,392,256]{3,2,1,0:T(8,128)(2,1)S(1)}, f16[2,2,392,256]{3,2,1,0:T(8,128)(2,1)S(1)}, u32[]{:S(2)}, u32[]{:S(2)}) %collective-permute-start.38) | collective-permute-done | bytes 802848 | tf_op jit(solution)/shard_map/ppermute | solution.py:173
  415.3 3.4 fusion.14
  422.8 5.9 collective-permute-start.39
  428.7 6.9 %collective-permute-done.32 = f16[4,2,528,256]{3,2,1,0:T(8,128)(2,1)} collective-permute-done((f16[4,2,528,256]{3,2,1,0:T(8,128)(2,1)}, f16[4,2,528,256]{3,2,1,0:T(8,128)(2,1)}, u32[]{:S(2)}, u32[]{:S(2)}) %collective-permute-start.32) | collective-permute-done | bytes 2162720 | tf_op jit(solution)/shard_map/ppermute | solution.py:173
  435.6 3.3 fusion.4
  442.0 3.3 collective-permute-start.35
  448.3 3.9 fusion.1
  455.2 38.3 %collective-permute-done.42 = f16[2,2,392,256]{3,2,1,0:T(8,128)(2,1)} collective-permute-done((f16[2,2,392,256]{3,2,1,0:T(8,128)(2,1)S(1)}, f16[2,2,392,256]{3,2,1,0:T(8,128)(2,1)}, u32[]{:S(2)}, u32[]{:S(2)}) %collective-permute-start.42) | collective-permute-done | bytes 802848 | tf_op jit(solution)/shard_map/ppermute | solution.py:173
  500.0 8.0 %collective-permute-done.43 = f16[2,392,256]{2,1,0:T(8,128)(2,1)S(1)} collective-permute-done((f16[2,392,256]{2,1,0:T(8,128)(2,1)S(1)}, f16[2,392,256]{2,1,0:T(8,128)(2,1)S(1)}, u32[]{:S(2)}, u32[]{:S(2)}) %collective-permute-start.43) | collective-permute-done | bytes 401440 | tf_op jit(solution)/shard_map/ppermute | solution.py:173
  511.9 12.4 %collective-permute-start.29 = (f16[664,256]{1,0:T(8,128)(2,1)S(1)}, f16[664,256]{1,0:T(8,128)(2,1)S(1)}, u32[]{:S(2)}, u32[]{:S(2)}) collective-permute-start(f16[664,256]{1,0:T(8,128)(2,1)S(1)} %get-tuple-element.242), channel_id=1, source_target_pairs={{0,8},{1,9},{2,10},{3,11},{4,12},{5,13},{6,14},{7,15},{8,16},{9,17... | collective-permute-start | bytes 1019912 | tf_op jit(solution)/shard_map/ppermute | solution.py:173
  528.2 4.5 collective-permute-done.29
  532.7 6.8 %collective-permute-done.30 = f16[664,256]{1,0:T(8,128)(2,1)S(1)} collective-permute-done((f16[664,256]{1,0:T(8,128)(2,1)S(1)}, f16[664,256]{1,0:T(8,128)(2,1)S(1)}, u32[]{:S(2)}, u32[]{:S(2)}) %collective-permute-start.30) | collective-permute-done | bytes 340000 | tf_op jit(solution)/shard_map/ppermute | solution.py:173
  545.6 4.1 collective-permute-done.47
  550.3 4.1 collective-permute-done.48
  554.4 7.7 %collective-permute-start.49 = (f32[88,256]{1,0:T(8,128)S(1)}, f32[88,256]{1,0:T(8,128)S(1)}, u32[]{:S(2)}, u32[]{:S(2)}) collective-permute-start(f32[88,256]{1,0:T(8,128)S(1)} %add.497), channel_id=1, source_target_pairs={{0,8},{1,9},{2,10},{3,11},{4,12},{5,13},{6,14},{7,15},{8,0},{9,1},... | collective-permute-start | bytes 270344 | tf_op jit(solution)/shard_map/ppermute | solution.py:173
  564.5 3.4 collective-permute-start.50
  583.3 4.2 collective-permute-done.46
  589.4 3.8 multiply_add_fusion
  (483 shorter events, 142.5 us)
Async XLA Ops:
  7.2 177.0 %all-gather.2.cloned.1.call-start = ((), (), s32[]{:S(2)}) async-start(), calls=%async_computation | async-start | bytes 26763264 | tf_op jit(solution)/shard_map/all_gather | solution.py:1642
  8.8 6.3 %collective-permute-start.2 = (bf16[113664]{0:T(1024)(128)(2,1)S(1)}, bf16[113664]{0:T(1024)(128)(2,1)S(1)}, u32[]{:S(2)}, u32[]{:S(2)}) collective-permute-start(bf16[113664]{0:T(1024)(128)(2,1)S(1)} %slice.357), channel_id=1, source_target_pairs={{1,0},{2,1},{3,2},{4,3},{5,4},{6,5},{7,6},{8,7},{9,8},{10,9},{11,1... | collective-permute-start | bytes 681992 | tf_op jit(solution)/shard_map/ppermute | solution.py:173
  22.3 8.7 %collective-permute-start.3 = (bf16[1,5,128]{2,0,1:T(2,128)(2,1)S(1)}, bf16[1,5,128]{2,0,1:T(2,128)(2,1)S(1)}, u32[]{:S(2)}, u32[]{:S(2)}) collective-permute-start(bf16[1,5,128]{2,0,1:T(2,128)(2,1)S(1)} %broadcast_in_dim_reshape.3), channel_id=1, source_target_pairs={{0,1},{1,0},{2,3},{3,2},{4,5},{5,4},{6,7},{7,6},{8,9},{9,8},{10,11... | collective-permute-start | bytes 3848 | tf_op jit(solution)/shard_map/ppermute | solution.py:173
  23.3 18.1 %collective-permute-start = (f32[1,2,8,32,6]{3,2,0,4,1:T(8,128)S(1)}, f32[1,2,8,32,6]{3,2,0,4,1:T(8,128)S(1)}, u32[]{:S(2)}, u32[]{:S(2)}) collective-permute-start(f32[1,2,8,32,6]{3,2,0,4,1:T(8,128)S(1)} %maximum_bitcast_fusion), channel_id=1, source_target_pairs={{0,1},{1,0},{2,3},{3,2},{4,5},{5,4},{6,7},{7,6},{8,9},{9,8},{10,11... | collective-permute-start | bytes 36872 | tf_op jit(solution)/shard_map/ppermute | solution.py:173
  31.1 4.9 collective-permute-start.4
  36.0 3.8 collective-permute-start.5
  39.8 4.0 collective-permute-start.6
  41.5 4.9 collective-permute-start.1
  43.8 5.7 collective-permute-start.7
  208.1 2.4 collective-permute-start.10
  226.8 5.2 collective-permute-start.12
  241.0 2.7 collective-permute-start.13
  249.5 4.0 collective-permute-start.14
  265.7 2.7 collective-permute-start.15
  297.1 8.5 %collective-permute-start.17 = (f32[512,512]{1,0:T(8,128)}, f32[512,512]{1,0:T(8,128)S(1)}, u32[]{:S(2)}, u32[]{:S(2)}) collective-permute-start(f32[512,512]{1,0:T(8,128)} %get-tuple-element.150.mine_ref), channel_id=1, source_target_pairs={{0,1},{1,0},{2,3},{3,2},{4,5},{5,4},{6,7},{7,6},{8,9},{9,8},{10,11... | collective-permute-start | bytes 3145736 | tf_op jit(solution)/shard_map/ppermute | solution.py:173
  311.2 14.5 %collective-permute-start.18 = (bf16[512,256]{1,0:T(8,128)(2,1)S(1)}, bf16[512,256]{1,0:T(8,128)(2,1)S(1)}, u32[]{:S(2)}, u32[]{:S(2)}) collective-permute-start(bf16[512,256]{1,0:T(8,128)(2,1)S(1)} %get-tuple-element.157.refs_1_), channel_id=1, source_target_pairs={{0,1},{1,0},{2,3},{3,2},{4,5},{5,4},{6,7},{7,6},{8,9},{9,8},{10,11... | collective-permute-start | bytes 786440 | tf_op jit(solution)/shard_map/ppermute | solution.py:173
  317.2 20.9 %collective-permute-start.20 = (f32[8,512]{1,0:T(8,128)S(1)}, f32[8,512]{1,0:T(8,128)S(1)}, u32[]{:S(2)}, u32[]{:S(2)}) collective-permute-start(f32[8,512]{1,0:T(8,128)S(1)} %get-tuple-element.161), channel_id=1, source_target_pairs={{0,1},{1,0},{2,3},{3,2},{4,5},{5,4},{6,7},{7,6},{8,9},{9,8},{10,11... | collective-permute-start | bytes 49160 | tf_op jit(solution)/shard_map/ppermute | solution.py:173
  334.5 5.8 collective-permute-start.19
  340.0 15.4 %collective-permute-start.25 = (bf16[512,256]{1,0:T(8,128)(2,1)S(1)}, bf16[512,256]{1,0:T(8,128)(2,1)S(1)}, u32[]{:S(2)}, u32[]{:S(2)}) collective-permute-start(bf16[512,256]{1,0:T(8,128)(2,1)S(1)} %get-tuple-element.186.refs_1_), channel_id=1, source_target_pairs={{0,1},{1,0},{2,3},{3,2},{4,5},{5,4},{6,7},{7,6},{8,9},{9,8},{10,11... | collective-permute-start | bytes 786440 | tf_op jit(solution)/shard_map/ppermute | solution.py:173
  345.7 2.0 collective-permute-start.21
  347.7 3.6 collective-permute-start.22
  351.3 4.1 collective-permute-start.23
  355.4 8.7 %collective-permute-start.24 = (f32[8,128]{1,0:T(8,128)S(1)}, f32[8,128]{1,0:T(8,128)S(1)}, u32[]{:S(2)}, u32[]{:S(2)}) collective-permute-start(f32[8,128]{1,0:T(8,128)S(1)} %max.64), channel_id=1, source_target_pairs={{0,8},{1,9},{2,10},{3,11},{4,12},{5,13},{6,14},{7,15},{8,0},{9,1},... | collective-permute-start | bytes 12296 | tf_op jit(solution)/shard_map/ppermute | solution.py:173
  364.1 4.6 collective-permute-start.26
  375.0 19.5 %collective-permute-start.37 = (f16[2,2,392,256]{3,2,1,0:T(8,128)(2,1)S(1)}, f16[2,2,392,256]{3,2,1,0:T(8,128)(2,1)S(1)}, u32[]{:S(2)}, u32[]{:S(2)}) collective-permute-start(f16[2,2,392,256]{3,2,1,0:T(8,128)(2,1)S(1)} %get-tuple-element.235), channel_id=1, source_target_pairs={{0,8},{1,9},{2,10},{3,11},{4,12},{5,13},{6,14},{7,15}} | collective-permute-start | bytes 2408456 | tf_op jit(solution)/shard_map/ppermute | solution.py:173
  383.7 63.2 %collective-permute-start.27 = (f16[4,2,664,256]{3,2,1,0:T(8,128)(2,1)}, f16[4,2,664,256]{3,2,1,0:T(8,128)(2,1)}, u32[]{:S(2)}, u32[]{:S(2)}) collective-permute-start(f16[4,2,664,256]{3,2,1,0:T(8,128)(2,1)} %fusion.6), channel_id=1, source_target_pairs={{0,2},{1,3},{2,0},{3,1},{4,6},{5,7},{6,4},{7,5},{8,10},{9,11},{10,... | collective-permute-start | bytes 8159240 | tf_op jit(solution)/shard_map/ppermute | solution.py:173
  389.2 46.4 %collective-permute-start.32 = (f16[4,2,528,256]{3,2,1,0:T(8,128)(2,1)}, f16[4,2,528,256]{3,2,1,0:T(8,128)(2,1)}, u32[]{:S(2)}, u32[]{:S(2)}) collective-permute-start(f16[4,2,528,256]{3,2,1,0:T(8,128)(2,1)} %fusion.7), channel_id=1, source_target_pairs={{0,4},{1,5},{2,6},{3,7},{4,0},{5,1},{6,2},{7,3},{8,12},{9,13},{10,... | collective-permute-start | bytes 6488072 | tf_op jit(solution)/shard_map/ppermute | solution.py:173
  390.1 12.3 %collective-permute-start.40 = (f16[2,2,392,256]{3,2,1,0:T(8,128)(2,1)S(1)}, f16[2,2,392,256]{3,2,1,0:T(8,128)(2,1)S(1)}, u32[]{:S(2)}, u32[]{:S(2)}) collective-permute-start(f16[2,2,392,256]{3,2,1,0:T(8,128)(2,1)S(1)} %get-tuple-element.236), channel_id=1, source_target_pairs={{24,16},{25,17},{26,18},{27,19},{28,20},{29,21},{30,22},{31,23}} | collective-permute-start | bytes 2408456 | tf_op jit(solution)/shard_map/ppermute | solution.py:173
  396.2 19.1 %collective-permute-start.38 = (f16[2,2,392,256]{3,2,1,0:T(8,128)(2,1)S(1)}, f16[2,2,392,256]{3,2,1,0:T(8,128)(2,1)S(1)}, u32[]{:S(2)}, u32[]{:S(2)}) collective-permute-start(f16[2,2,392,256]{3,2,1,0:T(8,128)(2,1)S(1)} %fusion.13), channel_id=1, source_target_pairs={{0,8},{1,9},{2,10},{3,11},{4,12},{5,13},{6,14},{7,15},{8,16},{9,17... | collective-permute-start | bytes 2408456 | tf_op jit(solution)/shard_map/ppermute | solution.py:173
  418.7 23.3 %collective-permute-start.41 = (f16[2,2,392,256]{3,2,1,0:T(8,128)(2,1)S(1)}, f16[2,2,392,256]{3,2,1,0:T(8,128)(2,1)S(1)}, u32[]{:S(2)}, u32[]{:S(2)}) collective-permute-start(f16[2,2,392,256]{3,2,1,0:T(8,128)(2,1)S(1)} %get-tuple-element.234), channel_id=1, source_target_pairs={{16,8},{17,9},{18,10},{19,11},{20,12},{21,13},{22,14},{23,15},{24,... | collective-permute-start | bytes 2408456 | tf_op jit(solution)/shard_map/ppermute | solution.py:173
  422.8 29.7 %collective-permute-start.39 = (f16[2,2,392,256]{3,2,1,0:T(8,128)(2,1)}, f16[2,2,392,256]{3,2,1,0:T(8,128)(2,1)}, u32[]{:S(2)}, u32[]{:S(2)}) collective-permute-start(f16[2,2,392,256]{3,2,1,0:T(8,128)(2,1)} %get-tuple-element.233), channel_id=1, source_target_pairs={{0,8},{1,9},{2,10},{3,11},{4,12},{5,13},{6,14},{7,15},{8,16},{9,17... | collective-permute-start | bytes 2408456 | tf_op jit(solution)/shard_map/ppermute | solution.py:173
  441.4 56.2 %collective-permute-start.33 = (f16[2,528,256]{2,1,0:T(8,128)(2,1)}, f16[2,528,256]{2,1,0:T(8,128)(2,1)}, u32[]{:S(2)}, u32[]{:S(2)}) collective-permute-start(f16[2,528,256]{2,1,0:T(8,128)(2,1)} %get-tuple-element.239), channel_id=1, source_target_pairs={{0,8},{1,9},{2,10},{3,11},{4,12},{5,13},{6,14},{7,15},{8,16},{9,17... | collective-permute-start | bytes 1622024 | tf_op jit(solution)/shard_map/ppermute | solution.py:173
  441.4 56.2 %collective-permute-start.34 = (f16[2,528,256]{2,1,0:T(8,128)(2,1)}, f16[2,528,256]{2,1,0:T(8,128)(2,1)}, u32[]{:S(2)}, u32[]{:S(2)}) collective-permute-start(f16[2,528,256]{2,1,0:T(8,128)(2,1)} %get-tuple-element.241), channel_id=1, source_target_pairs={{0,16},{1,17},{2,18},{3,19},{4,20},{5,21},{6,22},{7,23},{8,24},{9,... | collective-permute-start | bytes 1622024 | tf_op jit(solution)/shard_map/ppermute | solution.py:173
  442.0 55.7 %collective-permute-start.35 = (f16[2,528,256]{2,1,0:T(8,128)(2,1)}, f16[2,528,256]{2,1,0:T(8,128)(2,1)S(1)}, u32[]{:S(2)}, u32[]{:S(2)}) collective-permute-start(f16[2,528,256]{2,1,0:T(8,128)(2,1)} %get-tuple-element.240), channel_id=1, source_target_pairs={{0,24},{1,25},{2,26},{3,27},{4,28},{5,29},{6,30},{7,31},{8,0},{9,1... | collective-permute-start | bytes 1622024 | tf_op jit(solution)/shard_map/ppermute | solution.py:173
  447.0 46.5 %collective-permute-start.42 = (f16[2,2,392,256]{3,2,1,0:T(8,128)(2,1)S(1)}, f16[2,2,392,256]{3,2,1,0:T(8,128)(2,1)}, u32[]{:S(2)}, u32[]{:S(2)}) collective-permute-start(f16[2,2,392,256]{3,2,1,0:T(8,128)(2,1)S(1)} %fusion.12), channel_id=1, source_target_pairs={{8,0},{9,1},{10,2},{11,3},{12,4},{13,5},{14,6},{15,7},{16,8},{17,9... | collective-permute-start | bytes 2408456 | tf_op jit(solution)/shard_map/ppermute | solution.py:173
  452.5 57.5 %collective-permute-start.28 = (f16[4,664,256]{2,1,0:T(8,128)(2,1)S(1)}, f16[4,664,256]{2,1,0:T(8,128)(2,1)}, u32[]{:S(2)}, u32[]{:S(2)}) collective-permute-start(f16[4,664,256]{2,1,0:T(8,128)(2,1)S(1)} %fusion.16), channel_id=1, source_target_pairs={{0,4},{1,5},{2,6},{3,7},{4,0},{5,1},{6,2},{7,3},{8,12},{9,13},{10,... | collective-permute-start | bytes 4079624 | tf_op jit(solution)/shard_map/ppermute | solution.py:173
  495.7 12.2 %collective-permute-start.43 = (f16[2,392,256]{2,1,0:T(8,128)(2,1)S(1)}, f16[2,392,256]{2,1,0:T(8,128)(2,1)S(1)}, u32[]{:S(2)}, u32[]{:S(2)}) collective-permute-start(f16[2,392,256]{2,1,0:T(8,128)(2,1)S(1)} %fusion.29), channel_id=1, source_target_pairs={{0,2},{1,3},{2,0},{3,1},{4,6},{5,7},{6,4},{7,5},{8,10},{9,11},{10,... | collective-permute-start | bytes 1204232 | tf_op jit(solution)/shard_map/ppermute | solution.py:173
  499.7 27.0 %collective-permute-start.36 = (f16[528,256]{1,0:T(8,128)(2,1)S(1)}, f16[528,256]{1,0:T(8,128)(2,1)S(1)}, u32[]{:S(2)}, u32[]{:S(2)}) collective-permute-start(f16[528,256]{1,0:T(8,128)(2,1)S(1)} %fusion.34), channel_id=1, source_target_pairs={{0,2},{1,3},{2,0},{3,1},{4,6},{5,7},{6,4},{7,5},{8,10},{9,11},{10,... | collective-permute-start | bytes 811016 | tf_op jit(solution)/shard_map/ppermute | solution.py:173
  508.1 19.4 %collective-permute-start.44 = (f16[392,256]{1,0:T(8,128)(2,1)S(1)}, f16[392,256]{1,0:T(8,128)(2,1)S(1)}, u32[]{:S(2)}, u32[]{:S(2)}) collective-permute-start(f16[392,256]{1,0:T(8,128)(2,1)S(1)} %fusion.35), channel_id=1, source_target_pairs={{0,4},{1,5},{2,6},{3,7},{4,0},{5,1},{6,2},{7,3},{8,12},{9,13},{10,... | collective-permute-start | bytes 602120 | tf_op jit(solution)/shard_map/ppermute | solution.py:173
  511.9 20.8 %collective-permute-start.29 = (f16[664,256]{1,0:T(8,128)(2,1)S(1)}, f16[664,256]{1,0:T(8,128)(2,1)S(1)}, u32[]{:S(2)}, u32[]{:S(2)}) collective-permute-start(f16[664,256]{1,0:T(8,128)(2,1)S(1)} %get-tuple-element.242), channel_id=1, source_target_pairs={{0,8},{1,9},{2,10},{3,11},{4,12},{5,13},{6,14},{7,15},{8,16},{9,17... | collective-permute-start | bytes 1019912 | tf_op jit(solution)/shard_map/ppermute | solution.py:173
  524.3 15.2 %collective-permute-start.30 = (f16[664,256]{1,0:T(8,128)(2,1)S(1)}, f16[664,256]{1,0:T(8,128)(2,1)S(1)}, u32[]{:S(2)}, u32[]{:S(2)}) collective-permute-start(f16[664,256]{1,0:T(8,128)(2,1)S(1)} %get-tuple-element.244), channel_id=1, source_target_pairs={{0,16},{1,17},{2,18},{3,19},{4,20},{5,21},{6,22},{7,23},{8,24},{9,... | collective-permute-start | bytes 1019912 | tf_op jit(solution)/shard_map/ppermute | solution.py:173
  524.3 17.9 %collective-permute-start.31 = (f16[664,256]{1,0:T(8,128)(2,1)S(1)}, f16[664,256]{1,0:T(8,128)(2,1)S(1)}, u32[]{:S(2)}, u32[]{:S(2)}) collective-permute-start(f16[664,256]{1,0:T(8,128)(2,1)S(1)} %get-tuple-element.243), channel_id=1, source_target_pairs={{0,24},{1,25},{2,26},{3,27},{4,28},{5,29},{6,30},{7,31},{8,0},{9,1... | collective-permute-start | bytes 1019912 | tf_op jit(solution)/shard_map/ppermute | solution.py:173
  545.1 4.6 collective-permute-start.47
  549.7 4.6 collective-permute-start.48
  554.4 10.2 %collective-permute-start.49 = (f32[88,256]{1,0:T(8,128)S(1)}, f32[88,256]{1,0:T(8,128)S(1)}, u32[]{:S(2)}, u32[]{:S(2)}) collective-permute-start(f32[88,256]{1,0:T(8,128)S(1)} %add.497), channel_id=1, source_target_pairs={{0,8},{1,9},{2,10},{3,11},{4,12},{5,13},{6,14},{7,15},{8,0},{9,1},... | collective-permute-start | bytes 270344 | tf_op jit(solution)/shard_map/ppermute | solution.py:173
  564.5 6.0 collective-permute-start.50
  570.7 5.0 collective-permute-start.45
  577.1 10.5 %collective-permute-start.46 = (f32[109568]{0:T(1024)S(1)}, f32[109568]{0:T(1024)S(1)}, u32[]{:S(2)}, u32[]{:S(2)}) collective-permute-start(f32[109568]{0:T(1024)S(1)} %slice.323), channel_id=1, source_target_pairs={{0,1},{1,2},{2,3},{3,4},{4,5},{5,6},{6,7},{7,8},{8,9},{9,10},{10,1... | collective-permute-start | bytes 1314824 | tf_op jit(solution)/shard_map/ppermute | solution.py:173
  (105 other events, 1215.9 us)
Sparse Core Ops, SparseCore 0:
  22.4 161.7 all-gather.1

commit v4 on v3

--- a/solution.py
+++ b/solution.py
@@ -293,7 +293,7 @@
         return self.values
 
 
-def scatter_part(place, grads, low_row, rows, order, scale):
+def scatter_part(place, grads, low_row, rows, order, scale, after=(), ahead=None):
     held, left, first, factor = (grads, list(range(len(place.digits))), low_row, scale)
 
     def part_of(dim, index):
@@ -313,22 +313,34 @@
         if size == 2 or axis != order[0]:
             for away in range(1, size):
                 sent = wire(part_of(dim, (me + away) % size))
-                total = total + plain(place.rotate(sent, axis, away))
+                if ahead is not None and axis == order[0] and away == 1:
+                    sent = ahead
+                got = place.rotate(sent, axis, away)
+                if axis == order[0] and after:
+                    got = lax.optimization_barrier((got, *after))[0]
+                total = total + plain(got)
+                last = (sent,)
         else:
-            flows = {1: None, -1: None}
+            flows, sent = ({1: None, -1: None}, {})
             for hops in range(size - 1):
                 for direction in (1, -1):
                     rank = me if direction > 0 else size - 1 - me
                     aim = jnp.minimum(size - 1 - hops + rank, size - 1)
                     aim = aim if direction > 0 else size - 1 - aim
                     value = part_of(dim, aim)
+                    if hops == 1 and axis == order[0] and after:
+                        flows[direction] = lax.optimization_barrier((flows[direction], *after))[0]
                     if flows[direction] is not None:
                         value = value + plain(flows[direction])
-                    flows[direction] = place.step(wire(value), axis, direction, hops)
+                    sent[direction] = wire(value)
+                    flows[direction] = place.step(sent[direction], axis, direction, hops)
             total = total + plain(flows[1]) + plain(flows[-1])
+            last = (sent[1], sent[-1])
+        if axis == order[0]:
+            leaving = last
         held, first, factor = (total, 0, 1.0)
         left.remove(axis)
-    return held
+    return (held, leaving)
 
 
 SHARES = (0.42, 0.33)
@@ -339,10 +351,22 @@
     axes = list(range(len(place.digits)))[::-1]
     total = 2 * rows
     cuts = [0] + [int(total * sum(SHARES[: i + 1]) / 8 + 0.5) * 8 for i in range(2)] + [total]
-    parts = []
-    for i in range(3):
-        order = axes[i:] + axes[:i]
-        parts.append(scatter_part(place, held, cuts[i], cuts[i + 1] - cuts[i], order, scale))
+    orders = [axes[i:] + axes[:i] for i in range(3)]
+    parts, after, ahead = ([None] * 3, (), [None] * 3)
+    for i in range(2):
+        axis = orders[i][0]
+        if place.digits[axis] == 2:
+            starts = [0] * len(axes) + [cuts[i], 0]
+            starts[axis] = 1 - place.coords[axis]
+            sizes = [1 if at == axis else size for at, size in enumerate(place.digits)]
+            sent = lax.dynamic_slice(held, starts, sizes + [cuts[i + 1] - cuts[i], HALF])
+            ahead[i] = wire(jnp.squeeze(sent, axis) * scale)
+            after = (*after, ahead[i])
+    for i in (2, 0, 1):
+        span = (cuts[i], cuts[i + 1] - cuts[i])
+        hold = () if i == 0 else after
+        parts[i], leaving = scatter_part(place, held, *span, orders[i], scale, hold, ahead[i])
+        after = leaving if i == 2 else after
     unit = 1.0 / scale
     parts = [part * unit for part in parts]
     square = sum(jnp.sum(part * part) for part in parts).reshape(1, 1)

time: 613 us -> 602 us (0.982)
  the two profiles are of different devices: /device:TPU:4 before, /device:TPU:24 now
where the time goes in v4:
time: 602 us; the launch traced here: 593 us
  waiting for transfers between devices  237 us (39%)
  Pallas kernels  125 us (21%)
  starting transfers between devices  84.7 us (14%)
  other arithmetic  53.3 us (9%)
  local copies, waits for them, and re-layouts  49.5 us (8%)
  between operations  35.3 us (6%)
  matrix products  7.59 us (1%)
    all_gather x1, waiting for transfers between devices, local(): table = lax.all_gather(block, ('dp', 'rows'), axis=0, tiled=True)  132 us
    ppermute x52, waiting for transfers between devices, move(): return lax.ppermute(value, ('dp', 'rows'), pairs)  105 us
    ppermute x52, starting transfers between devices, move(): return lax.ppermute(value, ('dp', 'rows'), pairs)  84.7 us
    pallas_call x10, Pallas kernels, one_step(): pl.pallas_call(body, grid_spec=pltpu.PrefetchScalarGridSpec(num_scalar_pr...  67.4 us
    unnamed x205, local copies, waits for them, and re-layouts  27.4 us
    pallas_call x12, Pallas kernels, grad_into(): pl.pallas_call(body, grid=(tiles,), in_specs=old_specs + [pl.BlockSpec((t...  21.8 us
    convert_element_type x12, other arithmetic, wire(): return values.astype(jnp.float16)  21 us
    pallas_call x2, Pallas kernels, conv_backward(): pl.pallas_call(body, grid_spec=pltpu.PrefetchScalarGridSpec(num_scalar_pr...  17.4 us
  transfers between devices with their start and end apart: 53, of which 26 were waited for; matrix products, arithmetic and copies ran while one was open for 11% of the time, Pallas kernels for 8%

profile of v4, /device:TPU:24, one launch (start us, length us, event | category | flops | bytes accessed | tf_op | source)
XLA Modules:
  0.0 592.7 jit_solution(8124061685119073064)
XLA Ops:
  8.8 3.7 collective-permute-start.2
  12.4 3.5 collective-permute-done.2
  15.9 5.3 concatenate.176
  36.4 2.5 collective-permute-done.5
  45.9 3.3 collective-permute-done.7
  50.1 131.9 %all-gather.2.cloned.1.call-done.one_ref.two_ref.out_ref.class_ref.kv_ref.weight_ref.rows_ref.qw_ref.ow_ref.refs_5_.refs_6_.ckv_ref.refs_7_ = bf16[25344,512]{1,0:T(8,128)(2,1)} async-done(((bf16[792,512]{1,0:T(8,128)(2,1)}), bf16[25344,512]{1,0:T(8,128)(2,1)}) %all-gather.2.cloned.1.call-update) | async-done | bytes 25952272 | tf_op jit(solution)/shard_map/all_gather | solution.py:1666
  182.0 5.1 shard_map.231
  192.7 5.5 shard_map.232
  200.6 5.5 shard_map.233
  209.1 4.8 shard_map.235
  217.9 4.2 shard_map.236
  225.7 3.5 shard_map.237.fw_ref.refs_8_
  230.5 6.5 %shard_map.238 = (bf16[512,512]{1,0:T(8,128)(2,1)S(1)}, f32[512,512]{1,0:T(8,128)S(1)}, bf16[512,512]{1,0:T(8,128)(2,1)S(1)}, f32[512,2048]{1,0:T(8,128)}, bf16[512,1024]{1,0:T(8,128)(2,1)S(1)}) custom-call(s32[4]{0:T(128)S(1)} %pad_add_fusion.info_ref, bf16[512,256]{1,0:T(8,128)(2,1)S(1)} %get-tuple-element.117.mine_ref, ...), custom_call_target="tpu_custom_call" | custom-call | flops 1342177280 | bytes 14680064 | tf_op jit(solution)/shard_map/pallas_call | solution.py:833
  242.3 4.8 shard_map.239
  247.3 3.6 convolution_convert_fusion
  251.1 8.6 %shard_map.240 = (f32[72,512]{1,0:T(8,128)S(1)}, f32[8,256]{1,0:T(8,128)S(1)}, f32[512,256]{1,0:T(8,128)S(1)}, bf16[512,256]{1,0:T(8,128)(2,1)S(1)}, bf16[512,25...) custom-call(s32[4]{0:T(128)S(1)} %pad_add_fusion.info_ref, ...), custom_call_target="tpu_custom_call" | custom-call | flops 1879048192 | bytes 10829824 | tf_op jit(solution)/shard_map/pallas_call | solution.py:833
  266.8 6.4 %shard_map.244 = (f32[512,512]{1,0:T(8,128)S(1)}, bf16[512,256]{1,0:T(8,128)(2,1)S(1)}, bf16[512,256]{1,0:T(8,128)(2,1)S(1)}, f32[8,512]{1,0:T(8,128)S(1)}, f32[8,256]{1,0:T(8,128)S(1)}, /*index=5*/f32[8,512]{1,0:T(8,128)S(1)}) custom-call(s32[4]{0:T(128)S(1)} %pad_add_fusion.info_ref, f32[512,512]{1,0:T(8,128)S(1)} %get-tuple-element.134.mine_ref, ...), custom_call_target="tpu_custom_call" | custom-call | flops 1879048192 | bytes 3227648 | tf_op jit(solution)/shard_map/pallas_call | solution.py:833
  275.8 17.1 %shard_map.248 = (f32[512,512]{1,0:T(8,128)}, bf16[512,256]{1,0:T(8,128)(2,1)S(1)}, bf16[512,768]{1,0:T(8,128)(2,1)S(1)}, f32[512,512]{1,0:T(8,128)}, f32[8,256]{1,0:T(8,128)S(1)}) custom-call(s32[4]{0:T(128)S(1)} %pad_add_fusion.info_ref, bf16[512,256]{1,0:T(8,128)(2,1)S(1)} %get-tuple-element.140.refs_2_.mine_ref, ...), custom_call_target="tpu_custom_call" | custom-call | flops 3489660928 | bytes 6307840 | tf_op jit(solution)/shard_map/pallas_call | solution.py:833
  302.3 3.0 shard_map.242
  305.3 4.6 shard_map.251
  310.4 4.1 shard_map.243
  324.7 8.8 %shard_map.253 = (f32[25344,256]{1,0:T(8,128)}, bf16[512,256]{1,0:T(8,128)(2,1)S(1)}, f32[8,256]{1,0:T(8,128)S(1)}) custom-call(s32[4]{0:T(128)S(1)} %pad_add_fusion.info_ref, f32[25344,256]{1,0:T(8,128)} %get-tuple-element.159.refs_0_, bf16[512,256]{1,0:T(8,128)(2,1)S(1)} %get-tuple-element.160.refs_1_, ...), custom_call_target="tpu_custom_call", output_to_operand_aliasing={{0}: (1, {})} | custom-call | flops 2415919104 | bytes 10223616 | tf_op jit(solution)/shard_map/pallas_call | solution.py:719
  339.3 5.3 shard_map.254
  348.1 2.6 shard_map.256
  356.3 8.6 %shard_map.258 = (f32[25344,256]{1,0:T(8,128)}, bf16[512,256]{1,0:T(8,128)(2,1)S(1)}, f32[8,256]{1,0:T(8,128)S(1)}) custom-call(s32[4]{0:T(128)S(1)} %pad_add_fusion.info_ref, f32[25344,256]{1,0:T(8,128)} %broadcast_dynamic-update-slice_fusion.1.refs_0_, bf16[512,256]{1,0:T(8,128)(2,1)S(1)} %get-tuple-element.189.refs_1_, ...), custom_call_target="tpu_custom_call", output_to_operand_aliasing={{0}: (1, {})} | custom-call | flops 2415919104 | bytes 10223616 | tf_op jit(solution)/shard_map/pallas_call | solution.py:719
  366.4 3.1 collective-permute-done.26
  373.5 3.2 fusion.19
  377.4 3.3 collective-permute-start.35
  380.7 4.1 fusion.7
  384.9 4.7 fusion.6
  395.3 3.5 fusion.15
  398.8 23.5 %collective-permute-start.36 = (f16[2,2,392,256]{3,2,1,0:T(8,128)(2,1)S(1)}, f16[2,2,392,256]{3,2,1,0:T(8,128)(2,1)S(1)}, u32[]{:S(2)}, u32[]{:S(2)}) collective-permute-start(f16[2,2,392,256]{3,2,1,0:T(8,128)(2,1)S(1)} %get-tuple-element.240), channel_id=1, source_target_pairs={{16,8},{17,9},{18,10},{19,11},{20,12},{21,13},{22,14},{23,15},{24,... | collective-permute-start | bytes 2408456 | tf_op jit(solution)/shard_map/ppermute | solution.py:173
  422.3 3.8 fusion.41
  431.0 5.0 collective-permute-done.36
  437.7 5.3 collective-permute-start.42
  443.0 3.3 fusion.4
  448.8 7.8 %collective-permute-start.37 = (f16[2,528,256]{2,1,0:T(8,128)(2,1)}, f16[2,528,256]{2,1,0:T(8,128)(2,1)S(1)}, u32[]{:S(2)}, u32[]{:S(2)}) collective-permute-start(f16[2,528,256]{2,1,0:T(8,128)(2,1)} %get-tuple-element.245), channel_id=1, source_target_pairs={{0,8},{1,9},{2,10},{3,11},{4,12},{5,13},{6,14},{7,15},{8,16},{9,17... | collective-permute-start | bytes 1622024 | tf_op jit(solution)/shard_map/ppermute | solution.py:173
  457.4 3.9 fusion.1
  469.7 29.3 %collective-permute-done.38 = f16[2,528,256]{2,1,0:T(8,128)(2,1)} collective-permute-done((f16[2,528,256]{2,1,0:T(8,128)(2,1)}, f16[2,528,256]{2,1,0:T(8,128)(2,1)}, u32[]{:S(2)}, u32[]{:S(2)}) %collective-permute-start.38) | collective-permute-done | bytes 540704 | tf_op jit(solution)/shard_map/ppermute | solution.py:173
  505.6 9.6 %collective-permute-start.30 = (f16[664,256]{1,0:T(8,128)(2,1)S(1)}, f16[664,256]{1,0:T(8,128)(2,1)S(1)}, u32[]{:S(2)}, u32[]{:S(2)}) collective-permute-start(f16[664,256]{1,0:T(8,128)(2,1)S(1)} %get-tuple-element.250), channel_id=1, source_target_pairs={{0,16},{1,17},{2,18},{3,19},{4,20},{5,21},{6,22},{7,23},{8,24},{9,... | collective-permute-start | bytes 1019912 | tf_op jit(solution)/shard_map/ppermute | solution.py:173
  518.6 4.0 collective-permute-done.29
  522.7 15.3 %collective-permute-done.30 = f16[664,256]{1,0:T(8,128)(2,1)S(1)} collective-permute-done((f16[664,256]{1,0:T(8,128)(2,1)S(1)}, f16[664,256]{1,0:T(8,128)(2,1)S(1)}, u32[]{:S(2)}, u32[]{:S(2)}) %collective-permute-start.30) | collective-permute-done | bytes 340000 | tf_op jit(solution)/shard_map/ppermute | solution.py:173
  541.3 4.1 collective-permute-done.47
  545.9 4.2 collective-permute-done.48
  550.2 4.5 collective-permute-done.49
  555.0 5.7 collective-permute-done.50
  573.5 5.1 collective-permute-done.46
  580.5 3.8 multiply_add_fusion
  (478 shorter events, 134.0 us)
Async XLA Ops:
  7.2 174.9 %all-gather.2.cloned.1.call-start = ((), (), s32[]{:S(2)}) async-start(), calls=%async_computation | async-start | bytes 26763264 | tf_op jit(solution)/shard_map/all_gather | solution.py:1666
  8.8 7.2 %collective-permute-start.2 = (bf16[113664]{0:T(1024)(128)(2,1)S(1)}, bf16[113664]{0:T(1024)(128)(2,1)S(1)}, u32[]{:S(2)}, u32[]{:S(2)}) collective-permute-start(bf16[113664]{0:T(1024)(128)(2,1)S(1)} %slice.357), channel_id=1, source_target_pairs={{1,0},{2,1},{3,2},{4,3},{5,4},{6,5},{7,6},{8,7},{9,8},{10,9},{11,1... | collective-permute-start | bytes 681992 | tf_op jit(solution)/shard_map/ppermute | solution.py:173
  23.2 8.1 %collective-permute-start.3 = (bf16[1,5,128]{2,0,1:T(2,128)(2,1)S(1)}, bf16[1,5,128]{2,0,1:T(2,128)(2,1)S(1)}, u32[]{:S(2)}, u32[]{:S(2)}) collective-permute-start(bf16[1,5,128]{2,0,1:T(2,128)(2,1)S(1)} %broadcast_in_dim_reshape.3), channel_id=1, source_target_pairs={{0,1},{1,0},{2,3},{3,2},{4,5},{5,4},{6,7},{7,6},{8,9},{9,8},{10,11... | collective-permute-start | bytes 3848 | tf_op jit(solution)/shard_map/ppermute | solution.py:173
  23.4 16.4 %collective-permute-start = (f32[1,2,8,32,6]{3,2,0,4,1:T(8,128)S(1)}, f32[1,2,8,32,6]{3,2,0,4,1:T(8,128)S(1)}, u32[]{:S(2)}, u32[]{:S(2)}) collective-permute-start(f32[1,2,8,32,6]{3,2,0,4,1:T(8,128)S(1)} %maximum_bitcast_fusion), channel_id=1, source_target_pairs={{0,1},{1,0},{2,3},{3,2},{4,5},{5,4},{6,7},{7,6},{8,9},{9,8},{10,11... | collective-permute-start | bytes 36872 | tf_op jit(solution)/shard_map/ppermute | solution.py:173
  31.4 3.7 collective-permute-start.4
  35.1 3.8 collective-permute-start.5
  38.9 4.6 collective-permute-start.6
  39.8 4.7 collective-permute-start.1
  43.5 5.8 collective-permute-start.7
  206.7 2.4 collective-permute-start.10
  225.4 5.1 collective-permute-start.12
  239.6 2.7 collective-permute-start.13
  247.0 4.0 collective-permute-start.14
  264.1 2.7 collective-permute-start.15
  295.1 10.2 %collective-permute-start.17 = (f32[512,512]{1,0:T(8,128)}, f32[512,512]{1,0:T(8,128)}, u32[]{:S(2)}, u32[]{:S(2)}) collective-permute-start(f32[512,512]{1,0:T(8,128)} %get-tuple-element.153.mine_ref), channel_id=1, source_target_pairs={{0,1},{1,0},{2,3},{3,2},{4,5},{5,4},{6,7},{7,6},{8,9},{9,8},{10,11... | collective-permute-start | bytes 3145736 | tf_op jit(solution)/shard_map/ppermute | solution.py:173
  310.0 14.6 %collective-permute-start.18 = (bf16[512,256]{1,0:T(8,128)(2,1)S(1)}, bf16[512,256]{1,0:T(8,128)(2,1)S(1)}, u32[]{:S(2)}, u32[]{:S(2)}) collective-permute-start(bf16[512,256]{1,0:T(8,128)(2,1)S(1)} %get-tuple-element.160.refs_1_), channel_id=1, source_target_pairs={{0,1},{1,0},{2,3},{3,2},{4,5},{5,4},{6,7},{7,6},{8,9},{9,8},{10,11... | collective-permute-start | bytes 786440 | tf_op jit(solution)/shard_map/ppermute | solution.py:173
  315.9 21.0 %collective-permute-start.20 = (f32[8,512]{1,0:T(8,128)S(1)}, f32[8,512]{1,0:T(8,128)S(1)}, u32[]{:S(2)}, u32[]{:S(2)}) collective-permute-start(f32[8,512]{1,0:T(8,128)S(1)} %get-tuple-element.164), channel_id=1, source_target_pairs={{0,1},{1,0},{2,3},{3,2},{4,5},{5,4},{6,7},{7,6},{8,9},{9,8},{10,11... | collective-permute-start | bytes 49160 | tf_op jit(solution)/shard_map/ppermute | solution.py:173
  333.4 5.8 collective-permute-start.19
  338.9 17.3 %collective-permute-start.25 = (bf16[512,256]{1,0:T(8,128)(2,1)S(1)}, bf16[512,256]{1,0:T(8,128)(2,1)S(1)}, u32[]{:S(2)}, u32[]{:S(2)}) collective-permute-start(bf16[512,256]{1,0:T(8,128)(2,1)S(1)} %get-tuple-element.189.refs_1_), channel_id=1, source_target_pairs={{0,1},{1,0},{2,3},{3,2},{4,5},{5,4},{6,7},{7,6},{8,9},{9,8},{10,11... | collective-permute-start | bytes 786440 | tf_op jit(solution)/shard_map/ppermute | solution.py:173
  344.6 2.0 collective-permute-start.21
  346.6 4.1 collective-permute-start.22
  350.8 3.9 collective-permute-start.23
  354.7 10.3 %collective-permute-start.24 = (f32[8,128]{1,0:T(8,128)S(1)}, f32[8,128]{1,0:T(8,128)S(1)}, u32[]{:S(2)}, u32[]{:S(2)}) collective-permute-start(f32[8,128]{1,0:T(8,128)S(1)} %max.64), channel_id=1, source_target_pairs={{0,8},{1,9},{2,10},{3,11},{4,12},{5,13},{6,14},{7,15},{8,0},{9,1},... | collective-permute-start | bytes 12296 | tf_op jit(solution)/shard_map/ppermute | solution.py:173
  365.0 4.6 collective-permute-start.26
  376.7 12.9 %collective-permute-start.33 = (f16[2,2,392,256]{3,2,1,0:T(8,128)(2,1)S(1)}, f16[2,2,392,256]{3,2,1,0:T(8,128)(2,1)S(1)}, u32[]{:S(2)}, u32[]{:S(2)}) collective-permute-start(f16[2,2,392,256]{3,2,1,0:T(8,128)(2,1)S(1)} %get-tuple-element.241), channel_id=1, source_target_pairs={{0,8},{1,9},{2,10},{3,11},{4,12},{5,13},{6,14},{7,15}} | collective-permute-start | bytes 2408456 | tf_op jit(solution)/shard_map/ppermute | solution.py:173
  377.4 17.9 %collective-permute-start.35 = (f16[2,2,392,256]{3,2,1,0:T(8,128)(2,1)}, f16[2,2,392,256]{3,2,1,0:T(8,128)(2,1)}, u32[]{:S(2)}, u32[]{:S(2)}) collective-permute-start(f16[2,2,392,256]{3,2,1,0:T(8,128)(2,1)} %get-tuple-element.242), channel_id=1, source_target_pairs={{24,16},{25,17},{26,18},{27,19},{28,20},{29,21},{30,22},{31,23}} | collective-permute-start | bytes 2408456 | tf_op jit(solution)/shard_map/ppermute | solution.py:173
  391.3 4.0 collective-permute-start.34
  392.3 64.4 %collective-permute-start.27 = (f16[4,2,664,256]{3,2,1,0:T(8,128)(2,1)}, f16[4,2,664,256]{3,2,1,0:T(8,128)(2,1)}, u32[]{:S(2)}, u32[]{:S(2)}) collective-permute-start(f16[4,2,664,256]{3,2,1,0:T(8,128)(2,1)} %fusion.6), channel_id=1, source_target_pairs={{0,2},{1,3},{2,0},{3,1},{4,6},{5,7},{6,4},{7,5},{8,10},{9,11},{10,... | collective-permute-start | bytes 8159240 | tf_op jit(solution)/shard_map/ppermute | solution.py:173
  393.6 49.4 %collective-permute-start.32 = (f16[4,2,528,256]{3,2,1,0:T(8,128)(2,1)}, f16[4,2,528,256]{3,2,1,0:T(8,128)(2,1)}, u32[]{:S(2)}, u32[]{:S(2)}) collective-permute-start(f16[4,2,528,256]{3,2,1,0:T(8,128)(2,1)} %fusion.7), channel_id=1, source_target_pairs={{0,4},{1,5},{2,6},{3,7},{4,0},{5,1},{6,2},{7,3},{8,12},{9,13},{10,... | collective-permute-start | bytes 6488072 | tf_op jit(solution)/shard_map/ppermute | solution.py:173
  398.8 37.2 %collective-permute-start.36 = (f16[2,2,392,256]{3,2,1,0:T(8,128)(2,1)S(1)}, f16[2,2,392,256]{3,2,1,0:T(8,128)(2,1)S(1)}, u32[]{:S(2)}, u32[]{:S(2)}) collective-permute-start(f16[2,2,392,256]{3,2,1,0:T(8,128)(2,1)S(1)} %get-tuple-element.240), channel_id=1, source_target_pairs={{16,8},{17,9},{18,10},{19,11},{20,12},{21,13},{22,14},{23,15},{24,... | collective-permute-start | bytes 2408456 | tf_op jit(solution)/shard_map/ppermute | solution.py:173
  429.7 32.0 %collective-permute-start.41 = (f16[2,2,392,256]{3,2,1,0:T(8,128)(2,1)}, f16[2,2,392,256]{3,2,1,0:T(8,128)(2,1)S(1)}, u32[]{:S(2)}, u32[]{:S(2)}) collective-permute-start(f16[2,2,392,256]{3,2,1,0:T(8,128)(2,1)} %get-tuple-element.239), channel_id=1, source_target_pairs={{0,8},{1,9},{2,10},{3,11},{4,12},{5,13},{6,14},{7,15},{8,16},{9,17... | collective-permute-start | bytes 2408456 | tf_op jit(solution)/shard_map/ppermute | solution.py:173
  437.7 27.0 %collective-permute-start.42 = (f16[2,2,392,256]{3,2,1,0:T(8,128)(2,1)S(1)}, f16[2,2,392,256]{3,2,1,0:T(8,128)(2,1)}, u32[]{:S(2)}, u32[]{:S(2)}) collective-permute-start(f16[2,2,392,256]{3,2,1,0:T(8,128)(2,1)S(1)} %fusion.13), channel_id=1, source_target_pairs={{8,0},{9,1},{10,2},{11,3},{12,4},{13,5},{14,6},{15,7},{16,8},{17,9... | collective-permute-start | bytes 2408456 | tf_op jit(solution)/shard_map/ppermute | solution.py:173
  448.8 20.9 %collective-permute-start.37 = (f16[2,528,256]{2,1,0:T(8,128)(2,1)}, f16[2,528,256]{2,1,0:T(8,128)(2,1)S(1)}, u32[]{:S(2)}, u32[]{:S(2)}) collective-permute-start(f16[2,528,256]{2,1,0:T(8,128)(2,1)} %get-tuple-element.245), channel_id=1, source_target_pairs={{0,8},{1,9},{2,10},{3,11},{4,12},{5,13},{6,14},{7,15},{8,16},{9,17... | collective-permute-start | bytes 1622024 | tf_op jit(solution)/shard_map/ppermute | solution.py:173
  456.6 42.4 %collective-permute-start.38 = (f16[2,528,256]{2,1,0:T(8,128)(2,1)}, f16[2,528,256]{2,1,0:T(8,128)(2,1)}, u32[]{:S(2)}, u32[]{:S(2)}) collective-permute-start(f16[2,528,256]{2,1,0:T(8,128)(2,1)} %get-tuple-element.247), channel_id=1, source_target_pairs={{0,16},{1,17},{2,18},{3,19},{4,20},{5,21},{6,22},{7,23},{8,24},{9,... | collective-permute-start | bytes 1622024 | tf_op jit(solution)/shard_map/ppermute | solution.py:173
  456.6 42.4 %collective-permute-start.39 = (f16[2,528,256]{2,1,0:T(8,128)(2,1)}, f16[2,528,256]{2,1,0:T(8,128)(2,1)}, u32[]{:S(2)}, u32[]{:S(2)}) collective-permute-start(f16[2,528,256]{2,1,0:T(8,128)(2,1)} %get-tuple-element.246), channel_id=1, source_target_pairs={{0,24},{1,25},{2,26},{3,27},{4,28},{5,29},{6,30},{7,31},{8,0},{9,1... | collective-permute-start | bytes 1622024 | tf_op jit(solution)/shard_map/ppermute | solution.py:173
  461.7 41.7 %collective-permute-start.28 = (f16[4,664,256]{2,1,0:T(8,128)(2,1)S(1)}, f16[4,664,256]{2,1,0:T(8,128)(2,1)}, u32[]{:S(2)}, u32[]{:S(2)}) collective-permute-start(f16[4,664,256]{2,1,0:T(8,128)(2,1)S(1)} %fusion.16), channel_id=1, source_target_pairs={{0,4},{1,5},{2,6},{3,7},{4,0},{5,1},{6,2},{7,3},{8,12},{9,13},{10,... | collective-permute-start | bytes 4079624 | tf_op jit(solution)/shard_map/ppermute | solution.py:173
  466.9 34.5 %collective-permute-start.43 = (f16[2,392,256]{2,1,0:T(8,128)(2,1)S(1)}, f16[2,392,256]{2,1,0:T(8,128)(2,1)S(1)}, u32[]{:S(2)}, u32[]{:S(2)}) collective-permute-start(f16[2,392,256]{2,1,0:T(8,128)(2,1)S(1)} %fusion.29), channel_id=1, source_target_pairs={{0,2},{1,3},{2,0},{3,1},{4,6},{5,7},{6,4},{7,5},{8,10},{9,11},{10,... | collective-permute-start | bytes 1204232 | tf_op jit(solution)/shard_map/ppermute | solution.py:173
  501.1 16.1 %collective-permute-start.40 = (f16[528,256]{1,0:T(8,128)(2,1)S(1)}, f16[528,256]{1,0:T(8,128)(2,1)S(1)}, u32[]{:S(2)}, u32[]{:S(2)}) collective-permute-start(f16[528,256]{1,0:T(8,128)(2,1)S(1)} %fusion.34), channel_id=1, source_target_pairs={{0,2},{1,3},{2,0},{3,1},{4,6},{5,7},{6,4},{7,5},{8,10},{9,11},{10,... | collective-permute-start | bytes 811016 | tf_op jit(solution)/shard_map/ppermute | solution.py:173
  501.6 16.3 %collective-permute-start.44 = (f16[392,256]{1,0:T(8,128)(2,1)S(1)}, f16[392,256]{1,0:T(8,128)(2,1)S(1)}, u32[]{:S(2)}, u32[]{:S(2)}) collective-permute-start(f16[392,256]{1,0:T(8,128)(2,1)S(1)} %fusion.35), channel_id=1, source_target_pairs={{0,4},{1,5},{2,6},{3,7},{4,0},{5,1},{6,2},{7,3},{8,12},{9,13},{10,... | collective-permute-start | bytes 602120 | tf_op jit(solution)/shard_map/ppermute | solution.py:173
  505.3 17.3 %collective-permute-start.29 = (f16[664,256]{1,0:T(8,128)(2,1)S(1)}, f16[664,256]{1,0:T(8,128)(2,1)S(1)}, u32[]{:S(2)}, u32[]{:S(2)}) collective-permute-start(f16[664,256]{1,0:T(8,128)(2,1)S(1)} %get-tuple-element.248), channel_id=1, source_target_pairs={{0,8},{1,9},{2,10},{3,11},{4,12},{5,13},{6,14},{7,15},{8,16},{9,17... | collective-permute-start | bytes 1019912 | tf_op jit(solution)/shard_map/ppermute | solution.py:173
  505.6 32.3 %collective-permute-start.30 = (f16[664,256]{1,0:T(8,128)(2,1)S(1)}, f16[664,256]{1,0:T(8,128)(2,1)S(1)}, u32[]{:S(2)}, u32[]{:S(2)}) collective-permute-start(f16[664,256]{1,0:T(8,128)(2,1)S(1)} %get-tuple-element.250), channel_id=1, source_target_pairs={{0,16},{1,17},{2,18},{3,19},{4,20},{5,21},{6,22},{7,23},{8,24},{9,... | collective-permute-start | bytes 1019912 | tf_op jit(solution)/shard_map/ppermute | solution.py:173
  515.2 22.7 %collective-permute-start.31 = (f16[664,256]{1,0:T(8,128)(2,1)S(1)}, f16[664,256]{1,0:T(8,128)(2,1)S(1)}, u32[]{:S(2)}, u32[]{:S(2)}) collective-permute-start(f16[664,256]{1,0:T(8,128)(2,1)S(1)} %get-tuple-element.249), channel_id=1, source_target_pairs={{0,24},{1,25},{2,26},{3,27},{4,28},{5,29},{6,30},{7,31},{8,0},{9,1... | collective-permute-start | bytes 1019912 | tf_op jit(solution)/shard_map/ppermute | solution.py:173
  540.9 4.6 collective-permute-start.47
  545.5 4.6 collective-permute-start.48
  550.2 4.6 collective-permute-start.49
  554.8 5.9 collective-permute-start.50
  560.8 5.0 collective-permute-start.45
  567.2 11.4 %collective-permute-start.46 = (f32[109568]{0:T(1024)S(1)}, f32[109568]{0:T(1024)S(1)}, u32[]{:S(2)}, u32[]{:S(2)}) collective-permute-start(f32[109568]{0:T(1024)S(1)} %slice.323), channel_id=1, source_target_pairs={{0,1},{1,2},{2,3},{3,4},{4,5},{5,6},{6,7},{7,8},{8,9},{9,10},{10,1... | collective-permute-start | bytes 1314824 | tf_op jit(solution)/shard_map/ppermute | solution.py:173
  (103 other events, 1037.4 us)
Sparse Core Ops, SparseCore 0:
  23.3 158.6 all-gather.1

commit v5 on v4

--- a/solution.py
+++ b/solution.py
@@ -213,8 +213,12 @@
     def chip_sum(self, value):
         stride = 2
         while stride < self.count:
-            value = value + self.swap(value, stride)
-            stride *= 2
+            if 2 * stride < self.count:
+                near, far, both = [self.swap(value, stride * n) for n in (1, 2, 3)]
+                value = (value + near) + (far + both)
+            else:
+                value = value + self.swap(value, stride)
+            stride *= 4
         return value
 
 
@@ -280,11 +284,16 @@
 
     def exchange(self, beside=None):
         if self.stride < self.place.count:
-            got = self.place.swap(self.values, self.stride)
+            several = self.stride > 1 and 2 * self.stride < self.place.count
+            times = (1, 2, 3) if several else (1,)
+            got = [self.place.swap(self.values, self.stride * n) for n in times]
             if beside is not None:
-                got, beside = lax.optimization_barrier((got, beside))
-            self.values = lax.optimization_barrier(jnp.maximum(self.values, got))
-            self.stride *= 2
+                *got, beside = lax.optimization_barrier((*got, beside))
+            values = self.values
+            for one in got:
+                values = jnp.maximum(values, one)
+            self.values = lax.optimization_barrier(values)
+            self.stride *= 4 if several else 2
         return beside
 
     def finish(self):

time: 602 us -> 598 us (level)
  the two profiles are of different devices: /device:TPU:24 before, /device:TPU:4 now
where the time goes in v5:
time: 598 us; the launch traced here: 588 us
  waiting for transfers between devices  243 us (41%)
  Pallas kernels  125 us (21%)
  starting transfers between devices  74.6 us (12%)
  other arithmetic  53.3 us (9%)
  local copies, waits for them, and re-layouts  49.4 us (8%)
  between operations  35.4 us (6%)
  matrix products  7.6 us (1%)
    all_gather x1, waiting for transfers between devices, local(): table = lax.all_gather(block, ('dp', 'rows'), axis=0, tiled=True)  134 us
    ppermute x56, waiting for transfers between devices, move(): return lax.ppermute(value, ('dp', 'rows'), pairs)  109 us
    ppermute x56, starting transfers between devices, move(): return lax.ppermute(value, ('dp', 'rows'), pairs)  74.5 us
    pallas_call x10, Pallas kernels, one_step(): pl.pallas_call(body, grid_spec=pltpu.PrefetchScalarGridSpec(num_scalar_pr...  67.4 us
    unnamed x203, local copies, waits for them, and re-layouts  26.6 us
    pallas_call x12, Pallas kernels, grad_into(): pl.pallas_call(body, grid=(tiles,), in_specs=old_specs + [pl.BlockSpec((t...  21.9 us
    convert_element_type x12, other arithmetic, wire(): return values.astype(jnp.float16)  21 us
    pallas_call x2, Pallas kernels, conv_backward(): pl.pallas_call(body, grid_spec=pltpu.PrefetchScalarGridSpec(num_scalar_pr...  17.4 us
  transfers between devices with their start and end apart: 57, of which 29 were waited for; matrix products, arithmetic and copies ran while one was open for 11% of the time, Pallas kernels for 7%

profile of v5, /device:TPU:4, one launch (start us, length us, event | category | flops | bytes accessed | tf_op | source)
XLA Modules:
  0.0 588.4 jit_solution(469111076791456840)
XLA Ops:
  8.8 2.8 collective-permute-start.2
  11.5 3.5 collective-permute-done.2
  15.0 5.3 concatenate.176
  31.1 3.3 collective-permute-start.4
  36.1 3.7 collective-permute-done.5
  50.3 133.9 %all-gather.2.cloned.1.call-done.one_ref.two_ref.out_ref.class_ref.kv_ref.weight_ref.rows_ref.qw_ref.ow_ref.refs_5_.refs_6_.ckv_ref.refs_7_ = bf16[25344,512]{1,0:T(8,128)(2,1)} async-done(((bf16[792,512]{1,0:T(8,128)(2,1)}), bf16[25344,512]{1,0:T(8,128)(2,1)}) %all-gather.2.cloned.1.call-update) | async-done | bytes 25952272 | tf_op jit(solution)/shard_map/all_gather | solution.py:1675
  184.2 5.1 shard_map.231
  194.9 5.5 shard_map.232
  202.8 5.5 shard_map.233
  211.2 4.8 shard_map.235
  220.1 4.2 shard_map.236
  227.9 3.5 shard_map.237.fw_ref.refs_8_
  232.7 6.5 %shard_map.238 = (bf16[512,512]{1,0:T(8,128)(2,1)S(1)}, f32[512,512]{1,0:T(8,128)S(1)}, bf16[512,512]{1,0:T(8,128)(2,1)S(1)}, f32[512,2048]{1,0:T(8,128)}, bf16[512,1024]{1,0:T(8,128)(2,1)S(1)}) custom-call(s32[4]{0:T(128)S(1)} %pad_add_fusion.info_ref, bf16[512,256]{1,0:T(8,128)(2,1)S(1)} %get-tuple-element.119.mine_ref, ...), custom_call_target="tpu_custom_call" | custom-call | flops 1342177280 | bytes 14680064 | tf_op jit(solution)/shard_map/pallas_call | solution.py:842
  244.4 4.8 shard_map.239
  249.5 3.6 convolution_convert_fusion
  253.3 8.6 %shard_map.240 = (f32[72,512]{1,0:T(8,128)S(1)}, f32[8,256]{1,0:T(8,128)S(1)}, f32[512,256]{1,0:T(8,128)S(1)}, bf16[512,256]{1,0:T(8,128)(2,1)S(1)}, bf16[512,25...) custom-call(s32[4]{0:T(128)S(1)} %pad_add_fusion.info_ref, ...), custom_call_target="tpu_custom_call" | custom-call | flops 1879048192 | bytes 10829824 | tf_op jit(solution)/shard_map/pallas_call | solution.py:842
  268.9 6.4 %shard_map.244 = (f32[512,512]{1,0:T(8,128)S(1)}, bf16[512,256]{1,0:T(8,128)(2,1)S(1)}, bf16[512,256]{1,0:T(8,128)(2,1)S(1)}, f32[8,512]{1,0:T(8,128)S(1)}, f32[8,256]{1,0:T(8,128)S(1)}, /*index=5*/f32[8,512]{1,0:T(8,128)S(1)}) custom-call(s32[4]{0:T(128)S(1)} %pad_add_fusion.info_ref, f32[512,512]{1,0:T(8,128)S(1)} %get-tuple-element.136.mine_ref, ...), custom_call_target="tpu_custom_call" | custom-call | flops 1879048192 | bytes 3227648 | tf_op jit(solution)/shard_map/pallas_call | solution.py:842
  277.9 17.1 %shard_map.248 = (f32[512,512]{1,0:T(8,128)}, bf16[512,256]{1,0:T(8,128)(2,1)S(1)}, bf16[512,768]{1,0:T(8,128)(2,1)S(1)}, f32[512,512]{1,0:T(8,128)}, f32[8,256]{1,0:T(8,128)S(1)}) custom-call(s32[4]{0:T(128)S(1)} %pad_add_fusion.info_ref, bf16[512,256]{1,0:T(8,128)(2,1)S(1)} %get-tuple-element.142.refs_2_.mine_ref, ...), custom_call_target="tpu_custom_call" | custom-call | flops 3489660928 | bytes 6307840 | tf_op jit(solution)/shard_map/pallas_call | solution.py:842
  304.5 3.0 shard_map.242
  307.6 4.6 shard_map.251
  312.5 4.1 shard_map.243
  326.9 8.8 %shard_map.253 = (f32[25344,256]{1,0:T(8,128)}, bf16[512,256]{1,0:T(8,128)(2,1)S(1)}, f32[8,256]{1,0:T(8,128)S(1)}) custom-call(s32[4]{0:T(128)S(1)} %pad_add_fusion.info_ref, f32[25344,256]{1,0:T(8,128)} %get-tuple-element.161.refs_0_, bf16[512,256]{1,0:T(8,128)(2,1)S(1)} %get-tuple-element.162.refs_1_, ...), custom_call_target="tpu_custom_call", output_to_operand_aliasing={{0}: (1, {})} | custom-call | flops 2415919104 | bytes 10223616 | tf_op jit(solution)/shard_map/pallas_call | solution.py:728
  341.5 5.3 shard_map.254
  352.3 2.7 shard_map.256
  366.8 8.7 %shard_map.258 = (f32[25344,256]{1,0:T(8,128)}, bf16[512,256]{1,0:T(8,128)(2,1)S(1)}, f32[8,256]{1,0:T(8,128)S(1)}) custom-call(s32[4]{0:T(128)S(1)} %pad_add_fusion.info_ref, f32[25344,256]{1,0:T(8,128)} %broadcast_dynamic-update-slice_fusion.1.refs_0_, bf16[512,256]{1,0:T(8,128)(2,1)S(1)} %get-tuple-element.192.refs_1_, ...), custom_call_target="tpu_custom_call", output_to_operand_aliasing={{0}: (1, {})} | custom-call | flops 2415919104 | bytes 10223616 | tf_op jit(solution)/shard_map/pallas_call | solution.py:728
  375.4 3.2 fusion.19
  382.0 4.1 fusion.7
  386.1 4.7 fusion.6
  390.8 4.9 collective-permute-done.35
  397.4 4.7 collective-permute-start.36
  404.4 12.0 %collective-permute-done.36 = f16[2,2,392,256]{3,2,1,0:T(8,128)(2,1)S(1)} collective-permute-done((f16[2,2,392,256]{3,2,1,0:T(8,128)(2,1)S(1)}, f16[2,2,392,256]{3,2,1,0:T(8,128)(2,1)S(1)}, u32[]{:S(2)}, u32[]{:S(2)}) %collective-permute-start.36) | collective-permute-done | bytes 802848 | tf_op jit(solution)/shard_map/ppermute | solution.py:173
  416.4 3.5 fusion.15
  420.6 3.8 fusion.41
  428.0 5.1 collective-permute-start.43
  436.0 12.8 %collective-permute-done.34 = f16[4,2,528,256]{3,2,1,0:T(8,128)(2,1)} collective-permute-done((f16[4,2,528,256]{3,2,1,0:T(8,128)(2,1)}, f16[4,2,528,256]{3,2,1,0:T(8,128)(2,1)}, u32[]{:S(2)}, u32[]{:S(2)}) %collective-permute-start.34) | collective-permute-done | bytes 2162720 | tf_op jit(solution)/shard_map/ppermute | solution.py:173
  448.8 3.3 fusion.4
  454.9 5.5 collective-permute-done.29
  460.4 3.9 fusion.1
  467.6 5.0 collective-permute-done.44
  475.1 23.3 %collective-permute-done.40 = f16[2,528,256]{2,1,0:T(8,128)(2,1)} collective-permute-done((f16[2,528,256]{2,1,0:T(8,128)(2,1)}, f16[2,528,256]{2,1,0:T(8,128)(2,1)}, u32[]{:S(2)}, u32[]{:S(2)}) %collective-permute-start.40) | collective-permute-done | bytes 540704 | tf_op jit(solution)/shard_map/ppermute | solution.py:173
  503.9 11.7 %collective-permute-start.31 = (f16[664,256]{1,0:T(8,128)(2,1)S(1)}, f16[664,256]{1,0:T(8,128)(2,1)S(1)}, u32[]{:S(2)}, u32[]{:S(2)}) collective-permute-start(f16[664,256]{1,0:T(8,128)(2,1)S(1)} %get-tuple-element.252), channel_id=1, source_target_pairs={{0,8},{1,9},{2,10},{3,11},{4,12},{5,13},{6,14},{7,15},{8,16},{9,17... | collective-permute-start | bytes 1019912 | tf_op jit(solution)/shard_map/ppermute | solution.py:173
  522.1 8.7 %collective-permute-done.32 = f16[664,256]{1,0:T(8,128)(2,1)S(1)} collective-permute-done((f16[664,256]{1,0:T(8,128)(2,1)S(1)}, f16[664,256]{1,0:T(8,128)(2,1)S(1)}, u32[]{:S(2)}, u32[]{:S(2)}) %collective-permute-start.32) | collective-permute-done | bytes 340000 | tf_op jit(solution)/shard_map/ppermute | solution.py:173
  541.8 5.8 collective-permute-start.52
  547.5 3.4 collective-permute-start.53
  551.0 3.3 collective-permute-done.53
  554.4 2.9 collective-permute-done.54
  570.0 4.2 collective-permute-done.48
  576.2 3.8 multiply_add_fusion
  (480 shorter events, 144.1 us)
Async XLA Ops:
  7.2 177.0 %all-gather.2.cloned.1.call-start = ((), (), s32[]{:S(2)}) async-start(), calls=%async_computation | async-start | bytes 26763264 | tf_op jit(solution)/shard_map/all_gather | solution.py:1675
  8.8 6.3 %collective-permute-start.2 = (bf16[113664]{0:T(1024)(128)(2,1)S(1)}, bf16[113664]{0:T(1024)(128)(2,1)S(1)}, u32[]{:S(2)}, u32[]{:S(2)}) collective-permute-start(bf16[113664]{0:T(1024)(128)(2,1)S(1)} %slice.357), channel_id=1, source_target_pairs={{1,0},{2,1},{3,2},{4,3},{5,4},{6,5},{7,6},{8,7},{9,8},{10,9},{11,1... | collective-permute-start | bytes 681992 | tf_op jit(solution)/shard_map/ppermute | solution.py:173
  22.3 8.7 %collective-permute-start.3 = (bf16[1,5,128]{2,0,1:T(2,128)(2,1)S(1)}, bf16[1,5,128]{2,0,1:T(2,128)(2,1)S(1)}, u32[]{:S(2)}, u32[]{:S(2)}) collective-permute-start(bf16[1,5,128]{2,0,1:T(2,128)(2,1)S(1)} %broadcast_in_dim_reshape.3), channel_id=1, source_target_pairs={{0,1},{1,0},{2,3},{3,2},{4,5},{5,4},{6,7},{7,6},{8,9},{9,8},{10,11... | collective-permute-start | bytes 3848 | tf_op jit(solution)/shard_map/ppermute | solution.py:173
  23.3 18.1 %collective-permute-start = (f32[1,2,8,32,6]{3,2,0,4,1:T(8,128)S(1)}, f32[1,2,8,32,6]{3,2,0,4,1:T(8,128)S(1)}, u32[]{:S(2)}, u32[]{:S(2)}) collective-permute-start(f32[1,2,8,32,6]{3,2,0,4,1:T(8,128)S(1)} %maximum_bitcast_fusion), channel_id=1, source_target_pairs={{0,1},{1,0},{2,3},{3,2},{4,5},{5,4},{6,7},{7,6},{8,9},{9,8},{10,11... | collective-permute-start | bytes 36872 | tf_op jit(solution)/shard_map/ppermute | solution.py:173
  31.1 4.9 collective-permute-start.4
  36.0 3.8 collective-permute-start.5
  39.8 4.0 collective-permute-start.6
  41.5 4.9 collective-permute-start.1
  43.8 5.7 collective-permute-start.7
  227.5 5.2 collective-permute-start.12
  249.2 4.0 collective-permute-start.14
  296.6 11.0 %collective-permute-start.17 = (f32[512,512]{1,0:T(8,128)}, f32[512,512]{1,0:T(8,128)}, u32[]{:S(2)}, u32[]{:S(2)}) collective-permute-start(f32[512,512]{1,0:T(8,128)} %get-tuple-element.155.mine_ref), channel_id=1, source_target_pairs={{0,1},{1,0},{2,3},{3,2},{4,5},{5,4},{6,7},{7,6},{8,9},{9,8},{10,11... | collective-permute-start | bytes 3145736 | tf_op jit(solution)/shard_map/ppermute | solution.py:173
  312.2 14.6 %collective-permute-start.18 = (bf16[512,256]{1,0:T(8,128)(2,1)S(1)}, bf16[512,256]{1,0:T(8,128)(2,1)S(1)}, u32[]{:S(2)}, u32[]{:S(2)}) collective-permute-start(bf16[512,256]{1,0:T(8,128)(2,1)S(1)} %get-tuple-element.162.refs_1_), channel_id=1, source_target_pairs={{0,1},{1,0},{2,3},{3,2},{4,5},{5,4},{6,7},{7,6},{8,9},{9,8},{10,11... | collective-permute-start | bytes 786440 | tf_op jit(solution)/shard_map/ppermute | solution.py:173
  318.1 21.0 %collective-permute-start.20 = (f32[8,512]{1,0:T(8,128)S(1)}, f32[8,512]{1,0:T(8,128)S(1)}, u32[]{:S(2)}, u32[]{:S(2)}) collective-permute-start(f32[8,512]{1,0:T(8,128)S(1)} %get-tuple-element.166), channel_id=1, source_target_pairs={{0,1},{1,0},{2,3},{3,2},{4,5},{5,4},{6,7},{7,6},{8,9},{9,8},{10,11... | collective-permute-start | bytes 49160 | tf_op jit(solution)/shard_map/ppermute | solution.py:173
  335.7 5.8 collective-permute-start.19
  341.1 25.6 %collective-permute-start.28 = (bf16[512,256]{1,0:T(8,128)(2,1)S(1)}, bf16[512,256]{1,0:T(8,128)(2,1)S(1)}, u32[]{:S(2)}, u32[]{:S(2)}) collective-permute-start(bf16[512,256]{1,0:T(8,128)(2,1)S(1)} %get-tuple-element.192.refs_1_), channel_id=1, source_target_pairs={{0,1},{1,0},{2,3},{3,2},{4,5},{5,4},{6,7},{7,6},{8,9},{9,8},{10,11... | collective-permute-start | bytes 786440 | tf_op jit(solution)/shard_map/ppermute | solution.py:173
  348.8 6.2 %collective-permute-start.22 = (f32[8,128]{1,0:T(8,128)S(1)}, f32[8,128]{1,0:T(8,128)S(1)}, u32[]{:S(2)}, u32[]{:S(2)}) collective-permute-start(f32[8,128]{1,0:T(8,128)S(1)} %max.68), channel_id=1, source_target_pairs={{0,2},{1,3},{2,0},{3,1},{4,6},{5,7},{6,4},{7,5},{8,10},{9,11},{10,... | collective-permute-start | bytes 12296 | tf_op jit(solution)/shard_map/ppermute | solution.py:173
  349.3 5.6 collective-permute-start.23
  350.8 4.5 collective-permute-start.24
  355.3 7.4 %collective-permute-start.25 = (f32[8,128]{1,0:T(8,128)S(1)}, f32[8,128]{1,0:T(8,128)S(1)}, u32[]{:S(2)}, u32[]{:S(2)}) collective-permute-start(f32[8,128]{1,0:T(8,128)S(1)} %maximum_maximum_fusion.1), channel_id=1, source_target_pairs={{0,8},{1,9},{2,10},{3,11},{4,12},{5,13},{6,14},{7,15},{8,0},{9,1},... | collective-permute-start | bytes 12296 | tf_op jit(solution)/shard_map/ppermute | solution.py:173
  355.4 7.3 %collective-permute-start.26 = (f32[8,128]{1,0:T(8,128)S(1)}, f32[8,128]{1,0:T(8,128)S(1)}, u32[]{:S(2)}, u32[]{:S(2)}) collective-permute-start(f32[8,128]{1,0:T(8,128)S(1)} %maximum_maximum_fusion.1), channel_id=1, source_target_pairs={{0,16},{1,17},{2,18},{3,19},{4,20},{5,21},{6,22},{7,23},{8,24},{9,... | collective-permute-start | bytes 12296 | tf_op jit(solution)/shard_map/ppermute | solution.py:173
  357.3 5.4 collective-permute-start.27
  378.6 17.2 %collective-permute-start.35 = (f16[2,2,392,256]{3,2,1,0:T(8,128)(2,1)S(1)}, f16[2,2,392,256]{3,2,1,0:T(8,128)(2,1)S(1)}, u32[]{:S(2)}, u32[]{:S(2)}) collective-permute-start(f16[2,2,392,256]{3,2,1,0:T(8,128)(2,1)S(1)} %get-tuple-element.245), channel_id=1, source_target_pairs={{0,8},{1,9},{2,10},{3,11},{4,12},{5,13},{6,14},{7,15}} | collective-permute-start | bytes 2408456 | tf_op jit(solution)/shard_map/ppermute | solution.py:173
  380.4 24.0 %collective-permute-start.37 = (f16[2,2,392,256]{3,2,1,0:T(8,128)(2,1)}, f16[2,2,392,256]{3,2,1,0:T(8,128)(2,1)}, u32[]{:S(2)}, u32[]{:S(2)}) collective-permute-start(f16[2,2,392,256]{3,2,1,0:T(8,128)(2,1)} %get-tuple-element.246), channel_id=1, source_target_pairs={{24,16},{25,17},{26,18},{27,19},{28,20},{29,21},{30,22},{31,23}} | collective-permute-start | bytes 2408456 | tf_op jit(solution)/shard_map/ppermute | solution.py:173
  397.4 19.0 %collective-permute-start.36 = (f16[2,2,392,256]{3,2,1,0:T(8,128)(2,1)S(1)}, f16[2,2,392,256]{3,2,1,0:T(8,128)(2,1)S(1)}, u32[]{:S(2)}, u32[]{:S(2)}) collective-permute-start(f16[2,2,392,256]{3,2,1,0:T(8,128)(2,1)S(1)} %fusion.14), channel_id=1, source_target_pairs={{0,8},{1,9},{2,10},{3,11},{4,12},{5,13},{6,14},{7,15},{8,16},{9,17... | collective-permute-start | bytes 2408456 | tf_op jit(solution)/shard_map/ppermute | solution.py:173
  402.2 58.3 %collective-permute-start.29 = (f16[4,2,664,256]{3,2,1,0:T(8,128)(2,1)}, f16[4,2,664,256]{3,2,1,0:T(8,128)(2,1)}, u32[]{:S(2)}, u32[]{:S(2)}) collective-permute-start(f16[4,2,664,256]{3,2,1,0:T(8,128)(2,1)} %fusion.6), channel_id=1, source_target_pairs={{0,2},{1,3},{2,0},{3,1},{4,6},{5,7},{6,4},{7,5},{8,10},{9,11},{10,... | collective-permute-start | bytes 8159240 | tf_op jit(solution)/shard_map/ppermute | solution.py:173
  402.9 46.0 %collective-permute-start.34 = (f16[4,2,528,256]{3,2,1,0:T(8,128)(2,1)}, f16[4,2,528,256]{3,2,1,0:T(8,128)(2,1)}, u32[]{:S(2)}, u32[]{:S(2)}) collective-permute-start(f16[4,2,528,256]{3,2,1,0:T(8,128)(2,1)} %fusion.7), channel_id=1, source_target_pairs={{0,4},{1,5},{2,6},{3,7},{4,0},{5,1},{6,2},{7,3},{8,12},{9,13},{10,... | collective-permute-start | bytes 6488072 | tf_op jit(solution)/shard_map/ppermute | solution.py:173
  419.9 13.1 %collective-permute-start.38 = (f16[2,2,392,256]{3,2,1,0:T(8,128)(2,1)S(1)}, f16[2,2,392,256]{3,2,1,0:T(8,128)(2,1)S(1)}, u32[]{:S(2)}, u32[]{:S(2)}) collective-permute-start(f16[2,2,392,256]{3,2,1,0:T(8,128)(2,1)S(1)} %get-tuple-element.244), channel_id=1, source_target_pairs={{16,8},{17,9},{18,10},{19,11},{20,12},{21,13},{22,14},{23,15},{24,... | collective-permute-start | bytes 2408456 | tf_op jit(solution)/shard_map/ppermute | solution.py:173
  428.0 36.7 %collective-permute-start.43 = (f16[2,2,392,256]{3,2,1,0:T(8,128)(2,1)}, f16[2,2,392,256]{3,2,1,0:T(8,128)(2,1)S(1)}, u32[]{:S(2)}, u32[]{:S(2)}) collective-permute-start(f16[2,2,392,256]{3,2,1,0:T(8,128)(2,1)} %get-tuple-element.243), channel_id=1, source_target_pairs={{0,8},{1,9},{2,10},{3,11},{4,12},{5,13},{6,14},{7,15},{8,16},{9,17... | collective-permute-start | bytes 2408456 | tf_op jit(solution)/shard_map/ppermute | solution.py:173
  434.7 37.9 %collective-permute-start.44 = (f16[2,2,392,256]{3,2,1,0:T(8,128)(2,1)S(1)}, f16[2,2,392,256]{3,2,1,0:T(8,128)(2,1)}, u32[]{:S(2)}, u32[]{:S(2)}) collective-permute-start(f16[2,2,392,256]{3,2,1,0:T(8,128)(2,1)S(1)} %fusion.13), channel_id=1, source_target_pairs={{8,0},{9,1},{10,2},{11,3},{12,4},{13,5},{14,6},{15,7},{16,8},{17,9... | collective-permute-start | bytes 2408456 | tf_op jit(solution)/shard_map/ppermute | solution.py:173
  454.6 20.4 %collective-permute-start.39 = (f16[2,528,256]{2,1,0:T(8,128)(2,1)}, f16[2,528,256]{2,1,0:T(8,128)(2,1)S(1)}, u32[]{:S(2)}, u32[]{:S(2)}) collective-permute-start(f16[2,528,256]{2,1,0:T(8,128)(2,1)} %get-tuple-element.249), channel_id=1, source_target_pairs={{0,8},{1,9},{2,10},{3,11},{4,12},{5,13},{6,14},{7,15},{8,16},{9,17... | collective-permute-start | bytes 1622024 | tf_op jit(solution)/shard_map/ppermute | solution.py:173
  454.9 43.5 %collective-permute-start.40 = (f16[2,528,256]{2,1,0:T(8,128)(2,1)}, f16[2,528,256]{2,1,0:T(8,128)(2,1)}, u32[]{:S(2)}, u32[]{:S(2)}) collective-permute-start(f16[2,528,256]{2,1,0:T(8,128)(2,1)} %get-tuple-element.251), channel_id=1, source_target_pairs={{0,16},{1,17},{2,18},{3,19},{4,20},{5,21},{6,22},{7,23},{8,24},{9,... | collective-permute-start | bytes 1622024 | tf_op jit(solution)/shard_map/ppermute | solution.py:173
  460.4 38.0 %collective-permute-start.41 = (f16[2,528,256]{2,1,0:T(8,128)(2,1)}, f16[2,528,256]{2,1,0:T(8,128)(2,1)}, u32[]{:S(2)}, u32[]{:S(2)}) collective-permute-start(f16[2,528,256]{2,1,0:T(8,128)(2,1)} %get-tuple-element.250), channel_id=1, source_target_pairs={{0,24},{1,25},{2,26},{3,27},{4,28},{5,29},{6,30},{7,31},{8,0},{9,1... | collective-permute-start | bytes 1622024 | tf_op jit(solution)/shard_map/ppermute | solution.py:173
  464.6 37.4 %collective-permute-start.30 = (f16[4,664,256]{2,1,0:T(8,128)(2,1)S(1)}, f16[4,664,256]{2,1,0:T(8,128)(2,1)}, u32[]{:S(2)}, u32[]{:S(2)}) collective-permute-start(f16[4,664,256]{2,1,0:T(8,128)(2,1)S(1)} %fusion.16), channel_id=1, source_target_pairs={{0,4},{1,5},{2,6},{3,7},{4,0},{5,1},{6,2},{7,3},{8,12},{9,13},{10,... | collective-permute-start | bytes 4079624 | tf_op jit(solution)/shard_map/ppermute | solution.py:173
  474.9 25.7 %collective-permute-start.45 = (f16[2,392,256]{2,1,0:T(8,128)(2,1)S(1)}, f16[2,392,256]{2,1,0:T(8,128)(2,1)S(1)}, u32[]{:S(2)}, u32[]{:S(2)}) collective-permute-start(f16[2,392,256]{2,1,0:T(8,128)(2,1)S(1)} %fusion.29), channel_id=1, source_target_pairs={{0,2},{1,3},{2,0},{3,1},{4,6},{5,7},{6,4},{7,5},{8,10},{9,11},{10,... | collective-permute-start | bytes 1204232 | tf_op jit(solution)/shard_map/ppermute | solution.py:173
  500.5 17.6 %collective-permute-start.42 = (f16[528,256]{1,0:T(8,128)(2,1)S(1)}, f16[528,256]{1,0:T(8,128)(2,1)S(1)}, u32[]{:S(2)}, u32[]{:S(2)}) collective-permute-start(f16[528,256]{1,0:T(8,128)(2,1)S(1)} %fusion.34), channel_id=1, source_target_pairs={{0,2},{1,3},{2,0},{3,1},{4,6},{5,7},{6,4},{7,5},{8,10},{9,11},{10,... | collective-permute-start | bytes 811016 | tf_op jit(solution)/shard_map/ppermute | solution.py:173
  500.7 18.1 %collective-permute-start.46 = (f16[392,256]{1,0:T(8,128)(2,1)S(1)}, f16[392,256]{1,0:T(8,128)(2,1)S(1)}, u32[]{:S(2)}, u32[]{:S(2)}) collective-permute-start(f16[392,256]{1,0:T(8,128)(2,1)S(1)} %fusion.35), channel_id=1, source_target_pairs={{0,4},{1,5},{2,6},{3,7},{4,0},{5,1},{6,2},{7,3},{8,12},{9,13},{10,... | collective-permute-start | bytes 602120 | tf_op jit(solution)/shard_map/ppermute | solution.py:173
  503.9 18.1 %collective-permute-start.31 = (f16[664,256]{1,0:T(8,128)(2,1)S(1)}, f16[664,256]{1,0:T(8,128)(2,1)S(1)}, u32[]{:S(2)}, u32[]{:S(2)}) collective-permute-start(f16[664,256]{1,0:T(8,128)(2,1)S(1)} %get-tuple-element.252), channel_id=1, source_target_pairs={{0,8},{1,9},{2,10},{3,11},{4,12},{5,13},{6,14},{7,15},{8,16},{9,17... | collective-permute-start | bytes 1019912 | tf_op jit(solution)/shard_map/ppermute | solution.py:173
  515.6 15.2 %collective-permute-start.32 = (f16[664,256]{1,0:T(8,128)(2,1)S(1)}, f16[664,256]{1,0:T(8,128)(2,1)S(1)}, u32[]{:S(2)}, u32[]{:S(2)}) collective-permute-start(f16[664,256]{1,0:T(8,128)(2,1)S(1)} %get-tuple-element.254), channel_id=1, source_target_pairs={{0,16},{1,17},{2,18},{3,19},{4,20},{5,21},{6,22},{7,23},{8,24},{9,... | collective-permute-start | bytes 1019912 | tf_op jit(solution)/shard_map/ppermute | solution.py:173
  515.6 15.2 %collective-permute-start.33 = (f16[664,256]{1,0:T(8,128)(2,1)S(1)}, f16[664,256]{1,0:T(8,128)(2,1)S(1)}, u32[]{:S(2)}, u32[]{:S(2)}) collective-permute-start(f16[664,256]{1,0:T(8,128)(2,1)S(1)} %get-tuple-element.253), channel_id=1, source_target_pairs={{0,24},{1,25},{2,26},{3,27},{4,28},{5,29},{6,30},{7,31},{8,0},{9,1... | collective-permute-start | bytes 1019912 | tf_op jit(solution)/shard_map/ppermute | solution.py:173
  533.7 4.6 collective-permute-start.49
  534.5 4.5 collective-permute-start.50
  536.3 5.4 collective-permute-start.51
  541.8 9.2 %collective-permute-start.52 = (f32[88,256]{1,0:T(8,128)S(1)}, f32[88,256]{1,0:T(8,128)S(1)}, u32[]{:S(2)}, u32[]{:S(2)}) collective-permute-start(f32[88,256]{1,0:T(8,128)S(1)} %add_add_fusion.1), channel_id=1, source_target_pairs={{0,8},{1,9},{2,10},{3,11},{4,12},{5,13},{6,14},{7,15},{8,0},{9,1},... | collective-permute-start | bytes 270344 | tf_op jit(solution)/shard_map/ppermute | solution.py:173
  547.5 6.9 %collective-permute-start.53 = (f32[88,256]{1,0:T(8,128)S(1)}, f32[88,256]{1,0:T(8,128)S(1)}, u32[]{:S(2)}, u32[]{:S(2)}) collective-permute-start(f32[88,256]{1,0:T(8,128)S(1)} %add_add_fusion.1), channel_id=1, source_target_pairs={{0,16},{1,17},{2,18},{3,19},{4,20},{5,21},{6,22},{7,23},{8,24},{9,... | collective-permute-start | bytes 270344 | tf_op jit(solution)/shard_map/ppermute | solution.py:173
  550.9 6.3 %collective-permute-start.54 = (f32[88,256]{1,0:T(8,128)S(1)}, f32[88,256]{1,0:T(8,128)S(1)}, u32[]{:S(2)}, u32[]{:S(2)}) collective-permute-start(f32[88,256]{1,0:T(8,128)S(1)} %add_add_fusion.1), channel_id=1, source_target_pairs={{0,24},{1,25},{2,26},{3,27},{4,28},{5,29},{6,30},{7,31},{8,16},{9,... | collective-permute-start | bytes 270344 | tf_op jit(solution)/shard_map/ppermute | solution.py:173
  557.4 5.0 collective-permute-start.47
  563.8 10.5 %collective-permute-start.48 = (f32[109568]{0:T(1024)S(1)}, f32[109568]{0:T(1024)S(1)}, u32[]{:S(2)}, u32[]{:S(2)}) collective-permute-start(f32[109568]{0:T(1024)S(1)} %slice.323), channel_id=1, source_target_pairs={{0,1},{1,2},{2,3},{3,4},{4,5},{5,6},{6,7},{7,8},{8,9},{9,10},{10,1... | collective-permute-start | bytes 1314824 | tf_op jit(solution)/shard_map/ppermute | solution.py:173
  (106 other events, 1072.0 us)
Sparse Core Ops, SparseCore 0:
  22.4 161.7 all-gather.1

commit v6 on v5

--- a/solution.py
+++ b/solution.py
@@ -319,7 +319,7 @@
         dim = left.index(axis)
         me, size = (place.coords[axis], place.digits[axis])
         total = part_of(dim, me)
-        if size == 2 or axis != order[0]:
+        if size == 2 or axis == order[-1]:
             for away in range(1, size):
                 sent = wire(part_of(dim, (me + away) % size))
                 if ahead is not None and axis == order[0] and away == 1:

time: 598 us -> 608 us (1.017)
  starting transfers between devices: 74.6 us -> 82.1 us
    ppermute x56 -> x59, starting transfers between devices: 74.5 us -> 82.1 us  [move(): return lax.ppermute(value, ('dp', 'rows'), pairs)]
    convert_element_type x12 -> x15, other arithmetic: 21 us -> 24.8 us  [wire(): return values.astype(jnp.float16)]
    ppermute x56 -> x59, waiting for transfers between devices: 109 us -> 108 us  [move(): return lax.ppermute(value, ('dp', 'rows'), pairs)]
  transfers between devices with their start and end apart: 57 -> 60, of which waited for: 29 -> 29; matrix products, arithmetic and copies ran while one was open for 11% -> 11% of each run, Pallas kernels for 7% -> 7%
where the time goes in v6:
time: 608 us; the launch traced here: 596 us
  waiting for transfers between devices  242 us (40%)
  Pallas kernels  125 us (21%)
  starting transfers between devices  82.1 us (14%)
  other arithmetic  57.6 us (9%)
  local copies, waits for them, and re-layouts  46.9 us (8%)
  between operations  35.5 us (6%)
  matrix products  7.59 us (1%)
    all_gather x1, waiting for transfers between devices, local(): table = lax.all_gather(block, ('dp', 'rows'), axis=0, tiled=True)  134 us
    ppermute x59, waiting for transfers between devices, move(): return lax.ppermute(value, ('dp', 'rows'), pairs)  108 us
    ppermute x59, starting transfers between devices, move(): return lax.ppermute(value, ('dp', 'rows'), pairs)  82.1 us
    pallas_call x10, Pallas kernels, one_step(): pl.pallas_call(body, grid_spec=pltpu.PrefetchScalarGridSpec(num_scalar_pr...  67.4 us
    convert_element_type x15, other arithmetic, wire(): return values.astype(jnp.float16)  24.8 us
    unnamed x203, local copies, waits for them, and re-layouts  24.1 us
    pallas_call x12, Pallas kernels, grad_into(): pl.pallas_call(body, grid=(tiles,), in_specs=old_specs + [pl.BlockSpec((t...  21.8 us
    pallas_call x2, Pallas kernels, conv_backward(): pl.pallas_call(body, grid_spec=pltpu.PrefetchScalarGridSpec(num_scalar_pr...  17.4 us
  transfers between devices with their start and end apart: 60, of which 29 were waited for; matrix products, arithmetic and copies ran while one was open for 11% of the time, Pallas kernels for 7%

profile of v6, /device:TPU:4, one launch (start us, length us, event | category | flops | bytes accessed | tf_op | source)
XLA Modules:
  0.0 596.3 jit_solution(16673874966858264642)
XLA Ops:
  8.8 2.8 collective-permute-start.2
  11.5 3.5 collective-permute-done.2
  15.0 5.3 concatenate.176
  31.1 3.3 collective-permute-start.4
  36.1 3.7 collective-permute-done.5
  50.3 133.9 %all-gather.2.cloned.1.call-done.one_ref.two_ref.out_ref.class_ref.kv_ref.weight_ref.rows_ref.qw_ref.ow_ref.refs_5_.refs_6_.ckv_ref.refs_7_ = bf16[25344,512]{1,0:T(8,128)(2,1)} async-done(((bf16[792,512]{1,0:T(8,128)(2,1)}), bf16[25344,512]{1,0:T(8,128)(2,1)}) %all-gather.2.cloned.1.call-update) | async-done | bytes 25952272 | tf_op jit(solution)/shard_map/all_gather | solution.py:1675
  184.2 5.1 shard_map.231
  194.9 5.5 shard_map.232
  202.8 5.5 shard_map.233
  211.2 4.8 shard_map.235
  220.1 4.2 shard_map.236
  227.9 3.5 shard_map.237.fw_ref.refs_8_
  232.8 6.4 %shard_map.238 = (bf16[512,512]{1,0:T(8,128)(2,1)S(1)}, f32[512,512]{1,0:T(8,128)S(1)}, bf16[512,512]{1,0:T(8,128)(2,1)S(1)}, f32[512,2048]{1,0:T(8,128)}, bf16[512,1024]{1,0:T(8,128)(2,1)S(1)}) custom-call(s32[4]{0:T(128)S(1)} %pad_add_fusion.info_ref, bf16[512,256]{1,0:T(8,128)(2,1)S(1)} %get-tuple-element.119.mine_ref, ...), custom_call_target="tpu_custom_call" | custom-call | flops 1342177280 | bytes 14680064 | tf_op jit(solution)/shard_map/pallas_call | solution.py:842
  244.5 4.8 shard_map.239
  249.5 3.6 convolution_convert_fusion
  253.3 8.6 %shard_map.240 = (f32[72,512]{1,0:T(8,128)S(1)}, f32[8,256]{1,0:T(8,128)S(1)}, f32[512,256]{1,0:T(8,128)S(1)}, bf16[512,256]{1,0:T(8,128)(2,1)S(1)}, bf16[512,25...) custom-call(s32[4]{0:T(128)S(1)} %pad_add_fusion.info_ref, ...), custom_call_target="tpu_custom_call" | custom-call | flops 1879048192 | bytes 10829824 | tf_op jit(solution)/shard_map/pallas_call | solution.py:842
  268.9 6.4 %shard_map.244 = (f32[512,512]{1,0:T(8,128)S(1)}, bf16[512,256]{1,0:T(8,128)(2,1)S(1)}, bf16[512,256]{1,0:T(8,128)(2,1)S(1)}, f32[8,512]{1,0:T(8,128)S(1)}, f32[8,256]{1,0:T(8,128)S(1)}, /*index=5*/f32[8,512]{1,0:T(8,128)S(1)}) custom-call(s32[4]{0:T(128)S(1)} %pad_add_fusion.info_ref, f32[512,512]{1,0:T(8,128)S(1)} %get-tuple-element.136.mine_ref, ...), custom_call_target="tpu_custom_call" | custom-call | flops 1879048192 | bytes 3227648 | tf_op jit(solution)/shard_map/pallas_call | solution.py:842
  277.9 17.1 %shard_map.248 = (f32[512,512]{1,0:T(8,128)}, bf16[512,256]{1,0:T(8,128)(2,1)S(1)}, bf16[512,768]{1,0:T(8,128)(2,1)S(1)}, f32[512,512]{1,0:T(8,128)}, f32[8,256]{1,0:T(8,128)S(1)}) custom-call(s32[4]{0:T(128)S(1)} %pad_add_fusion.info_ref, bf16[512,256]{1,0:T(8,128)(2,1)S(1)} %get-tuple-element.142.refs_2_.mine_ref, ...), custom_call_target="tpu_custom_call" | custom-call | flops 3489660928 | bytes 6307840 | tf_op jit(solution)/shard_map/pallas_call | solution.py:842
  304.5 3.0 shard_map.242
  307.5 4.6 shard_map.251
  312.5 4.1 shard_map.243
  326.8 8.8 %shard_map.253 = (f32[25344,256]{1,0:T(8,128)}, bf16[512,256]{1,0:T(8,128)(2,1)S(1)}, f32[8,256]{1,0:T(8,128)S(1)}) custom-call(s32[4]{0:T(128)S(1)} %pad_add_fusion.info_ref, f32[25344,256]{1,0:T(8,128)} %get-tuple-element.161.refs_0_, bf16[512,256]{1,0:T(8,128)(2,1)S(1)} %get-tuple-element.162.refs_1_, ...), custom_call_target="tpu_custom_call", output_to_operand_aliasing={{0}: (1, {})} | custom-call | flops 2415919104 | bytes 10223616 | tf_op jit(solution)/shard_map/pallas_call | solution.py:728
  341.4 5.3 shard_map.254
  352.2 2.7 shard_map.256
  366.7 8.7 %shard_map.258 = (f32[25344,256]{1,0:T(8,128)}, bf16[512,256]{1,0:T(8,128)(2,1)S(1)}, f32[8,256]{1,0:T(8,128)S(1)}) custom-call(s32[4]{0:T(128)S(1)} %pad_add_fusion.info_ref, f32[25344,256]{1,0:T(8,128)} %broadcast_dynamic-update-slice_fusion.1.refs_0_, bf16[512,256]{1,0:T(8,128)(2,1)S(1)} %get-tuple-element.192.refs_1_, ...), custom_call_target="tpu_custom_call", output_to_operand_aliasing={{0}: (1, {})} | custom-call | flops 2415919104 | bytes 10223616 | tf_op jit(solution)/shard_map/pallas_call | solution.py:728
  375.3 3.2 fusion.22
  381.9 4.2 fusion.7
  386.1 4.7 fusion.6
  390.8 4.9 collective-permute-done.35
  397.4 4.7 collective-permute-start.36
  404.3 12.1 %collective-permute-done.36 = f16[2,2,392,256]{3,2,1,0:T(8,128)(2,1)S(1)} collective-permute-done((f16[2,2,392,256]{3,2,1,0:T(8,128)(2,1)S(1)}, f16[2,2,392,256]{3,2,1,0:T(8,128)(2,1)S(1)}, u32[]{:S(2)}, u32[]{:S(2)}) %collective-permute-start.36) | collective-permute-done | bytes 802848 | tf_op jit(solution)/shard_map/ppermute | solution.py:173
  416.4 3.7 fusion.15
  420.8 3.8 fusion.43
  427.5 21.1 %collective-permute-done.34 = f16[4,2,528,256]{3,2,1,0:T(8,128)(2,1)} collective-permute-done((f16[4,2,528,256]{3,2,1,0:T(8,128)(2,1)}, f16[4,2,528,256]{3,2,1,0:T(8,128)(2,1)}, u32[]{:S(2)}, u32[]{:S(2)}) %collective-permute-start.34) | collective-permute-done | bytes 2162720 | tf_op jit(solution)/shard_map/ppermute | solution.py:173
  448.6 3.3 fusion.4
  460.4 3.9 fusion.1
  464.3 2.9 collective-permute-done.39
  467.4 4.4 collective-permute-start.40
  474.5 9.9 %collective-permute-done.46 = f16[2,2,392,256]{3,2,1,0:T(8,128)(2,1)S(1)} collective-permute-done((f16[2,2,392,256]{3,2,1,0:T(8,128)(2,1)S(1)}, f16[2,2,392,256]{3,2,1,0:T(8,128)(2,1)S(1)}, u32[]{:S(2)}, u32[]{:S(2)}) %collective-permute-start.46) | collective-permute-done | bytes 802848 | tf_op jit(solution)/shard_map/ppermute | solution.py:173
  496.0 4.2 collective-permute-start.41
  508.1 5.3 collective-permute-start.31
  515.0 2.8 collective-permute-start.33
  517.8 13.2 %collective-permute-done.44 = f16[2,528,256]{2,1,0:T(8,128)(2,1)S(1)} collective-permute-done((f16[2,528,256]{2,1,0:T(8,128)(2,1)S(1)}, f16[2,528,256]{2,1,0:T(8,128)(2,1)S(1)}, u32[]{:S(2)}, u32[]{:S(2)}) %collective-permute-start.44) | collective-permute-done | bytes 540704 | tf_op jit(solution)/shard_map/ppermute | solution.py:173
  534.5 8.2 %collective-permute-done.32 = f16[664,256]{1,0:T(8,128)(2,1)S(1)} collective-permute-done((f16[664,256]{1,0:T(8,128)(2,1)S(1)}, f16[664,256]{1,0:T(8,128)(2,1)S(1)}, u32[]{:S(2)}, u32[]{:S(2)}) %collective-permute-start.32) | collective-permute-done | bytes 340000 | tf_op jit(solution)/shard_map/ppermute | solution.py:173
  553.9 4.3 collective-permute-start.55
  560.8 4.3 collective-permute-done.56
  578.2 4.0 collective-permute-done.51
  584.0 3.8 multiply_add_fusion
  (489 shorter events, 158.6 us)
Async XLA Ops:
  7.2 177.0 %all-gather.2.cloned.1.call-start = ((), (), s32[]{:S(2)}) async-start(), calls=%async_computation | async-start | bytes 26763264 | tf_op jit(solution)/shard_map/all_gather | solution.py:1675
  8.8 6.3 %collective-permute-start.2 = (bf16[113664]{0:T(1024)(128)(2,1)S(1)}, bf16[113664]{0:T(1024)(128)(2,1)S(1)}, u32[]{:S(2)}, u32[]{:S(2)}) collective-permute-start(bf16[113664]{0:T(1024)(128)(2,1)S(1)} %slice.357), channel_id=1, source_target_pairs={{1,0},{2,1},{3,2},{4,3},{5,4},{6,5},{7,6},{8,7},{9,8},{10,9},{11,1... | collective-permute-start | bytes 681992 | tf_op jit(solution)/shard_map/ppermute | solution.py:173
  22.3 8.7 %collective-permute-start.3 = (bf16[1,5,128]{2,0,1:T(2,128)(2,1)S(1)}, bf16[1,5,128]{2,0,1:T(2,128)(2,1)S(1)}, u32[]{:S(2)}, u32[]{:S(2)}) collective-permute-start(bf16[1,5,128]{2,0,1:T(2,128)(2,1)S(1)} %broadcast_in_dim_reshape.3), channel_id=1, source_target_pairs={{0,1},{1,0},{2,3},{3,2},{4,5},{5,4},{6,7},{7,6},{8,9},{9,8},{10,11... | collective-permute-start | bytes 3848 | tf_op jit(solution)/shard_map/ppermute | solution.py:173
  23.3 18.1 %collective-permute-start = (f32[1,2,8,32,6]{3,2,0,4,1:T(8,128)S(1)}, f32[1,2,8,32,6]{3,2,0,4,1:T(8,128)S(1)}, u32[]{:S(2)}, u32[]{:S(2)}) collective-permute-start(f32[1,2,8,32,6]{3,2,0,4,1:T(8,128)S(1)} %maximum_bitcast_fusion), channel_id=1, source_target_pairs={{0,1},{1,0},{2,3},{3,2},{4,5},{5,4},{6,7},{7,6},{8,9},{9,8},{10,11... | collective-permute-start | bytes 36872 | tf_op jit(solution)/shard_map/ppermute | solution.py:173
  31.1 4.9 collective-permute-start.4
  41.5 4.9 collective-permute-start.1
  43.8 5.7 collective-permute-start.7
  227.6 5.2 collective-permute-start.12
  296.6 10.9 %collective-permute-start.17 = (f32[512,512]{1,0:T(8,128)}, f32[512,512]{1,0:T(8,128)}, u32[]{:S(2)}, u32[]{:S(2)}) collective-permute-start(f32[512,512]{1,0:T(8,128)} %get-tuple-element.155.mine_ref), channel_id=1, source_target_pairs={{0,1},{1,0},{2,3},{3,2},{4,5},{5,4},{6,7},{7,6},{8,9},{9,8},{10,11... | collective-permute-start | bytes 3145736 | tf_op jit(solution)/shard_map/ppermute | solution.py:173
  312.2 14.6 %collective-permute-start.18 = (bf16[512,256]{1,0:T(8,128)(2,1)S(1)}, bf16[512,256]{1,0:T(8,128)(2,1)S(1)}, u32[]{:S(2)}, u32[]{:S(2)}) collective-permute-start(bf16[512,256]{1,0:T(8,128)(2,1)S(1)} %get-tuple-element.162.refs_1_), channel_id=1, source_target_pairs={{0,1},{1,0},{2,3},{3,2},{4,5},{5,4},{6,7},{7,6},{8,9},{9,8},{10,11... | collective-permute-start | bytes 786440 | tf_op jit(solution)/shard_map/ppermute | solution.py:173
  318.1 21.0 %collective-permute-start.20 = (f32[8,512]{1,0:T(8,128)S(1)}, f32[8,512]{1,0:T(8,128)S(1)}, u32[]{:S(2)}, u32[]{:S(2)}) collective-permute-start(f32[8,512]{1,0:T(8,128)S(1)} %get-tuple-element.166), channel_id=1, source_target_pairs={{0,1},{1,0},{2,3},{3,2},{4,5},{5,4},{6,7},{7,6},{8,9},{9,8},{10,11... | collective-permute-start | bytes 49160 | tf_op jit(solution)/shard_map/ppermute | solution.py:173
  335.6 5.8 collective-permute-start.19
  341.0 25.6 %collective-permute-start.28 = (bf16[512,256]{1,0:T(8,128)(2,1)S(1)}, bf16[512,256]{1,0:T(8,128)(2,1)S(1)}, u32[]{:S(2)}, u32[]{:S(2)}) collective-permute-start(bf16[512,256]{1,0:T(8,128)(2,1)S(1)} %get-tuple-element.192.refs_1_), channel_id=1, source_target_pairs={{0,1},{1,0},{2,3},{3,2},{4,5},{5,4},{6,7},{7,6},{8,9},{9,8},{10,11... | collective-permute-start | bytes 786440 | tf_op jit(solution)/shard_map/ppermute | solution.py:173
  348.7 6.2 %collective-permute-start.22 = (f32[8,128]{1,0:T(8,128)S(1)}, f32[8,128]{1,0:T(8,128)S(1)}, u32[]{:S(2)}, u32[]{:S(2)}) collective-permute-start(f32[8,128]{1,0:T(8,128)S(1)} %max.68), channel_id=1, source_target_pairs={{0,2},{1,3},{2,0},{3,1},{4,6},{5,7},{6,4},{7,5},{8,10},{9,11},{10,... | collective-permute-start | bytes 12296 | tf_op jit(solution)/shard_map/ppermute | solution.py:173
  349.3 5.7 collective-permute-start.23
  350.7 4.5 collective-permute-start.24
  355.2 7.4 %collective-permute-start.25 = (f32[8,128]{1,0:T(8,128)S(1)}, f32[8,128]{1,0:T(8,128)S(1)}, u32[]{:S(2)}, u32[]{:S(2)}) collective-permute-start(f32[8,128]{1,0:T(8,128)S(1)} %maximum_maximum_fusion.1), channel_id=1, source_target_pairs={{0,8},{1,9},{2,10},{3,11},{4,12},{5,13},{6,14},{7,15},{8,0},{9,1},... | collective-permute-start | bytes 12296 | tf_op jit(solution)/shard_map/ppermute | solution.py:173
  355.3 7.3 %collective-permute-start.26 = (f32[8,128]{1,0:T(8,128)S(1)}, f32[8,128]{1,0:T(8,128)S(1)}, u32[]{:S(2)}, u32[]{:S(2)}) collective-permute-start(f32[8,128]{1,0:T(8,128)S(1)} %maximum_maximum_fusion.1), channel_id=1, source_target_pairs={{0,16},{1,17},{2,18},{3,19},{4,20},{5,21},{6,22},{7,23},{8,24},{9,... | collective-permute-start | bytes 12296 | tf_op jit(solution)/shard_map/ppermute | solution.py:173
  357.2 5.4 collective-permute-start.27
  378.5 17.2 %collective-permute-start.35 = (f16[2,2,392,256]{3,2,1,0:T(8,128)(2,1)S(1)}, f16[2,2,392,256]{3,2,1,0:T(8,128)(2,1)S(1)}, u32[]{:S(2)}, u32[]{:S(2)}) collective-permute-start(f16[2,2,392,256]{3,2,1,0:T(8,128)(2,1)S(1)} %get-tuple-element.245), channel_id=1, source_target_pairs={{0,8},{1,9},{2,10},{3,11},{4,12},{5,13},{6,14},{7,15}} | collective-permute-start | bytes 2408456 | tf_op jit(solution)/shard_map/ppermute | solution.py:173
  380.3 24.0 %collective-permute-start.37 = (f16[2,2,392,256]{3,2,1,0:T(8,128)(2,1)}, f16[2,2,392,256]{3,2,1,0:T(8,128)(2,1)}, u32[]{:S(2)}, u32[]{:S(2)}) collective-permute-start(f16[2,2,392,256]{3,2,1,0:T(8,128)(2,1)} %get-tuple-element.246), channel_id=1, source_target_pairs={{24,16},{25,17},{26,18},{27,19},{28,20},{29,21},{30,22},{31,23}} | collective-permute-start | bytes 2408456 | tf_op jit(solution)/shard_map/ppermute | solution.py:173
  397.4 19.0 %collective-permute-start.36 = (f16[2,2,392,256]{3,2,1,0:T(8,128)(2,1)S(1)}, f16[2,2,392,256]{3,2,1,0:T(8,128)(2,1)S(1)}, u32[]{:S(2)}, u32[]{:S(2)}) collective-permute-start(f16[2,2,392,256]{3,2,1,0:T(8,128)(2,1)S(1)} %fusion.14), channel_id=1, source_target_pairs={{0,8},{1,9},{2,10},{3,11},{4,12},{5,13},{6,14},{7,15},{8,16},{9,17... | collective-permute-start | bytes 2408456 | tf_op jit(solution)/shard_map/ppermute | solution.py:173
  402.1 58.3 %collective-permute-start.29 = (f16[4,2,664,256]{3,2,1,0:T(8,128)(2,1)}, f16[4,2,664,256]{3,2,1,0:T(8,128)(2,1)}, u32[]{:S(2)}, u32[]{:S(2)}) collective-permute-start(f16[4,2,664,256]{3,2,1,0:T(8,128)(2,1)} %fusion.6), channel_id=1, source_target_pairs={{0,2},{1,3},{2,0},{3,1},{4,6},{5,7},{6,4},{7,5},{8,10},{9,11},{10,... | collective-permute-start | bytes 8159240 | tf_op jit(solution)/shard_map/ppermute | solution.py:173
  402.7 45.9 %collective-permute-start.34 = (f16[4,2,528,256]{3,2,1,0:T(8,128)(2,1)}, f16[4,2,528,256]{3,2,1,0:T(8,128)(2,1)}, u32[]{:S(2)}, u32[]{:S(2)}) collective-permute-start(f16[4,2,528,256]{3,2,1,0:T(8,128)(2,1)} %fusion.7), channel_id=1, source_target_pairs={{0,4},{1,5},{2,6},{3,7},{4,0},{5,1},{6,2},{7,3},{8,12},{9,13},{10,... | collective-permute-start | bytes 6488072 | tf_op jit(solution)/shard_map/ppermute | solution.py:173
  420.1 5.8 collective-permute-start.38
  452.2 15.0 %collective-permute-start.39 = (f16[2,528,256]{2,1,0:T(8,128)(2,1)S(1)}, f16[2,528,256]{2,1,0:T(8,128)(2,1)S(1)}, u32[]{:S(2)}, u32[]{:S(2)}) collective-permute-start(f16[2,528,256]{2,1,0:T(8,128)(2,1)S(1)} %get-tuple-element.251), channel_id=1, source_target_pairs={{0,8},{1,9},{2,10},{3,11},{4,12},{5,13},{6,14},{7,15}} | collective-permute-start | bytes 1622024 | tf_op jit(solution)/shard_map/ppermute | solution.py:173
  455.3 29.1 %collective-permute-start.46 = (f16[2,2,392,256]{3,2,1,0:T(8,128)(2,1)S(1)}, f16[2,2,392,256]{3,2,1,0:T(8,128)(2,1)S(1)}, u32[]{:S(2)}, u32[]{:S(2)}) collective-permute-start(f16[2,2,392,256]{3,2,1,0:T(8,128)(2,1)S(1)} %copy-done.71), channel_id=1, source_target_pairs={{0,8},{1,9},{2,10},{3,11},{4,12},{5,13},{6,14},{7,15},{8,16},{9,17... | collective-permute-start | bytes 2408456 | tf_op jit(solution)/shard_map/ppermute | solution.py:173
  456.7 27.7 %collective-permute-start.47 = (f16[2,2,392,256]{3,2,1,0:T(8,128)(2,1)S(1)}, f16[2,2,392,256]{3,2,1,0:T(8,128)(2,1)S(1)}, u32[]{:S(2)}, u32[]{:S(2)}) collective-permute-start(f16[2,2,392,256]{3,2,1,0:T(8,128)(2,1)S(1)} %fusion.13), channel_id=1, source_target_pairs={{8,0},{9,1},{10,2},{11,3},{12,4},{13,5},{14,6},{15,7},{16,8},{17,9... | collective-permute-start | bytes 2408456 | tf_op jit(solution)/shard_map/ppermute | solution.py:173
  458.0 30.8 %collective-permute-start.42 = (f16[2,528,256]{2,1,0:T(8,128)(2,1)S(1)}, f16[2,528,256]{2,1,0:T(8,128)(2,1)S(1)}, u32[]{:S(2)}, u32[]{:S(2)}) collective-permute-start(f16[2,528,256]{2,1,0:T(8,128)(2,1)S(1)} %get-tuple-element.252), channel_id=1, source_target_pairs={{24,16},{25,17},{26,18},{27,19},{28,20},{29,21},{30,22},{31,23}} | collective-permute-start | bytes 1622024 | tf_op jit(solution)/shard_map/ppermute | solution.py:173
  467.4 23.6 %collective-permute-start.40 = (f16[2,528,256]{2,1,0:T(8,128)(2,1)S(1)}, f16[2,528,256]{2,1,0:T(8,128)(2,1)S(1)}, u32[]{:S(2)}, u32[]{:S(2)}) collective-permute-start(f16[2,528,256]{2,1,0:T(8,128)(2,1)S(1)} %fusion.19), channel_id=1, source_target_pairs={{0,8},{1,9},{2,10},{3,11},{4,12},{5,13},{6,14},{7,15},{8,16},{9,17... | collective-permute-start | bytes 1622024 | tf_op jit(solution)/shard_map/ppermute | solution.py:173
  473.1 32.7 %collective-permute-start.30 = (f16[4,664,256]{2,1,0:T(8,128)(2,1)}, f16[4,664,256]{2,1,0:T(8,128)(2,1)S(1)}, u32[]{:S(2)}, u32[]{:S(2)}) collective-permute-start(f16[4,664,256]{2,1,0:T(8,128)(2,1)} %fusion.16), channel_id=1, source_target_pairs={{0,4},{1,5},{2,6},{3,7},{4,0},{5,1},{6,2},{7,3},{8,12},{9,13},{10,... | collective-permute-start | bytes 4079624 | tf_op jit(solution)/shard_map/ppermute | solution.py:173
  487.2 13.0 %collective-permute-start.48 = (f16[2,392,256]{2,1,0:T(8,128)(2,1)}, f16[2,392,256]{2,1,0:T(8,128)(2,1)}, u32[]{:S(2)}, u32[]{:S(2)}) collective-permute-start(f16[2,392,256]{2,1,0:T(8,128)(2,1)} %fusion.31), channel_id=1, source_target_pairs={{0,2},{1,3},{2,0},{3,1},{4,6},{5,7},{6,4},{7,5},{8,10},{9,11},{10,... | collective-permute-start | bytes 1204232 | tf_op jit(solution)/shard_map/ppermute | solution.py:173
  492.1 9.4 %collective-permute-start.43 = (f16[2,528,256]{2,1,0:T(8,128)(2,1)}, f16[2,528,256]{2,1,0:T(8,128)(2,1)}, u32[]{:S(2)}, u32[]{:S(2)}) collective-permute-start(f16[2,528,256]{2,1,0:T(8,128)(2,1)} %get-tuple-element.250), channel_id=1, source_target_pairs={{16,8},{17,9},{18,10},{19,11},{20,12},{21,13},{22,14},{23,15},{24,... | collective-permute-start | bytes 1622024 | tf_op jit(solution)/shard_map/ppermute | solution.py:173
  496.0 19.0 %collective-permute-start.41 = (f16[2,528,256]{2,1,0:T(8,128)(2,1)S(1)}, f16[2,528,256]{2,1,0:T(8,128)(2,1)S(1)}, u32[]{:S(2)}, u32[]{:S(2)}) collective-permute-start(f16[2,528,256]{2,1,0:T(8,128)(2,1)S(1)} %get-tuple-element.249), channel_id=1, source_target_pairs={{0,8},{1,9},{2,10},{3,11},{4,12},{5,13},{6,14},{7,15},{8,16},{9,17... | collective-permute-start | bytes 1622024 | tf_op jit(solution)/shard_map/ppermute | solution.py:173
  503.1 27.9 %collective-permute-start.44 = (f16[2,528,256]{2,1,0:T(8,128)(2,1)S(1)}, f16[2,528,256]{2,1,0:T(8,128)(2,1)S(1)}, u32[]{:S(2)}, u32[]{:S(2)}) collective-permute-start(f16[2,528,256]{2,1,0:T(8,128)(2,1)S(1)} %fusion.18), channel_id=1, source_target_pairs={{8,0},{9,1},{10,2},{11,3},{12,4},{13,5},{14,6},{15,7},{16,8},{17,9... | collective-permute-start | bytes 1622024 | tf_op jit(solution)/shard_map/ppermute | solution.py:173
  504.4 29.3 %collective-permute-start.49 = (f16[392,256]{1,0:T(8,128)(2,1)S(1)}, f16[392,256]{1,0:T(8,128)(2,1)S(1)}, u32[]{:S(2)}, u32[]{:S(2)}) collective-permute-start(f16[392,256]{1,0:T(8,128)(2,1)S(1)} %fusion.37), channel_id=1, source_target_pairs={{0,4},{1,5},{2,6},{3,7},{4,0},{5,1},{6,2},{7,3},{8,12},{9,13},{10,... | collective-permute-start | bytes 602120 | tf_op jit(solution)/shard_map/ppermute | solution.py:173
  508.1 26.4 %collective-permute-start.31 = (f16[664,256]{1,0:T(8,128)(2,1)S(1)}, f16[664,256]{1,0:T(8,128)(2,1)S(1)}, u32[]{:S(2)}, u32[]{:S(2)}) collective-permute-start(f16[664,256]{1,0:T(8,128)(2,1)S(1)} %get-tuple-element.253), channel_id=1, source_target_pairs={{0,8},{1,9},{2,10},{3,11},{4,12},{5,13},{6,14},{7,15},{8,16},{9,17... | collective-permute-start | bytes 1019912 | tf_op jit(solution)/shard_map/ppermute | solution.py:173
  513.4 29.3 %collective-permute-start.32 = (f16[664,256]{1,0:T(8,128)(2,1)S(1)}, f16[664,256]{1,0:T(8,128)(2,1)S(1)}, u32[]{:S(2)}, u32[]{:S(2)}) collective-permute-start(f16[664,256]{1,0:T(8,128)(2,1)S(1)} %get-tuple-element.255), channel_id=1, source_target_pairs={{0,16},{1,17},{2,18},{3,19},{4,20},{5,21},{6,22},{7,23},{8,24},{9,... | collective-permute-start | bytes 1019912 | tf_op jit(solution)/shard_map/ppermute | solution.py:173
  515.0 27.7 %collective-permute-start.33 = (f16[664,256]{1,0:T(8,128)(2,1)S(1)}, f16[664,256]{1,0:T(8,128)(2,1)S(1)}, u32[]{:S(2)}, u32[]{:S(2)}) collective-permute-start(f16[664,256]{1,0:T(8,128)(2,1)S(1)} %get-tuple-element.254), channel_id=1, source_target_pairs={{0,24},{1,25},{2,26},{3,27},{4,28},{5,29},{6,30},{7,31},{8,0},{9,1... | collective-permute-start | bytes 1019912 | tf_op jit(solution)/shard_map/ppermute | solution.py:173
  532.5 11.1 %collective-permute-start.45 = (f16[528,256]{1,0:T(8,128)(2,1)S(1)}, f16[528,256]{1,0:T(8,128)(2,1)S(1)}, u32[]{:S(2)}, u32[]{:S(2)}) collective-permute-start(f16[528,256]{1,0:T(8,128)(2,1)S(1)} %fusion.36), channel_id=1, source_target_pairs={{0,2},{1,3},{2,0},{3,1},{4,6},{5,7},{6,4},{7,5},{8,10},{9,11},{10,... | collective-permute-start | bytes 811016 | tf_op jit(solution)/shard_map/ppermute | solution.py:173
  546.3 4.6 collective-permute-start.52
  548.1 4.5 collective-permute-start.53
  548.4 5.4 collective-permute-start.54
  553.9 6.8 %collective-permute-start.55 = (f32[88,256]{1,0:T(8,128)S(1)}, f32[88,256]{1,0:T(8,128)S(1)}, u32[]{:S(2)}, u32[]{:S(2)}) collective-permute-start(f32[88,256]{1,0:T(8,128)S(1)} %add_add_fusion.1), channel_id=1, source_target_pairs={{0,8},{1,9},{2,10},{3,11},{4,12},{5,13},{6,14},{7,15},{8,0},{9,1},... | collective-permute-start | bytes 270344 | tf_op jit(solution)/shard_map/ppermute | solution.py:173
  558.2 6.9 %collective-permute-start.56 = (f32[88,256]{1,0:T(8,128)S(1)}, f32[88,256]{1,0:T(8,128)S(1)}, u32[]{:S(2)}, u32[]{:S(2)}) collective-permute-start(f32[88,256]{1,0:T(8,128)S(1)} %add_add_fusion.1), channel_id=1, source_target_pairs={{0,16},{1,17},{2,18},{3,19},{4,20},{5,21},{6,22},{7,23},{8,24},{9,... | collective-permute-start | bytes 270344 | tf_op jit(solution)/shard_map/ppermute | solution.py:173
  558.2 6.9 %collective-permute-start.57 = (f32[88,256]{1,0:T(8,128)S(1)}, f32[88,256]{1,0:T(8,128)S(1)}, u32[]{:S(2)}, u32[]{:S(2)}) collective-permute-start(f32[88,256]{1,0:T(8,128)S(1)} %add_add_fusion.1), channel_id=1, source_target_pairs={{0,24},{1,25},{2,26},{3,27},{4,28},{5,29},{6,30},{7,31},{8,16},{9,... | collective-permute-start | bytes 270344 | tf_op jit(solution)/shard_map/ppermute | solution.py:173
  565.2 5.0 collective-permute-start.50
  571.7 10.5 %collective-permute-start.51 = (f32[109568]{0:T(1024)S(1)}, f32[109568]{0:T(1024)S(1)}, u32[]{:S(2)}, u32[]{:S(2)}) collective-permute-start(f32[109568]{0:T(1024)S(1)} %slice.323), channel_id=1, source_target_pairs={{0,1},{1,2},{2,3},{3,4},{4,5},{5,6},{6,7},{7,8},{8,9},{9,10},{10,1... | collective-permute-start | bytes 1314824 | tf_op jit(solution)/shard_map/ppermute | solution.py:173
  (109 other events, 1158.7 us)
Sparse Core Ops, SparseCore 0:
  22.4 161.7 all-gather.1
